TPU v7x, 32 devices: a whole 2x2x4 slice. The times are simulated.
32 devices in a mesh: rows: 4 (over y, core), mp: 8 (over z, x).
Axes of the slice: x: 2, y: 2, z: 4, core: 2. Of those that a mesh axis runs over, the one named last changes fastest.
Arguments:
- tokens: bfloat16 [8192, 1024], P(('rows', 'mp')), may hold values from -6 to 6
- segment_ids: int32 [8192], P('rows'), may hold values from 0 to 3, as said below
- cotangent: bfloat16 [8192, 1024], P(('rows', 'mp')), may hold values from -6 to 6
- ln_attn_gain: float32 [2, 1024], replicated, may hold values from 0.25 to 1.75
- ln_attn_bias: float32 [2, 1024], replicated, may hold values from -4 to 4
- qkv_weight: bfloat16 [2, 1024, 3, 1024], P(None, None, None, 'mp'), may hold values from -0.1875 to 0.1875
- qv_bias: float32 [2, 2, 1024], P(None, None, 'mp'), may hold values from -4 to 4
- head_scale: float32 [2, 16], replicated, may hold values from 0.25 to 1.75
- out_weight: bfloat16 [2, 1024, 1024], P(None, 'mp'), may hold values from -0.1875 to 0.1875
- out_bias: float32 [2, 1024], replicated, may hold values from -4 to 4
- ln_post_gain: float32 [2, 1024], replicated, may hold values from 0.25 to 1.75
- ln_post_bias: float32 [2, 1024], replicated, may hold values from -4 to 4
- ln_ffn_gain: float32 [2, 1024], replicated, may hold values from 0.25 to 1.75
- ln_ffn_bias: float32 [2, 1024], replicated, may hold values from -4 to 4
- fc1_weight: bfloat16 [2, 1024, 4096], P(None, None, 'mp'), may hold values from -0.1875 to 0.1875
- fc1_bias: float32 [2, 4096], P(None, 'mp'), may hold values from -4 to 4
- mid_gain: float32 [2, 4096], P(None, 'mp'), may hold values from 0.25 to 1.75
- mid_bias: float32 [2, 4096], P(None, 'mp'), may hold values from -4 to 4
- fc2_weight: bfloat16 [2, 4096, 1024], P(None, 'mp'), may hold values from -0.09375 to 0.09375
- fc2_bias: float32 [2, 1024], replicated, may hold values from -4 to 4
Outputs:
- layer_output: bfloat16 [8192, 1024], P(('rows', 'mp'))
- input_grad: float32 [8192, 1024], P(('rows', 'mp'))
- ln_attn_gain_grad: float32 [2, 1024], replicated
- ln_attn_bias_grad: float32 [2, 1024], replicated
- qkv_weight_grad: float32 [2, 1024, 3, 1024], P(None, None, None, 'mp')
- qv_bias_grad: float32 [2, 2, 1024], P(None, None, 'mp')
- head_scale_grad: float32 [2, 16], replicated
- out_weight_grad: float32 [2, 1024, 1024], P(None, 'mp')
- out_bias_grad: float32 [2, 1024], replicated
- ln_post_gain_grad: float32 [2, 1024], replicated
- ln_post_bias_grad: float32 [2, 1024], replicated
- ln_ffn_gain_grad: float32 [2, 1024], replicated
- ln_ffn_bias_grad: float32 [2, 1024], replicated
- fc1_weight_grad: float32 [2, 1024, 4096], P(None, None, 'mp')
- fc1_bias_grad: float32 [2, 4096], P(None, 'mp')
- mid_gain_grad: float32 [2, 4096], P(None, 'mp')
- mid_bias_grad: float32 [2, 4096], P(None, 'mp')
- fc2_weight_grad: float32 [2, 4096, 1024], P(None, 'mp')
- fc2_bias_grad: float32 [2, 1024], replicated
Inputs may be any that keep to these rules, and one draw needn't show every extreme that they name: `segment_ids`: ids restart at 0 in every aligned group of 2048 tokens and never fall within it; in each group document 0 holds more than 1792 tokens and documents 1 to 3 lie in the group's last 256 tokens.
All inputs are finite; a program needn't handle non-finite values.
Results may differ from a plain program's by a relative error of at most 0.022.
Values may be sent and summed in bfloat16 or wider, within the bound.
A program may use at most 256 MiB of HBM per device.

v0:
```python
from functools import partial

import jax
import jax.numpy as jnp
from jax import lax
from jax.experimental import pallas as pl
from jax.experimental.pallas import tpu as pltpu
from jax.sharding import Mesh
from jax.sharding import PartitionSpec as P

epsilon = 1e-05
masked = -1e30


def partner(shard, axis, stride):
    return lax.ppermute(shard, axis, [(i, i ^ 1 << stride) for i in range(lax.axis_size(axis))])


def norm_local(values, gain_row, bias_row):
    average = jnp.mean(values, axis=-1, keepdims=True)
    centered = values - average
    spread = jnp.mean(centered * centered, axis=-1, keepdims=True)
    factor = lax.rsqrt(spread + epsilon)
    normal = centered * factor
    return (normal * gain_row + bias_row, normal, factor)


def norm_back(grad_out, normal, factor, gain_row):
    scaled = grad_out * gain_row
    inner_sum = jnp.mean(scaled * normal, axis=-1, keepdims=True)
    return factor * (scaled - jnp.mean(scaled, axis=-1, keepdims=True) - normal * inner_sum)


def collect_rows(normed_b):
    return lax.all_gather(normed_b, "mp", axis=0, tiled=True)


def collect_grads(gradient_b):
    return lax.all_gather(gradient_b, "mp", axis=0, tiled=True)


def reduce_branch(operand_b, weight_b, local_rows):

    def partial_term(first_row, count):
        return jnp.dot(operand_b, weight_b, preferred_element_type=jnp.float32)

    return lax.psum_scatter(
        partial_term(jnp.int32(0), local_rows * lax.axis_size("mp")).astype(jnp.bfloat16),
        "mp",
        scatter_dimension=0,
        tiled=True,
    ).astype(jnp.float32)


def reduce_grads(operand_b, weight_b, local_rows):

    def partial_term(first_row, count):
        return jnp.einsum("tc,dc->td", operand_b, weight_b, preferred_element_type=jnp.float32)

    return lax.psum_scatter(
        partial_term(jnp.int32(0), local_rows * lax.axis_size("mp")).astype(jnp.bfloat16),
        "mp",
        scatter_dimension=0,
        tiled=True,
    ).astype(jnp.float32)


def hidden_stats(first_sum, second_sum):
    return lax.psum((first_sum, second_sum), "mp")


def hidden_grad_stats(first_sum, second_sum):
    return lax.psum((first_sum, second_sum), "mp")


def join_cols(mine, other, is_upper):
    lower_part = jnp.where(is_upper, other, mine)
    upper_part = jnp.where(is_upper, mine, other)
    return jnp.concatenate([lower_part, upper_part], axis=-1)


def join_rows(mine, other, is_upper):
    lower_part = jnp.where(is_upper, other, mine)
    upper_part = jnp.where(is_upper, mine, other)
    return jnp.concatenate([lower_part, upper_part], axis=0)


def split_cols(values, cols_here, is_upper):
    lower_part = values[..., :cols_here]
    upper_part = values[..., cols_here:]
    return (
        jnp.where(is_upper, upper_part, lower_part),
        jnp.where(is_upper, lower_part, upper_part),
    )


def masked_scores(query_block, key_rows, query_start, block_rows, doc_rows, positions):
    factor = query_block.shape[-1] ** (-0.5)
    scores = (
        jnp.einsum("qhe,khe->hqk", query_block, key_rows, preferred_element_type=jnp.float32)
        * factor
    )
    query_place = query_start + jnp.arange(block_rows, dtype=jnp.int32)
    query_docs = lax.dynamic_slice_in_dim(doc_rows, query_start, block_rows, 0)
    allowed = (query_docs[:, None] == doc_rows[None, :]) & (
        query_place[:, None] >= positions[None, :]
    )
    return jnp.where(allowed[None], scores, masked)


def attend_forward(queries, key_rows, value_rows, doc_rows, row_offset):
    total_rows = queries.shape[0]
    block_rows = min(512, total_rows)
    positions = jnp.arange(key_rows.shape[0], dtype=jnp.int32)

    def one_block(first_row):
        query_block = lax.dynamic_slice_in_dim(queries, first_row, block_rows, 0)
        scores = masked_scores(
            query_block, key_rows, row_offset + first_row, block_rows, doc_rows, positions
        )
        row_peak = jnp.max(scores, axis=-1, keepdims=True)
        weights = jnp.exp(scores - row_peak)
        totals = jnp.sum(weights, axis=-1, keepdims=True)
        probabilities = (weights / totals).astype(jnp.bfloat16)
        output = jnp.einsum(
            "hqk,khe->qhe", probabilities, value_rows, preferred_element_type=jnp.float32
        )
        return (output, (row_peak + jnp.log(totals))[..., 0])

    starts = jnp.arange(total_rows // block_rows, dtype=jnp.int32) * block_rows
    outputs, log_totals = lax.map(one_block, starts)
    return (outputs.reshape(queries.shape), log_totals)


def attend_backward(queries, key_rows, value_rows, doc_rows, row_offset, log_totals, grad_out):
    total_rows = queries.shape[0]
    block_rows = min(512, total_rows)
    positions = jnp.arange(key_rows.shape[0], dtype=jnp.int32)
    factor = queries.shape[-1] ** (-0.5)

    def one_block(running, first_row):
        key_grad, value_grad = running
        query_block = lax.dynamic_slice_in_dim(queries, first_row, block_rows, 0)
        grad_block = lax.dynamic_slice_in_dim(grad_out, first_row, block_rows, 0)
        scores = masked_scores(
            query_block, key_rows, row_offset + first_row, block_rows, doc_rows, positions
        )
        block_totals = lax.dynamic_index_in_dim(
            log_totals, first_row // block_rows, 0, keepdims=False
        )
        probabilities = jnp.exp(scores - block_totals[..., None])
        prob_grad = jnp.einsum(
            "qhe,khe->hqk", grad_block, value_rows, preferred_element_type=jnp.float32
        )
        inner_sum = jnp.sum(probabilities * prob_grad, axis=-1, keepdims=True)
        score_grad = (probabilities * (prob_grad - inner_sum)).astype(jnp.bfloat16)
        query_grad = (
            jnp.einsum("hqk,khe->qhe", score_grad, key_rows, preferred_element_type=jnp.float32)
            * factor
        )
        key_grad = (
            key_grad
            + jnp.einsum(
                "hqk,qhe->khe", score_grad, query_block, preferred_element_type=jnp.float32
            )
            * factor
        )
        value_grad = value_grad + jnp.einsum(
            "hqk,qhe->khe",
            probabilities.astype(jnp.bfloat16),
            grad_block,
            preferred_element_type=jnp.float32,
        )
        return ((key_grad, value_grad), query_grad)

    starts = jnp.arange(total_rows // block_rows, dtype=jnp.int32) * block_rows
    zero_grads = jnp.zeros(key_rows.shape, jnp.float32)
    (key_grad, value_grad), query_grads = lax.scan(one_block, (zero_grads, zero_grads), starts)
    return (query_grads.reshape(queries.shape), key_grad, value_grad)


def stack_layers(layer_list, members):
    stacked = []
    for member_index in range(members):
        stacked.append(jnp.stack([entry[member_index] for entry in layer_list], axis=0))
    return stacked


def per_device(
    tokens,
    segment_ids,
    cotangent,
    ln_attn_gain,
    ln_attn_bias,
    qkv_weight,
    qv_bias,
    head_scale,
    out_weight,
    out_bias,
    ln_post_gain,
    ln_post_bias,
    ln_ffn_gain,
    ln_ffn_bias,
    fc1_weight,
    fc1_bias,
    mid_gain,
    mid_bias,
    fc2_weight,
    fc2_bias,
):
    layers = qkv_weight.shape[0]
    local_rows = tokens.shape[0]
    model_width = tokens.shape[1]
    cols_here = qkv_weight.shape[3]
    heads_all = head_scale.shape[1]
    head_width = model_width // heads_all
    pair_cols = 2 * cols_here
    pair_heads = pair_cols // head_width
    group_rows = segment_ids.shape[0]
    half_rows = group_rows // 2
    hidden_all = fc1_weight.shape[2] * lax.axis_size("mp")
    device_index = lax.axis_index("mp")
    is_upper = device_index % 2 == 1
    own_start = jnp.where(is_upper, half_rows, 0).astype(jnp.int32)
    other_start = jnp.where(is_upper, 0, half_rows).astype(jnp.int32)
    first_head = device_index // 2 * pair_heads
    pair_onehot = (
        (first_head + jnp.arange(pair_heads, dtype=jnp.int32))[:, None]
        == jnp.arange(heads_all, dtype=jnp.int32)[None, :]
    ).astype(jnp.float32)
    residual = tokens.astype(jnp.float32)
    stored = []
    for layer_index in range(layers):
        attn_in, attn_normal, attn_factor = norm_local(
            residual, ln_attn_gain[layer_index], ln_attn_bias[layer_index]
        )
        attn_rows = collect_rows(attn_in.astype(jnp.bfloat16))
        qkv_here = qkv_weight[layer_index].reshape(model_width, 3 * cols_here)
        projected = jnp.dot(attn_rows, qkv_here, preferred_element_type=jnp.float32).reshape(
            -1, 3, cols_here
        )
        bias_pair = qv_bias[layer_index]
        query_mine = (projected[:, 0] + bias_pair[0]).astype(jnp.bfloat16)
        key_mine = projected[:, 1].astype(jnp.bfloat16)
        value_mine = (projected[:, 2] + bias_pair[1]).astype(jnp.bfloat16)
        query_send = lax.dynamic_slice_in_dim(query_mine, other_start, half_rows, 0)
        query_recv, key_recv, value_recv = partner((query_send, key_mine, value_mine), "mp", 0)
        query_own = lax.dynamic_slice_in_dim(query_mine, own_start, half_rows, 0)
        queries = join_cols(query_own, query_recv, is_upper).reshape(
            half_rows, pair_heads, head_width
        )
        key_rows = join_cols(key_mine, key_recv, is_upper).reshape(
            group_rows, pair_heads, head_width
        )
        value_rows = join_cols(value_mine, value_recv, is_upper).reshape(
            group_rows, pair_heads, head_width
        )
        attended, log_totals = attend_forward(queries, key_rows, value_rows, segment_ids, own_start)
        pair_scale = jnp.sum(pair_onehot * head_scale[layer_index][None, :], axis=1)
        scaled_half = (
            (attended * pair_scale[None, :, None])
            .astype(jnp.bfloat16)
            .reshape(half_rows, pair_cols)
        )
        own_cols, other_cols = split_cols(scaled_half, cols_here, is_upper)
        scaled_recv = partner(other_cols, "mp", 0)
        scaled_mine = join_rows(own_cols, scaled_recv, is_upper)
        branch = (
            reduce_branch(scaled_mine, out_weight[layer_index], local_rows) + out_bias[layer_index]
        )
        post_out, post_normal, post_factor = norm_local(
            branch, ln_post_gain[layer_index], ln_post_bias[layer_index]
        )
        middle = residual + post_out
        ffn_in, ffn_normal, ffn_factor = norm_local(
            middle, ln_ffn_gain[layer_index], ln_ffn_bias[layer_index]
        )
        ffn_rows = collect_rows(ffn_in.astype(jnp.bfloat16))
        before_gelu = (
            jnp.dot(ffn_rows, fc1_weight[layer_index], preferred_element_type=jnp.float32)
            + fc1_bias[layer_index]
        )
        activated = jax.nn.gelu(before_gelu, approximate=False)
        first_sum, second_sum = hidden_stats(
            jnp.sum(activated, axis=1), jnp.sum(activated * activated, axis=1)
        )
        average = first_sum / hidden_all
        spread = second_sum / hidden_all - average * average
        hidden_factor = lax.rsqrt(spread + epsilon)[:, None]
        hidden_normal = (activated - average[:, None]) * hidden_factor
        mixed_b = (hidden_normal * mid_gain[layer_index] + mid_bias[layer_index]).astype(
            jnp.bfloat16
        )
        ffn_out = reduce_branch(mixed_b, fc2_weight[layer_index], local_rows)
        stored.append(
            (
                attn_normal,
                attn_factor,
                attn_rows,
                queries,
                key_rows,
                value_rows,
                attended,
                log_totals,
                pair_scale,
                scaled_mine,
                post_normal,
                post_factor,
                ffn_normal,
                ffn_factor,
                ffn_rows,
                before_gelu,
                hidden_normal,
                hidden_factor,
                mixed_b,
            )
        )
        residual = middle + ffn_out + fc2_bias[layer_index]
    layer_output = residual.astype(jnp.bfloat16)
    gradient = cotangent.astype(jnp.float32)
    sharded_list = []
    shared_list = []
    for layer_index in reversed(range(layers)):
        (
            attn_normal,
            attn_factor,
            attn_rows,
            queries,
            key_rows,
            value_rows,
            attended,
            log_totals,
            pair_scale,
            scaled_mine,
            post_normal,
            post_factor,
            ffn_normal,
            ffn_factor,
            ffn_rows,
            before_gelu,
            hidden_normal,
            hidden_factor,
            mixed_b,
        ) = stored[layer_index]
        qkv_here = qkv_weight[layer_index].reshape(model_width, 3 * cols_here)
        second_shift_grad = jnp.sum(gradient, axis=0)
        grad_rows = collect_grads(gradient.astype(jnp.bfloat16))
        mixed_grad = jnp.einsum(
            "td,fd->tf", grad_rows, fc2_weight[layer_index], preferred_element_type=jnp.float32
        )
        second_grad = jnp.einsum(
            "tf,td->fd", mixed_b, grad_rows, preferred_element_type=jnp.float32
        )
        hidden_gain_grad = jnp.sum(mixed_grad * hidden_normal, axis=0)
        hidden_shift_grad = jnp.sum(mixed_grad, axis=0)
        normal_grad = mixed_grad * mid_gain[layer_index]
        grad_first, grad_second = hidden_grad_stats(
            jnp.sum(normal_grad, axis=1), jnp.sum(normal_grad * hidden_normal, axis=1)
        )
        active_grad = hidden_factor * (
            normal_grad
            - grad_first[:, None] / hidden_all
            - hidden_normal * grad_second[:, None] / hidden_all
        )
        gelu_pull = jax.vjp(partial(jax.nn.gelu, approximate=False), before_gelu)[1]
        pre_grad_b = gelu_pull(active_grad)[0].astype(jnp.bfloat16)
        first_shift_grad = jnp.sum(pre_grad_b, axis=0, dtype=jnp.float32)
        first_grad = jnp.einsum(
            "td,tf->df", ffn_rows, pre_grad_b, preferred_element_type=jnp.float32
        )
        ffn_in_grad = reduce_grads(pre_grad_b, fc1_weight[layer_index], local_rows)
        ffn_gain_grad = jnp.sum(ffn_in_grad * ffn_normal, axis=0)
        ffn_bias_grad = jnp.sum(ffn_in_grad, axis=0)
        middle_grad = gradient + norm_back(
            ffn_in_grad, ffn_normal, ffn_factor, ln_ffn_gain[layer_index]
        )
        post_gain_grad = jnp.sum(middle_grad * post_normal, axis=0)
        post_bias_grad = jnp.sum(middle_grad, axis=0)
        branch_grad = norm_back(middle_grad, post_normal, post_factor, ln_post_gain[layer_index])
        out_shift_grad = jnp.sum(branch_grad, axis=0)
        branch_rows = collect_grads(branch_grad.astype(jnp.bfloat16))
        scaled_grad = jnp.einsum(
            "td,cd->tc", branch_rows, out_weight[layer_index], preferred_element_type=jnp.float32
        )
        out_grad = jnp.einsum(
            "tc,td->cd", scaled_mine, branch_rows, preferred_element_type=jnp.float32
        )
        grad_send = lax.dynamic_slice_in_dim(scaled_grad, other_start, half_rows, 0)
        grad_recv = partner(grad_send.astype(jnp.bfloat16), "mp", 0).astype(grad_send.dtype)
        grad_own = lax.dynamic_slice_in_dim(scaled_grad, own_start, half_rows, 0)
        scaled_pair = join_cols(grad_own, grad_recv, is_upper).reshape(
            half_rows, pair_heads, head_width
        )
        pair_scale_grad = jnp.sum(attended * scaled_pair, axis=(0, 2))
        scale_grad = jnp.sum(pair_onehot * pair_scale_grad[:, None], axis=0)
        attended_grad_b = (scaled_pair * pair_scale[None, :, None]).astype(jnp.bfloat16)
        query_grad, key_grad, value_grad = attend_backward(
            queries, key_rows, value_rows, segment_ids, own_start, log_totals, attended_grad_b
        )
        query_own, query_other = split_cols(
            query_grad.reshape(half_rows, pair_cols), cols_here, is_upper
        )
        key_own, key_other = split_cols(
            key_grad.reshape(group_rows, pair_cols), cols_here, is_upper
        )
        value_own, value_other = split_cols(
            value_grad.reshape(group_rows, pair_cols), cols_here, is_upper
        )
        query_recv, key_recv, value_recv = (
            partner(query_other.astype(jnp.bfloat16), "mp", 0).astype(query_other.dtype),
            partner(key_other.astype(jnp.bfloat16), "mp", 0).astype(key_other.dtype),
            partner(value_other.astype(jnp.bfloat16), "mp", 0).astype(value_other.dtype),
        )
        query_grad_b = join_rows(query_own, query_recv, is_upper).astype(jnp.bfloat16)
        key_grad_b = (key_own + key_recv).astype(jnp.bfloat16)
        value_grad_b = (value_own + value_recv).astype(jnp.bfloat16)
        proj_grad = jnp.stack([query_grad_b, key_grad_b, value_grad_b], axis=1).reshape(
            -1, 3 * cols_here
        )
        pair_grad = jnp.stack(
            [
                jnp.sum(query_grad_b, axis=0, dtype=jnp.float32),
                jnp.sum(value_grad_b, axis=0, dtype=jnp.float32),
            ],
            axis=0,
        )
        qkv_grad = jnp.einsum(
            "td,tc->dc", attn_rows, proj_grad, preferred_element_type=jnp.float32
        ).reshape(model_width, 3, cols_here)
        attn_in_grad = reduce_grads(proj_grad, qkv_here, local_rows)
        attn_gain_grad = jnp.sum(attn_in_grad * attn_normal, axis=0)
        attn_bias_grad = jnp.sum(attn_in_grad, axis=0)
        gradient = middle_grad + norm_back(
            attn_in_grad, attn_normal, attn_factor, ln_attn_gain[layer_index]
        )
        sharded_list.insert(
            0,
            (
                qkv_grad,
                pair_grad,
                out_grad,
                first_grad,
                first_shift_grad,
                hidden_gain_grad,
                hidden_shift_grad,
                second_grad,
            ),
        )
        shared_list.insert(
            0,
            (
                attn_gain_grad,
                attn_bias_grad,
                scale_grad,
                out_shift_grad,
                post_gain_grad,
                post_bias_grad,
                ffn_gain_grad,
                ffn_bias_grad,
                second_shift_grad,
            ),
        )
    sharded = stack_layers(sharded_list, 8)
    shared = stack_layers(shared_list, 9)
    sharded = (
        lax.psum(sharded[0].astype(jnp.bfloat16), "rows").astype(jnp.float32),
        lax.psum(sharded[1].astype(jnp.bfloat16), "rows").astype(jnp.float32),
        lax.psum(sharded[2].astype(jnp.bfloat16), "rows").astype(jnp.float32),
        lax.psum(sharded[3].astype(jnp.bfloat16), "rows").astype(jnp.float32),
        lax.psum(sharded[4].astype(jnp.bfloat16), "rows").astype(jnp.float32),
        lax.psum(sharded[5].astype(jnp.bfloat16), "rows").astype(jnp.float32),
        lax.psum(sharded[6].astype(jnp.bfloat16), "rows").astype(jnp.float32),
        lax.psum(sharded[7].astype(jnp.bfloat16), "rows").astype(jnp.float32),
    )
    shared = lax.psum(
        (
            shared[0],
            shared[1],
            shared[2],
            shared[3],
            shared[4],
            shared[5],
            shared[6],
            shared[7],
            shared[8],
        ),
        ("rows", "mp"),
    )
    return (
        layer_output,
        gradient,
        shared[0],
        shared[1],
        sharded[0],
        sharded[1],
        shared[2],
        sharded[2],
        shared[3],
        shared[4],
        shared[5],
        shared[6],
        shared[7],
        sharded[3],
        sharded[4],
        sharded[5],
        sharded[6],
        sharded[7],
        shared[8],
    )


MESH_ID = pl.DeviceIdType.MESH
PLANE = ("core", "y", "x")
EVERY = ("y", "core", "z", "x")
f32 = jnp.float32
bf16 = jnp.bfloat16


def vmem_params(collective_id=None, mib=24):
    if collective_id is None:
        return pltpu.CompilerParams(vmem_limit_bytes=mib * 2**20)
    return pltpu.CompilerParams(
        vmem_limit_bytes=mib * 2**20, collective_id=collective_id, has_side_effects=True
    )


class Here:
    def __init__(self):
        self.x, self.y = lax.axis_index("x"), lax.axis_index("y")
        self.core, self.z = lax.axis_index("core"), lax.axis_index("z")

    def peer(self, flip_x, flip_y, flip_core, step_z):
        place = {}
        if flip_x:
            place["x"] = 1 - self.x
        if flip_y:
            place["y"] = 1 - self.y
        if flip_core:
            place["core"] = 1 - self.core
        if step_z:
            place["z"] = lax.rem(self.z + step_z, 4)
        return place

    def block(self, at_core, at_x, at_y):
        return (2 * at_core + lax.rem(at_y + self.z, 2)) * 2 + at_x


BY_X, BY_Y, BY_CORE = (1, 0, 0, 0), (0, 1, 0, 0), (0, 0, 1, 0)
BY_Z = tuple((0, 0, 0, step) for step in (1, 2, 3))
BY_LINE = BY_Z + tuple((0, 0, 1, step) for step in range(4))
BY_PLANE = tuple((flip & 1, flip >> 1 & 1, flip >> 2, 0) for flip in range(1, 8))


def remote(source, target, send_sem, recv_sem, place):
    return pltpu.make_async_remote_copy(
        src_ref=source,
        dst_ref=target,
        send_sem=send_sem,
        recv_sem=recv_sem,
        device_id=place,
        device_id_type=MESH_ID,
    )


def dma_sems(count):
    return pltpu.SemaphoreType.DMA((count,))


class Task:
    arrays = ()
    spaces = ()
    outs = ()
    out_spaces = ()
    scratch = ()
    reach = ()

    def between(self):
        pass

    def start(self, here, ins, outs, scratch):
        pass

    def middle(self, here, ins, outs, scratch):
        pass

    def finish(self, here, ins, outs, scratch):
        pass


def run_tasks(ids, *tasks, mib=24):
    reach = []
    for task in tasks:
        reach += [way for way in task.reach if way not in reach]

    def kernel(*refs):
        refs = list(refs)
        views = [[], [], []]
        for kind, name in enumerate(("arrays", "outs", "scratch")):
            for task in tasks:
                count = len(getattr(task, name))
                views[kind].append(refs[:count])
                refs = refs[count:]
        here = Here()
        barrier = pltpu.get_barrier_semaphore()
        for way in reach:
            pl.semaphore_signal(barrier, inc=1, device_id=here.peer(*way), device_id_type=MESH_ID)
        pl.semaphore_wait(barrier, len(reach))
        for task, *held in zip(tasks, *views):
            task.start(here, *held)

        def between():
            for task, *held in zip(tasks, *views):
                task.middle(here, *held)

        tasks[0].between = between
        for task, *held in zip(tasks, *views):
            task.finish(here, *held)

    results = pl.pallas_call(
        kernel,
        out_shape=[out for task in tasks for out in task.outs],
        in_specs=[pl.BlockSpec(memory_space=s) for task in tasks for s in task.spaces],
        out_specs=[pl.BlockSpec(memory_space=s) for task in tasks for s in task.out_spaces],
        scratch_shapes=[each for task in tasks for each in task.scratch],
        compiler_params=vmem_params(next(ids), mib),
    )(*[array for task in tasks for array in task.arrays])
    results = list(results)
    split = []
    for task in tasks:
        split.append(results[: len(task.outs)])
        results = results[len(task.outs) :]
    return split


class PlaneMove(Task):
    def __init__(self, values, back=False):
        self.back = back
        self.arrays, self.spaces = (values,), (pltpu.HBM,)
        self.outs = (jax.ShapeDtypeStruct(values.shape, values.dtype),)
        self.out_spaces = (pltpu.HBM,)
        self.scratch = (
            pltpu.VMEM((2, *values.shape), values.dtype),
            dma_sems(3),
            dma_sems(3),
        )
        self.reach = (BY_Y,) + BY_LINE

    def bend(self, here):
        return lax.rem(here.z + here.core, 2) == here.y

    def ends(self, here):
        targets = [{"core": here.z // 2, "z": 2 * y + here.core} for y in range(2)]
        at_home = [(here.z // 2 == here.core) & (2 * y + here.core == here.z) for y in range(2)]
        origin_core = lax.rem(here.z, 2)
        origin_z = 2 * here.core + lax.rem(here.y + origin_core, 2)
        origin_home = (origin_core == here.core) & (origin_z == here.z)
        return targets, at_home, {"core": origin_core, "z": origin_z}, origin_home

    def plan(self, here, ins, outs, scratch):
        held, send, recv = scratch
        targets, at_home, origin, origin_home = self.ends(here)
        bend = self.bend(here)
        to_y = here.peer(*BY_Y)
        legs = {}
        if not self.back:
            legs["own"] = (bend, pltpu.make_async_copy(ins[0], held.at[here.y], recv.at[1]))
            legs["over"] = (
                jnp.logical_not(bend),
                remote(ins[0], held.at[here.y], send.at[2], recv.at[0], to_y),
            )
            for y in range(2):
                away = remote(held.at[y], outs[0], send.at[y], recv.at[2], targets[y])
                stay = pltpu.make_async_copy(held.at[y], outs[0], recv.at[2])
                legs["away", y] = (bend & jnp.logical_not(at_home[y]), away)
                legs["stay", y] = (bend & at_home[y], stay)
        else:
            group = here.z // 2
            for y in range(2):
                mine = group == y
                away = remote(ins[0], held.at[y], send.at[2], recv.at[y], origin)
                stay = pltpu.make_async_copy(ins[0], held.at[y], recv.at[y])
                legs["away", y] = (mine & jnp.logical_not(origin_home), away)
                legs["stay", y] = (mine & origin_home, stay)
                own = pltpu.make_async_copy(held.at[y], outs[0], recv.at[2])
                legs["own", y] = (bend & (here.y == y), own)
                over = remote(held.at[y], outs[0], send.at[y], recv.at[2], to_y)
                legs["over", y] = (bend & (here.y != y), over)
        return legs

    def start(self, here, ins, outs, scratch):
        legs = self.plan(here, ins, outs, scratch)
        firsts = ("away", "stay") if self.back else ("own", "over")
        for key, (when, copy) in legs.items():
            if key in firsts or key[0] in firsts:
                pl.when(when)(copy.start)
        self.moved = False

    def middle(self, here, ins, outs, scratch):
        legs = self.plan(here, ins, outs, scratch)
        held, send, recv = scratch
        bend = self.bend(here)

        @pl.when(bend)
        def _():
            for slot in range(2):
                pltpu.make_async_copy(held.at[0], held.at[0], recv.at[slot]).wait()

        seconds = ("own", "over") if self.back else ("away", "stay")
        for key, (when, copy) in legs.items():
            if not isinstance(key, str) and key[0] in seconds:
                pl.when(when)(copy.start)
        self.moved = True

    def finish(self, here, ins, outs, scratch):
        if not self.moved:
            self.middle(here, ins, outs, scratch)
        legs = self.plan(here, ins, outs, scratch)
        pltpu.make_async_copy(outs[0], outs[0], scratch[2].at[2]).wait()
        for key, (when, copy) in legs.items():
            if key == "over" or key[0] in ("away", "over"):
                pl.when(when)(copy.wait_send)


class PlaneGather(Task):
    def __init__(self, block):
        rows, width = block.shape
        self.arrays, self.spaces = (block,), (pltpu.VMEM,)
        self.outs = (jax.ShapeDtypeStruct((8 * rows, width), block.dtype),)
        self.out_spaces = (pltpu.VMEM,)
        self.scratch = (dma_sems(11), dma_sems(11), pltpu.SemaphoreType.DMA)
        self.reach = (BY_X, BY_Y, BY_CORE)

    def place(self, here, o_ref, at_x, at_y, part=None):
        rows = o_ref.shape[0] // 8
        first = here.block(here.core, at_x, at_y) * rows
        if part is None:
            return o_ref.at[pl.ds(pl.multiple_of(first, rows), rows)]
        half = rows // 2
        return o_ref.at[pl.ds(pl.multiple_of(first + part * half, half), half)]

    def copies(self, here, x_ref, o_ref, send_sem, recv_sem):
        x, y = here.x, here.y
        half = x_ref.shape[0] // 2
        to_x, to_y, to_core = here.peer(*BY_X), here.peer(*BY_Y), here.peer(*BY_CORE)

        def copy(index, source, target, way):
            return remote(source, target, send_sem.at[index], recv_sem.at[index], way)

        def pass_on(index, way, *at):
            return copy(index, self.place(here, o_ref, *at), self.place(here, o_ref, *at), way)

        own = [self.place(here, o_ref, x, y, part) for part in (0, 1)]
        mine = [x_ref.at[pl.ds(part * half, half)] for part in (0, 1)]
        return [
            copy(0, mine[0], own[0], to_x),
            copy(1, mine[1], own[1], to_y),
            copy(2, mine[1], own[1], to_x),
            copy(3, mine[0], own[0], to_y),
            copy(4, x_ref, self.place(here, o_ref, x, y), to_core),
            pass_on(5, to_y, 1 - x, y, 0),
            pass_on(6, to_x, x, 1 - y, 1),
            pass_on(7, to_core, 1 - x, y),
            pass_on(8, to_core, x, 1 - y),
            pass_on(9, to_core, 1 - x, 1 - y, 0),
            pass_on(10, to_core, 1 - x, 1 - y, 1),
        ]

    def keep(self, here, x_ref, o_ref, own_sem):
        return pltpu.make_async_copy(x_ref, self.place(here, o_ref, here.x, here.y), own_sem)

    def start(self, here, ins, outs, scratch):
        copies = self.copies(here, ins[0], outs[0], scratch[0], scratch[1])
        for index in range(5):
            copies[index].start()
        self.keep(here, ins[0], outs[0], scratch[2]).start()

    def finish(self, here, ins, outs, scratch, work=None):
        rows = ins[0].shape[0]
        copies = self.copies(here, ins[0], outs[0], scratch[0], scratch[1])

        def done(flip_core, flip_x, flip_y):
            if work is not None:
                at_core = 1 - here.core if flip_core else here.core
                at_x = 1 - here.x if flip_x else here.x
                at_y = 1 - here.y if flip_y else here.y
                work(pl.multiple_of(here.block(at_core, at_x, at_y) * rows, rows))

        self.keep(here, ins[0], outs[0], scratch[2]).wait()
        done(0, 0, 0)
        copies[4].wait_recv()
        done(1, 0, 0)
        for index in range(4):
            copies[index].wait_recv()
            copies[5 + index].start()
        done(0, 1, 0)
        done(0, 0, 1)
        copies[7].wait_recv()
        done(1, 1, 0)
        copies[8].wait_recv()
        done(1, 0, 1)
        copies[5].wait_recv()
        copies[9].start()
        copies[6].wait_recv()
        copies[10].start()
        done(0, 1, 1)
        copies[9].wait_recv()
        copies[10].wait_recv()
        done(1, 1, 1)
        for each in copies:
            each.wait_send()


class PlaneScatter(Task):
    def __init__(self, rows, width, weight_dim):
        half = rows // 2
        self.weight_dim = weight_dim
        self.scratch = (
            pltpu.VMEM((4, rows, width), bf16),
            pltpu.VMEM((4, rows, width), bf16),
            pltpu.VMEM((rows, width), bf16),
            pltpu.VMEM((2, half, width), bf16),
            pltpu.VMEM((2, half, width), bf16),
            pltpu.VMEM((2, half, width), bf16),
            pltpu.VMEM((2, half, width), bf16),
            pltpu.VMEM((2, half, width), bf16),
            pltpu.VMEM((half, width), f32),
            pltpu.VMEM((half, width), f32),
            dma_sems(10),
            dma_sems(10),
        )
        self.reach = (BY_X, BY_Y, BY_CORE)

    def finish(self, here, ins, outs, scratch, rows_of, weight_of, early=None, idle=None):
        o_ref = outs[0]
        (
            sib_out,
            sib_in,
            diag_out,
            diag_in,
            last_x_out,
            last_y_out,
            last_x_in,
            last_y_in,
            wait_x,
            wait_y,
            send_sem,
            recv_sem,
        ) = scratch
        rows = o_ref.shape[0]
        half = rows // 2
        x, y, core = here.x, here.y, here.core
        to_x, to_y, to_core = here.peer(*BY_X), here.peer(*BY_Y), here.peer(*BY_CORE)

        def term(at_core, at_x, at_y):
            first = pl.multiple_of(here.block(at_core, at_x, at_y) * rows, rows)
            return lax.dot_general(
                rows_of(first),
                weight_of(),
                (((1,), (self.weight_dim,)), ((), ())),
                preferred_element_type=f32,
            )

        def copy(index, source, target, way):
            return remote(source, target, send_sem.at[index], recv_sem.at[index], way)

        places = ((1 - x, 1 - y), (1 - x, y), (x, 1 - y), (x, y))
        siblings = [copy(i, sib_out.at[i], sib_in.at[i], to_core) for i in range(4)]

        def help_sibling(i):
            sib_out[i] = term(1 - core, *places[i]).astype(bf16)
            siblings[i].start()

        def joined(i):
            mine = term(core, *places[i])
            siblings[i].wait_recv()
            return mine + sib_in[i].astype(f32)

        help_sibling(0)
        total = joined(0)
        diag_out[...] = total.astype(bf16)
        diag_x = copy(4, diag_out.at[pl.ds(0, half)], diag_in.at[0], to_x)
        diag_y = copy(5, diag_out.at[pl.ds(half, half)], diag_in.at[1], to_y)
        diag_x.start()
        diag_y.start()
        help_sibling(1)
        total = joined(1)
        last_x_out[0] = total[:half].astype(bf16)
        x_0 = copy(6, last_x_out.at[0], last_x_in.at[0], to_x)
        x_0.start()
        wait_x[...] = total[half:]
        if early is not None:
            early()
        help_sibling(2)
        total = joined(2)
        last_y_out[1] = total[half:].astype(bf16)
        y_1 = copy(7, last_y_out.at[1], last_y_in.at[1], to_y)
        y_1.start()
        wait_y[...] = total[:half]
        help_sibling(3)
        diag_y.wait_recv()
        last_x_out[1] = (wait_x[...] + diag_in[1].astype(f32)).astype(bf16)
        x_1 = copy(8, last_x_out.at[1], last_x_in.at[1], to_x)
        x_1.start()
        diag_x.wait_recv()
        last_y_out[0] = (wait_y[...] + diag_in[0].astype(f32)).astype(bf16)
        y_0 = copy(9, last_y_out.at[0], last_y_in.at[0], to_y)
        y_0.start()
        o_ref[...] = joined(3)
        if idle is not None:
            idle()
        for part, (by_x, by_y) in enumerate(((x_0, y_0), (x_1, y_1))):
            by_x.wait_recv()
            by_y.wait_recv()
            piece = pl.ds(part * half, half)
            o_ref[piece, :] += last_x_in[part].astype(f32) + last_y_in[part].astype(f32)
        for sent in (*siblings, diag_x, diag_y, x_0, y_1, x_1, y_0):
            sent.wait_send()


class PlaneSum(Task):
    def __init__(self, values):
        self.arrays, self.spaces = (values,), (pltpu.VMEM,)
        self.outs = (jax.ShapeDtypeStruct(values.shape, f32),)
        self.out_spaces = (pltpu.VMEM,)
        self.scratch = (pltpu.VMEM((7, *values.shape), f32), dma_sems(7), dma_sems(7))
        self.reach = BY_PLANE

    def copies(self, here, ins, scratch):
        got, send_sem, recv_sem = scratch
        return [
            remote(ins[0], got.at[i], send_sem.at[i], recv_sem.at[i], here.peer(*way))
            for i, way in enumerate(BY_PLANE)
        ]

    def start(self, here, ins, outs, scratch):
        for each in self.copies(here, ins, scratch):
            each.start()

    def finish(self, here, ins, outs, scratch):
        copies = self.copies(here, ins, scratch)
        for each in copies:
            each.wait_recv()
        got = scratch[0]
        by_x = [ins[0][...] + got[0]]
        for flip in (2, 4, 6):
            by_x.append(got[flip - 1] + got[flip])
        outs[0][...] = (by_x[0] + by_x[1]) + (by_x[2] + by_x[3])
        for each in copies:
            each.wait_send()


class LineGather(Task):
    def __init__(self, values):
        self.arrays, self.spaces = (values,), (pltpu.HBM,)
        self.outs = (jax.ShapeDtypeStruct((4, *values.shape), values.dtype),)
        self.out_spaces = (pltpu.HBM,)
        self.scratch = (dma_sems(4), dma_sems(3))
        self.reach = BY_Z

    def copies(self, here, ins, outs, scratch):
        target = outs[0].at[here.z]
        keep = pltpu.make_async_copy(ins[0], target, scratch[0].at[3])
        return keep, [
            remote(ins[0], target, scratch[0].at[i], scratch[1].at[i], here.peer(*way))
            for i, way in enumerate(BY_Z)
        ]

    def start(self, here, ins, outs, scratch):
        keep, copies = self.copies(here, ins, outs, scratch)
        for each in copies:
            each.start()
        keep.start()

    def finish(self, here, ins, outs, scratch):
        keep, copies = self.copies(here, ins, outs, scratch)
        for each in copies:
            each.wait()
        keep.wait()


class HeadGather(Task):
    def __init__(self, qkv, out, layer, midway=False):
        _, kinds, both, width = qkv.shape
        self.layer, self.midway = layer, midway
        self.arrays, self.spaces = (qkv, out), (pltpu.HBM,) * 2
        self.outs = (jax.ShapeDtypeStruct((kinds + 1, 2, both // 2, width), qkv.dtype),)
        self.out_spaces = (pltpu.HBM,)
        self.scratch = (dma_sems(8), dma_sems(8))
        self.reach = BY_LINE

    def pieces(self, outs, shard, part):
        half = outs[0].shape[3] // 2
        columns = pl.ds(pl.multiple_of(part * half, half), half)
        return outs[0].at[pl.ds(0, 3), shard, :, columns], outs[0].at[3, shard, :, columns]

    def copies(self, here, ins, outs, scratch):
        shard, target_core = lax.rem(here.z, 2), here.z // 2
        wide, half = outs[0].shape[2], outs[0].shape[3] // 2
        rows = pl.ds(pl.multiple_of(here.y * wide, wide), wide)
        columns = pl.ds(pl.multiple_of(here.core * half, half), half)
        sources = (ins[0].at[self.layer, :, rows, columns], ins[1].at[self.layer, rows, columns])
        targets = self.pieces(outs, shard, here.core)
        keeps, aways = [], []
        for kind in range(2):
            recv_sem = scratch[1].at[4 * kind + 2 * shard + here.core]
            keeps.append(pltpu.make_async_copy(sources[kind], targets[kind], recv_sem))
            for step in range(4):
                place = {"core": target_core, "z": lax.rem(here.z + step, 4)}
                send_sem = scratch[0].at[4 * kind + step]
                aways.append(remote(sources[kind], targets[kind], send_sem, recv_sem, place))
        return keeps, aways

    def begin(self, here, ins, outs, scratch):
        keeps, aways = self.copies(here, ins, outs, scratch)
        for index, each in enumerate(aways):
            if index % 4:
                each.start()
        at_home = here.z // 2 == here.core
        for kind in range(2):
            pl.when(at_home)(keeps[kind].start)
            pl.when(jnp.logical_not(at_home))(aways[4 * kind].start)

    def start(self, *held):
        if not self.midway:
            self.begin(*held)

    def middle(self, *held):
        if self.midway:
            self.begin(*held)

    def finish(self, here, ins, outs, scratch):
        keeps, aways = self.copies(here, ins, outs, scratch)
        for shard in range(2):
            for part in range(2):
                for kind, piece in enumerate(self.pieces(outs, shard, part)):
                    recv_sem = scratch[1].at[4 * kind + 2 * shard + part]
                    pltpu.make_async_copy(piece, piece, recv_sem).wait()
        for index, each in enumerate(aways):
            if index % 4:
                each.wait_send()
        for kind in range(2):
            pl.when(here.z // 2 != here.core)(aways[4 * kind].wait_send)


class LineScatter(Task):
    def __init__(self, values):
        shape = values.shape[1:]
        self.arrays, self.spaces = (values,), (pltpu.VMEM,)
        self.outs, self.out_spaces = (jax.ShapeDtypeStruct(shape, values.dtype),), (pltpu.VMEM,)
        self.scratch = (pltpu.VMEM((3, *shape), values.dtype), dma_sems(3), dma_sems(3))
        self.reach = BY_Z

    def copies(self, here, ins, scratch):
        got, send_sem, recv_sem = scratch
        return [
            remote(
                ins[0].at[lax.rem(here.z + i + 1, 4)],
                got.at[i],
                send_sem.at[i],
                recv_sem.at[i],
                here.peer(*way),
            )
            for i, way in enumerate(BY_Z)
        ]

    def start(self, here, ins, outs, scratch):
        for each in self.copies(here, ins, scratch):
            each.start()

    def finish(self, here, ins, outs, scratch):
        copies = self.copies(here, ins, scratch)
        for each in copies:
            each.wait_recv()
        total = ins[0][here.z].astype(f32)
        for i in range(3):
            total = total + scratch[0][i].astype(f32)
        outs[0][...] = total.astype(outs[0].dtype)
        for each in copies:
            each.wait_send()


class HeadScatter(Task):
    def __init__(self, values):
        kinds, _, wide, width = values.shape
        shape = (kinds, wide, width // 2)
        self.arrays, self.spaces = (values,), (pltpu.VMEM,)
        self.outs, self.out_spaces = (jax.ShapeDtypeStruct(shape, values.dtype),), (pltpu.VMEM,)
        self.scratch = (pltpu.VMEM((4, *shape), values.dtype), dma_sems(4), dma_sems(4))
        self.reach = BY_LINE

    def copies(self, here, ins, scratch):
        got, send_sem, recv_sem = scratch
        half = ins[0].shape[3] // 2
        triples = []
        for shard in range(2):
            for part in range(2):
                source = ins[0].at[:, shard, :, pl.ds(part * half, half)]
                target_z = 2 * here.core + shard
                slot = recv_sem.at[here.z]
                away = remote(
                    source,
                    got.at[here.z],
                    send_sem.at[2 * shard + part],
                    slot,
                    {"core": part, "z": target_z},
                )
                stay = pltpu.make_async_copy(source, got.at[here.z], slot)
                at_home = (target_z == here.z) & (here.core == part)
                triples.append((away, stay, at_home))
        return triples

    def start(self, here, ins, outs, scratch):
        for away, stay, at_home in self.copies(here, ins, scratch):
            pl.when(at_home)(stay.start)
            pl.when(jnp.logical_not(at_home))(away.start)

    def finish(self, here, ins, outs, scratch):
        got, send_sem, recv_sem = scratch
        for plane in range(4):
            pltpu.make_async_copy(got.at[plane], got.at[plane], recv_sem.at[plane]).wait()
        total = got[0].astype(f32)
        for plane in range(1, 4):
            total = total + got[plane].astype(f32)
        outs[0][...] = total.astype(outs[0].dtype)
        for away, stay, at_home in self.copies(here, ins, scratch):
            pl.when(jnp.logical_not(at_home))(away.wait_send)


class RowsGather(Task):
    def __init__(self, values):
        self.arrays, self.spaces = (values,), (pltpu.HBM,)
        self.outs = (jax.ShapeDtypeStruct((4, *values.shape), values.dtype),)
        self.out_spaces = (pltpu.HBM,)
        self.scratch = (dma_sems(4), dma_sems(3))
        self.reach = (BY_Y, BY_CORE)

    def copies(self, here, ins, outs, scratch):
        send_sem, recv_sem = scratch
        own = outs[0].at[2 * here.y + here.core]
        over = outs[0].at[2 * (1 - here.y) + here.core]
        to_y, to_core = here.peer(*BY_Y), here.peer(*BY_CORE)
        return (
            pltpu.make_async_copy(ins[0], own, send_sem.at[3]),
            remote(ins[0], own, send_sem.at[0], recv_sem.at[0], to_y),
            remote(ins[0], own, send_sem.at[1], recv_sem.at[1], to_core),
            remote(over, over, send_sem.at[2], recv_sem.at[2], to_core),
        )

    def start(self, here, ins, outs, scratch):
        keep, by_y, by_core, again = self.copies(here, ins, outs, scratch)
        by_y.start()
        by_core.start()
        keep.start()

    def finish(self, here, ins, outs, scratch):
        keep, by_y, by_core, again = self.copies(here, ins, outs, scratch)
        by_y.wait_recv()
        again.start()
        by_core.wait_recv()
        again.wait_recv()
        for each in (by_y, by_core, again):
            each.wait_send()
        keep.wait()


class PlaneThenLineSum(Task):
    def __init__(self, values, ready):
        rows, width = values.shape
        both = (rows + ready.shape[0], width)
        self.plane = PlaneSum(values)
        self.arrays, self.spaces = (values, ready), (pltpu.VMEM,) * 2
        self.outs, self.out_spaces = (jax.ShapeDtypeStruct(both, f32),), (pltpu.VMEM,)
        self.scratch = (
            *self.plane.scratch,
            pltpu.VMEM((4, *both), f32),
            pltpu.VMEM(both, f32),
            dma_sems(3),
            dma_sems(4),
        )
        self.reach = BY_PLANE + BY_Z

    def start(self, here, ins, outs, scratch):
        self.plane.start(here, ins[:1], None, scratch[:3])

    def finish(self, here, ins, outs, scratch):
        got, mine, send_sem, recv_sem = scratch[3:]
        rows = ins[0].shape[0]
        first = ins[1].shape[0]
        self.plane.finish(here, ins[:1], (mine.at[pl.ds(first, rows)],), scratch[:3])
        mine[:first, :] = ins[1][...]
        copies = [
            remote(mine, got.at[here.z], send_sem.at[i], recv_sem.at[here.z], here.peer(*way))
            for i, way in enumerate(BY_Z)
        ]
        for each in copies:
            each.start()
        keep = pltpu.make_async_copy(mine, got.at[here.z], recv_sem.at[here.z])
        keep.start()
        for plane in range(4):
            pltpu.make_async_copy(got.at[plane], got.at[plane], recv_sem.at[plane]).wait()
        outs[0][...] = (got[0] + got[1]) + (got[2] + got[3])
        for each in copies:
            each.wait_send()


def to_columns(upper, lower):
    place = lax.broadcasted_iota(jnp.int32, (128, upper.shape[1]), 0)
    return jnp.transpose(jnp.where(place < 64, upper, lower))


def both_columns(upper, lower):
    lane = lax.broadcasted_iota(jnp.int32, (upper.shape[0], 128), 1)
    return jnp.where(lane < 64, upper, lower)


def in_chunks(rows, chunk, step):
    def one(index, carry):
        step(pl.multiple_of(index * chunk, chunk))
        return carry

    lax.fori_loop(0, rows // chunk, one, 0)


def fold(values):
    total = values[:8]
    for first in range(8, values.shape[0], 8):
        total = total + values[first : first + 8]
    return total


class Parts(Task):
    def use(self, **parts):
        self.parts = parts
        self.scratch = list(self.scratch)
        self.at = {}
        reach = []
        for name, part in parts.items():
            self.at[name] = (len(self.scratch), len(self.scratch) + len(part.scratch))
            self.scratch += list(part.scratch)
            reach += [way for way in part.reach if way not in reach]
        self.reach = reach

    def held(self, scratch, name):
        first, last = self.at[name]
        return scratch[first:last]


CHUNK = 32


class FfnForward(Parts):
    def __init__(self, block, first, second, shift, gain, bias, layer, late):
        rows, width = block.shape
        hidden = first.shape[1]
        self.late = late
        self.arrays = (block, first, second, shift, gain, bias)
        self.spaces = (pltpu.VMEM,) * 2 + (pltpu.HBM if late else pltpu.VMEM,) + (pltpu.VMEM,) * 3
        self.outs = (
            jax.ShapeDtypeStruct((rows, width), f32),
            jax.ShapeDtypeStruct((8 * rows, width), bf16),
            jax.ShapeDtypeStruct((8 * rows, hidden), f32),
            jax.ShapeDtypeStruct((8 * rows, hidden), f32),
            jax.ShapeDtypeStruct((8 * rows, hidden), bf16),
            jax.ShapeDtypeStruct((2, 8 * rows), f32),
        )
        self.out_spaces = (pltpu.VMEM,) + (pltpu.HBM,) * 4 + (pltpu.VMEM,)
        self.scratch = (
            pltpu.VMEM((8 * rows, width), bf16),
            pltpu.VMEM((8 * rows, hidden), f32),
            pltpu.VMEM((8 * rows, hidden), f32),
            pltpu.VMEM((8 * rows, hidden), bf16),
            pltpu.VMEM((2, 8 * rows), f32),
            pltpu.VMEM((rows, 128), f32),
            dma_sems(4),
        )
        parts = dict(
            gather=PlaneGather(block),
            scatter=PlaneScatter(rows, width, 0),
            sums=PlaneSum(jax.ShapeDtypeStruct((2, 8 * rows), f32)),
        )
        if late:
            parts["second"] = WeightGather(second, layer, 0)
            self.outs += parts["second"].outs
            self.out_spaces += (pltpu.VMEM,)
        self.use(**parts)

    def start(self, here, ins, outs, scratch):
        self.parts["gather"].start(here, ins[:1], scratch[:1], self.held(scratch, "gather"))
        if self.late:
            held = self.held(scratch, "second")
            self.parts["second"].start(here, ins[2:3], outs[6:7], held)

    def finish(self, here, ins, outs, scratch):
        block_ref, first_ref, second_ref, shift_ref, gain_ref, bias_ref = ins
        out_ref, rows_out, slope_out, normal_out, mixed_out, total_ref = outs[:6]
        if self.late:
            second_ref = outs[6]
        rows_buf, before, active, mixed, sums, columns, save = scratch[:7]
        rows = block_ref.shape[0]
        hidden_all = 8 * first_ref.shape[1]

        def work(first):
            before[pl.ds(first, rows), :] = lax.dot_general(
                rows_buf[pl.ds(first, rows), :],
                first_ref[...],
                (((1,), (0,)), ((), ())),
                preferred_element_type=f32,
            )

            def step(at):
                piece = pl.ds(pl.multiple_of(first + at, CHUNK), CHUNK)
                u = before[piece, :] + shift_ref[...]
                area = 0.5 * (1.0 + lax.erf(u * 0.5**0.5))
                a = u * area
                active[piece, :] = a
                before[piece, :] = area + u * (jnp.exp(-0.5 * u * u) * (0.5 / jnp.pi) ** 0.5)
                columns[pl.ds(at, CHUNK), :] = both_columns(
                    jnp.sum(a, axis=1, keepdims=True), jnp.sum(a * a, axis=1, keepdims=True)
                )

            in_chunks(rows, CHUNK, step)
            turned = jnp.transpose(columns[...])
            sums[0:1, pl.ds(first, rows)] = turned[0:1]
            sums[1:2, pl.ds(first, rows)] = turned[64:65]

        self.parts["gather"].finish(
            here, ins[:1], scratch[:1], self.held(scratch, "gather"), work
        )
        held = self.held(scratch, "sums")
        self.parts["sums"].start(here, (sums,), None, held)
        keep_rows = pltpu.make_async_copy(rows_buf, rows_out, save.at[0])
        keep_rows.start()
        keep_slope = pltpu.make_async_copy(before, slope_out, save.at[1])
        keep_slope.start()
        self.parts["sums"].finish(here, (sums,), (total_ref,), held)
        if self.late:
            held = self.held(scratch, "second")
            self.parts["second"].finish(here, ins[2:3], outs[6:7], held)
        self.between()

        def rows_of(first):
            average = total_ref[0:1, pl.ds(first, rows)] / hidden_all
            spread = total_ref[1:2, pl.ds(first, rows)] / hidden_all - average * average
            columns[...] = to_columns(average, lax.rsqrt(spread + epsilon))

            def step(at):
                piece = pl.ds(pl.multiple_of(first + at, CHUNK), CHUNK)
                pair = columns[pl.ds(at, CHUNK), :]
                normal = (active[piece, :] - pair[:, 0:1]) * pair[:, 64:65]
                active[piece, :] = normal
                mixed[piece, :] = (normal * gain_ref[...] + bias_ref[...]).astype(bf16)

            in_chunks(rows, CHUNK, step)
            return mixed[pl.ds(first, rows), :]

        keep_mixed = pltpu.make_async_copy(mixed, mixed_out, save.at[2])
        keep_normal = pltpu.make_async_copy(active, normal_out, save.at[3])

        def idle():
            keep_mixed.start()
            keep_normal.start()

        self.parts["scatter"].finish(
            here,
            None,
            (out_ref,),
            self.held(scratch, "scatter"),
            rows_of,
            lambda: second_ref[...],
            idle=idle,
        )
        for each in (keep_rows, keep_slope, keep_mixed, keep_normal):
            each.wait()


class FfnBackward(Parts):
    def __init__(self, block, first, second, gain, slope, normal, mixed, ffn_rows, totals):
        rows, width = block.shape
        hidden = second.shape[0]
        self.arrays = (block, first, second, gain, totals, slope, normal, mixed, ffn_rows)
        self.spaces = (pltpu.VMEM,) * 5 + (pltpu.HBM,) * 4
        self.outs = (
            jax.ShapeDtypeStruct((rows, width), f32),
            jax.ShapeDtypeStruct((4, width, hidden // 4), bf16),
            jax.ShapeDtypeStruct((hidden // 4, width), bf16),
            jax.ShapeDtypeStruct((3, hidden), f32),
        )
        self.out_spaces = (pltpu.VMEM,) * 4
        self.scratch = (
            pltpu.VMEM((8 * rows, width), bf16),
            pltpu.VMEM((8 * rows, hidden), f32),
            pltpu.VMEM((8 * rows, hidden), f32),
            pltpu.VMEM((8 * rows, hidden), f32),
            pltpu.VMEM((8 * rows, hidden), bf16),
            pltpu.VMEM((8 * rows, width), bf16),
            pltpu.VMEM((8 * rows, hidden), bf16),
            pltpu.VMEM((hidden, width), f32),
            pltpu.VMEM((2, 8 * rows), f32),
            pltpu.VMEM((2, 8 * rows), f32),
            pltpu.VMEM((rows, 128), f32),
            pltpu.VMEM((rows, 128), f32),
            pltpu.VMEM((3, 8, hidden), f32),
            dma_sems(4),
            pltpu.VMEM((4, hidden // 4, width), bf16),
        )
        self.use(
            gather=PlaneGather(block),
            scatter=PlaneScatter(rows, width, 1),
            second=LineScatter(jax.ShapeDtypeStruct((4, hidden // 4, width), bf16)),
            sums=PlaneSum(jax.ShapeDtypeStruct((2, 8 * rows), f32)),
        )

    def loads(self, ins, scratch):
        targets = (scratch[2], scratch[4], scratch[1], scratch[5])
        return [
            pltpu.make_async_copy(source, target, scratch[13].at[i])
            for i, (source, target) in enumerate(zip((ins[6], ins[7], ins[5], ins[8]), targets))
        ]

    def start(self, here, ins, outs, scratch):
        self.parts["gather"].start(here, ins[:1], scratch[:1], self.held(scratch, "gather"))
        for each in self.loads(ins, scratch):
            each.start()

    def finish(self, here, ins, outs, scratch):
        block_ref, first_ref, second_ref, gain_ref, totals_ref = ins[:5]
        out_ref, first_grad, second_quarter, small_ref = outs
        second_grad = scratch[14]
        (
            rows_buf,
            slope,
            normal_buf,
            grads,
            mixed,
            ffn_rows,
            pre_grad,
            second_sum,
            sums,
            got,
            columns,
            factors,
            small,
        ) = scratch[:13]
        rows = block_ref.shape[0]
        hidden_all = 8 * first_ref.shape[1]
        load_normal, load_mixed, load_slope, load_rows = self.loads(ins, scratch)
        load_normal.wait()
        load_mixed.wait()
        second_sum[...] = jnp.zeros_like(second_sum)
        small[...] = jnp.zeros_like(small)

        def factor_columns(first):
            average = totals_ref[0:1, pl.ds(first, rows)] / hidden_all
            spread = totals_ref[1:2, pl.ds(first, rows)] / hidden_all - average * average
            factors[...] = to_columns(average, lax.rsqrt(spread + epsilon))

        def work(first):
            block = pl.ds(first, rows)
            grads[block, :] = lax.dot_general(
                rows_buf[block, :],
                second_ref[...],
                (((1,), (1,)), ((), ())),
                preferred_element_type=f32,
            )
            second_sum[...] += lax.dot_general(
                mixed[block, :],
                rows_buf[block, :],
                (((0,), (0,)), ((), ())),
                preferred_element_type=f32,
            )

            def step(at):
                piece = pl.ds(pl.multiple_of(first + at, CHUNK), CHUNK)
                normal = normal_buf[piece, :]
                grad = grads[piece, :]
                small[0] += fold(grad * normal)
                small[1] += fold(grad)
                scaled = grad * gain_ref[...]
                grads[piece, :] = scaled
                columns[pl.ds(at, CHUNK), :] = both_columns(
                    jnp.sum(scaled, axis=1, keepdims=True),
                    jnp.sum(scaled * normal, axis=1, keepdims=True),
                )

            in_chunks(rows, CHUNK, step)
            turned = jnp.transpose(columns[...])
            sums[0:1, pl.ds(first, rows)] = turned[0:1]
            sums[1:2, pl.ds(first, rows)] = turned[64:65]

        self.parts["gather"].finish(
            here, ins[:1], scratch[:1], self.held(scratch, "gather"), work
        )
        held = self.held(scratch, "sums")
        self.parts["sums"].start(here, (sums,), None, held)
        second_grad[...] = second_sum[...].astype(bf16).reshape(second_grad.shape)
        self.parts["second"].start(here, (second_grad,), None, self.held(scratch, "second"))
        self.parts["sums"].finish(here, (sums,), (got,), held)
        load_slope.wait()
        self.between()

        def rows_of(first):
            factor_columns(first)
            columns[...] = to_columns(
                got[0:1, pl.ds(first, rows)] / hidden_all,
                got[1:2, pl.ds(first, rows)] / hidden_all,
            )

            def step(at):
                piece = pl.ds(pl.multiple_of(first + at, CHUNK), CHUNK)
                pair = columns[pl.ds(at, CHUNK), :]
                factor = factors[pl.ds(at, CHUNK), :][:, 64:65]
                active_grad = factor * (
                    grads[piece, :] - pair[:, 0:1] - normal_buf[piece, :] * pair[:, 64:65]
                )
                rounded = (active_grad * slope[piece, :]).astype(bf16)
                pre_grad[piece, :] = rounded
                small[2] += fold(rounded.astype(f32))

            in_chunks(rows, CHUNK, step)
            return pre_grad[pl.ds(first, rows), :]

        def idle():
            load_rows.wait()
            whole = lax.dot_general(
                ffn_rows[...],
                pre_grad[...],
                (((0,), (0,)), ((), ())),
                preferred_element_type=f32,
            ).astype(bf16)
            part = first_grad.shape[2]
            for i in range(4):
                first_grad[i] = whole[:, i * part : (i + 1) * part]

        self.parts["scatter"].finish(
            here,
            None,
            (out_ref,),
            self.held(scratch, "scatter"),
            rows_of,
            lambda: first_ref[...],
            idle=idle,
        )
        held = self.held(scratch, "second")
        self.parts["second"].finish(here, (second_grad,), (second_quarter,), held)
        for i in range(3):
            small_ref[i : i + 1, :] = jnp.sum(small[i], axis=0, keepdims=True)


class WeightGather(Task):
    def __init__(self, weights, layer, axis, midway=False):
        self.layer, self.axis, self.midway = layer, axis, midway
        self.arrays, self.spaces = (weights,), (pltpu.HBM,)
        self.outs = (jax.ShapeDtypeStruct(weights.shape[1:], weights.dtype),)
        self.out_spaces = (pltpu.HBM,)
        self.scratch = (dma_sems(4), dma_sems(3))
        self.reach = BY_Z

    def copies(self, here, ins, outs, scratch):
        part = outs[0].shape[self.axis] // 4

        def cut(ref, at):
            piece = pl.ds(pl.multiple_of(at * part, part), part)
            return ref.at[piece, :] if self.axis == 0 else ref.at[:, piece]

        source = cut(ins[0].at[self.layer], 2 * here.y + here.core)
        target = cut(outs[0], here.z)
        keep = pltpu.make_async_copy(source, target, scratch[0].at[3])
        return keep, [
            remote(source, target, scratch[0].at[i], scratch[1].at[i], here.peer(*way))
            for i, way in enumerate(BY_Z)
        ]

    def begin(self, here, ins, outs, scratch):
        keep, copies = self.copies(here, ins, outs, scratch)
        for each in copies:
            each.start()
        keep.start()

    def start(self, *held):
        if not self.midway:
            self.begin(*held)

    def middle(self, *held):
        if self.midway:
            self.begin(*held)

    def finish(self, here, ins, outs, scratch):
        keep, copies = self.copies(here, ins, outs, scratch)
        for each in copies:
            each.wait()
        keep.wait()


class LineThenRows(Parts):
    moved = False

    def __init__(self, values):
        shape = jax.ShapeDtypeStruct(values.shape[1:], values.dtype)
        self.arrays, self.spaces = (values,), (pltpu.VMEM,)
        self.outs = (jax.ShapeDtypeStruct((4, *shape.shape), values.dtype),)
        self.out_spaces = (pltpu.HBM,)
        self.scratch = (pltpu.VMEM(shape.shape, values.dtype),)
        self.use(line=LineScatter(values), rows=RowsGather(shape))

    def start(self, here, ins, outs, scratch):
        self.parts["line"].start(here, ins, None, self.held(scratch, "line"))

    def middle(self, here, ins, outs, scratch):
        self.parts["line"].finish(here, ins, scratch[:1], self.held(scratch, "line"))
        self.parts["rows"].start(here, scratch[:1], outs, self.held(scratch, "rows"))
        self.moved = True

    def finish(self, here, ins, outs, scratch):
        if not self.moved:
            self.middle(here, ins, outs, scratch)
        self.parts["rows"].finish(here, scratch[:1], outs, self.held(scratch, "rows"))


BLOCK = 256
SPAN = 512


def head_masks(head_width, width):
    lane = lax.broadcasted_iota(jnp.int32, (1, width), 1)
    lower = (lane < head_width).astype(bf16)
    return lower, (1 - lower).astype(bf16)


def by_head(values, head_width):
    lower, upper = head_masks(head_width, values.shape[1])
    return jnp.concatenate([values * lower, values * upper], axis=0)


def from_heads(pair, head_width):
    rows = pair.shape[0] // 2
    lane = lax.broadcasted_iota(jnp.int32, (rows, pair.shape[1]), 1)
    return jnp.where(lane < head_width, pair[:rows], pair[rows:])


def tile_facts(doc_ref, first, key_first, keys):
    docs = doc_ref[:, pl.ds(first, BLOCK)]
    docs = jnp.concatenate([docs, docs], axis=1)
    key_docs = doc_ref[:, pl.ds(pl.multiple_of(key_first, keys), keys)]
    key_docs = jnp.transpose(jnp.broadcast_to(key_docs, (128, keys)))[:, 0:1]
    place = lax.broadcasted_iota(jnp.int32, (keys, 2 * BLOCK), 1)
    place = jnp.where(place >= BLOCK, place - BLOCK, place) + (first - key_first)
    allowed = (docs == key_docs) & (place >= lax.broadcasted_iota(jnp.int32, place.shape, 0))
    return docs, allowed


def attend_block(
    head_width, first, q_ref, k_ref, v_cols, doc_ref, o_ref, l_ref, s_buf, acc, top, total
):
    block = first // BLOCK
    last = first // SPAN
    pair = by_head(q_ref[pl.ds(first, BLOCK), :], head_width)

    def scores(at):
        keys = k_ref[pl.ds(pl.multiple_of(at * SPAN, SPAN), SPAN), :]
        return lax.dot_general(keys, pair, (((1,), (1,)), ((), ())), preferred_element_type=f32)

    top[...] = jnp.full_like(top, masked)

    def first_pass(at, carry):
        s = scores(at)
        s_buf[at] = s
        peak = s[:8]
        for row in range(8, SPAN, 8):
            peak = jnp.maximum(peak, s[row : row + 8])
        top[...] = jnp.maximum(top[...], peak)
        return carry

    lax.fori_loop(0, last, first_pass, 0)
    docs, allowed = tile_facts(doc_ref, first, last * SPAN, SPAN)
    s = jnp.where(allowed, scores(last), masked)
    shift = jnp.where(docs == 0, 0.0, masked)
    peak = jnp.maximum(
        jnp.max(top[...], axis=0, keepdims=True) + shift, jnp.max(s, axis=0, keepdims=True)
    )

    def weigh(at, p):
        values = v_cols[:, pl.ds(pl.multiple_of(at * SPAN, SPAN), SPAN)]
        return jnp.dot(values, p.astype(bf16), preferred_element_type=f32)

    p = jnp.exp(s - peak)
    total[...] = fold(p)
    acc[...] = weigh(last, p)
    base = peak - shift

    def second_pass(at, carry):
        p = jnp.exp(s_buf[at] - base)
        total[...] += fold(p)
        acc[...] += weigh(at, p)
        return carry

    lax.fori_loop(0, last, second_pass, 0)
    sums = jnp.sum(total[...], axis=0, keepdims=True)
    out = from_heads(jnp.transpose(acc[...] / sums), head_width)
    o_ref[pl.ds(first, BLOCK), :] = out
    l_ref[block] = peak + jnp.log(sums)
    return out


def attend_block_back(
    head_width,
    first,
    do,
    q_ref,
    k_ref,
    k_cols,
    v_ref,
    o_ref,
    l_ref,
    doc_ref,
    acc_k,
    acc_v,
    acc_q,
):
    block = first // BLOCK
    rows = pl.ds(first, BLOCK)
    pair_q = by_head(q_ref[rows, :], head_width)
    pair_do = by_head(do, head_width)
    out = o_ref[rows, :]
    inner = jnp.sum(
        jnp.concatenate([out, out], axis=0) * pair_do.astype(f32), axis=1, keepdims=True
    )
    inner = jnp.transpose(jnp.broadcast_to(inner, (2 * BLOCK, 128)))[0:1, :]
    logs = l_ref[block]
    docs, allowed = tile_facts(doc_ref, first, first, BLOCK)

    def step(at, base, allowed):
        piece = pl.ds(pl.multiple_of(at * BLOCK, BLOCK), BLOCK)
        s = lax.dot_general(
            k_ref[piece, :], pair_q, (((1,), (1,)), ((), ())), preferred_element_type=f32
        )
        dp = lax.dot_general(
            v_ref[piece, :], pair_do, (((1,), (1,)), ((), ())), preferred_element_type=f32
        )
        p = jnp.exp(s - base)
        if allowed is not None:
            p = jnp.where(allowed, p, 0.0)
        ds = (p * (dp - inner)).astype(bf16)
        acc_v[piece, :] += jnp.dot(p.astype(bf16), pair_do, preferred_element_type=f32)
        acc_k[piece, :] += jnp.dot(ds, pair_q, preferred_element_type=f32)
        return jnp.dot(k_cols[:, piece], ds, preferred_element_type=f32)

    acc_q[...] = step(block, logs, allowed)
    base = jnp.where(docs == 0, logs, -masked)

    def earlier(at, carry):
        acc_q[...] += step(at, base, None)
        return carry

    lax.fori_loop(0, block, earlier, 0)
    grad = from_heads(jnp.transpose(acc_q[...]), head_width)
    return (grad * head_width**-0.5).astype(bf16)


def turned(values):
    return jnp.transpose(values.astype(f32)).astype(bf16)


class AttnForward(Parts):
    def __init__(self, block, docs, scale, heads, biases, wide, layer, late):
        rows, width = block.shape
        self.head_width, self.layer, self.late = wide, layer, late
        here = 2 * wide
        self.arrays = (block, docs, scale, biases, *heads)
        self.spaces = (pltpu.VMEM,) * 3 + (pltpu.HBM if late else pltpu.VMEM,) * (1 + len(heads))
        column = jax.ShapeDtypeStruct((8 * rows, here), bf16)
        self.outs = (
            jax.ShapeDtypeStruct((rows, width), f32),
            jax.ShapeDtypeStruct((8 * rows, width), bf16),
            column,
            column,
            column,
            column,
            jax.ShapeDtypeStruct((8 * rows, here), f32),
            jax.ShapeDtypeStruct((8 * rows // BLOCK, 1, 2 * BLOCK), f32),
        )
        self.out_spaces = (pltpu.VMEM, pltpu.HBM) + (pltpu.VMEM,) * 6
        self.scratch = (
            pltpu.VMEM((8 * rows, width), bf16),
            pltpu.VMEM((here, 8 * rows), bf16),
            pltpu.VMEM((8 * rows // SPAN, SPAN, 2 * BLOCK), f32),
            pltpu.VMEM((here, 2 * BLOCK), f32),
            pltpu.VMEM((8, 2 * BLOCK), f32),
            pltpu.VMEM((8, 2 * BLOCK), f32),
            dma_sems(1),
        )
        parts = dict(gather=PlaneGather(block), scatter=PlaneScatter(rows, width, 0))
        if late:
            parts.update(heads=HeadGather(*heads, layer), biases=LineGather(biases))
            self.outs += parts["heads"].outs + parts["biases"].outs
            self.out_spaces += (pltpu.VMEM,) * 2
        self.use(**parts)

    def start(self, here, ins, outs, scratch):
        self.parts["gather"].start(here, ins[:1], scratch[:1], self.held(scratch, "gather"))
        if self.late:
            self.parts["heads"].start(here, ins[4:6], outs[8:9], self.held(scratch, "heads"))
            self.parts["biases"].start(here, ins[3:4], outs[9:10], self.held(scratch, "biases"))

    def finish(self, here, ins, outs, scratch):
        block_ref, doc_ref, scale_ref = ins[:3]
        heads_ref, bias_ref = outs[8:10] if self.late else (ins[4], ins[3])
        out_ref, rows_out, q_ref, k_ref, v_ref, z_ref, o_ref, l_ref = outs[:8]
        rows_buf, v_cols, s_buf, acc, top, total, save = scratch[:7]
        rows, model_width = block_ref.shape
        wide = self.head_width
        width = 2 * wide

        def bias_row(at):
            pair = [
                bias_ref[2 * here.core + i, self.layer : self.layer + 1, at : at + width]
                for i in range(2)
            ]
            lane = lax.broadcasted_iota(jnp.int32, (1, width), 1)
            return jnp.where(lane < wide, pair[0], pair[1])

        def work(first):
            block = pl.ds(first, rows)
            projected = lax.dot_general(
                rows_buf[block, :],
                heads_ref[0:3].reshape(3 * width, model_width),
                (((1,), (1,)), ((), ())),
                preferred_element_type=f32,
            )
            q = (projected[:, :width] + bias_row(0)).astype(bf16).astype(f32)
            q_ref[block, :] = (q * wide**-0.5).astype(bf16)
            k_ref[block, :] = projected[:, width : 2 * width].astype(bf16)
            v = (projected[:, 2 * width :] + bias_row(width)).astype(bf16)
            v_ref[block, :] = v
            v_cols[:, block] = turned(v)

        self.parts["gather"].finish(
            here,
            ins[:1],
            scratch[:1],
            self.held(scratch, "gather"),
            None if self.late else work,
        )
        keep_rows = pltpu.make_async_copy(rows_buf, rows_out, save.at[0])
        keep_rows.start()
        if self.late:
            self.parts["heads"].finish(here, ins[4:6], outs[8:9], self.held(scratch, "heads"))
            self.parts["biases"].finish(here, ins[3:4], outs[9:10], self.held(scratch, "biases"))
            in_chunks(8 * rows, rows, work)
        self.between()

        def rows_of(first):
            out = attend_block(
                wide, first, q_ref, k_ref, v_cols, doc_ref, o_ref, l_ref, s_buf, acc, top, total
            )
            z = (out * scale_ref[...]).astype(bf16)
            z_ref[pl.ds(first, rows), :] = z
            return z

        self.parts["scatter"].finish(
            here,
            None,
            (out_ref,),
            self.held(scratch, "scatter"),
            rows_of,
            lambda: heads_ref[3].reshape(width, model_width),
        )
        keep_rows.wait()


class AttnBackward(Parts):
    def __init__(self, block, docs, scale, heads, q, k, v, z, o, logs, attn_rows, ship):
        rows, width = block.shape
        kinds, _, wide, _ = heads.shape
        self.head_width = wide
        here = 2 * wide
        self.arrays = (block, docs, scale, heads, q, k, v, z, o, logs, attn_rows)
        self.spaces = (pltpu.VMEM,) * 10 + (pltpu.HBM,)
        self.outs = (
            jax.ShapeDtypeStruct((rows, width), f32),
            jax.ShapeDtypeStruct((kinds, wide, width // 2) if ship else heads.shape, bf16),
            jax.ShapeDtypeStruct((3, here), f32),
        )
        self.ship = ship
        self.out_spaces = (pltpu.VMEM,) * 3
        self.scratch = (
            pltpu.VMEM((8 * rows, width), bf16),
            pltpu.VMEM((8 * rows, width), bf16),
            pltpu.VMEM((here, 8 * rows), bf16),
            pltpu.VMEM((8 * rows, here), f32),
            pltpu.VMEM((8 * rows, here), f32),
            pltpu.VMEM((here, 2 * BLOCK), f32),
            pltpu.VMEM((8 * rows, 3 * here), bf16),
            pltpu.VMEM((here, width), f32),
            pltpu.VMEM((3, 8, here), f32),
            dma_sems(1),
            *([pltpu.VMEM(heads.shape, bf16)] if ship else []),
        )
        parts = dict(gather=PlaneGather(block), scatter=PlaneScatter(rows, width, 0))
        if ship:
            parts["heads"] = HeadScatter(heads)
        self.use(**parts)

    def load(self, ins, scratch):
        return pltpu.make_async_copy(ins[10], scratch[1], scratch[9].at[0])

    def start(self, here, ins, outs, scratch):
        self.parts["gather"].start(here, ins[:1], scratch[:1], self.held(scratch, "gather"))
        self.load(ins, scratch).start()

    def finish(self, here, ins, outs, scratch):
        block_ref, doc_ref, scale_ref, heads_ref, q_ref, k_ref, v_ref, z_ref, o_ref, l_ref = ins[:10]
        out_ref, quarter_ref, small_ref = outs
        (
            rows_buf,
            attn_rows,
            k_cols,
            acc_k,
            acc_v,
            acc_q,
            proj,
            out_sum,
            small,
        ) = scratch[:9]
        heads_grad = scratch[10] if self.ship else quarter_ref
        rows, model_width = block_ref.shape
        wide = self.head_width
        width = 2 * wide
        acc_k[...] = jnp.zeros_like(acc_k)
        acc_v[...] = jnp.zeros_like(acc_v)
        out_sum[...] = jnp.zeros_like(out_sum)
        small[...] = jnp.zeros_like(small)
        k_cols[...] = turned(k_ref[...])

        def work(first):
            block = pl.ds(first, rows)
            scaled_grad = lax.dot_general(
                rows_buf[block, :],
                heads_ref[3].reshape(width, model_width),
                (((1,), (1,)), ((), ())),
                preferred_element_type=f32,
            )
            out_sum[...] += lax.dot_general(
                z_ref[block, :],
                rows_buf[block, :],
                (((0,), (0,)), ((), ())),
                preferred_element_type=f32,
            )
            small[0] += fold(o_ref[block, :] * scaled_grad)
            grad = attend_block_back(
                wide,
                first,
                (scaled_grad * scale_ref[...]).astype(bf16),
                q_ref,
                k_ref,
                k_cols,
                v_ref,
                o_ref,
                l_ref,
                doc_ref,
                acc_k,
                acc_v,
                acc_q,
            )
            proj[block, 0:width] = grad
            small[1] += fold(grad.astype(f32))

        self.parts["gather"].finish(
            here, ins[:1], scratch[:1], self.held(scratch, "gather"), work
        )

        def settle(first):
            block = pl.ds(first, rows)
            proj[block, width : 2 * width] = acc_k[block, :].astype(bf16)
            value_grad = acc_v[block, :].astype(bf16)
            proj[block, 2 * width : 3 * width] = value_grad
            small[2] += fold(value_grad.astype(f32))

        in_chunks(8 * rows, rows, settle)
        self.between()

        def early():
            self.load(ins, scratch).wait()
            qkv_grad = lax.dot_general(
                proj[...],
                attn_rows[...],
                (((0,), (0,)), ((), ())),
                preferred_element_type=f32,
            )
            heads_grad[0:3] = qkv_grad.astype(bf16).reshape(3, 2, wide, model_width)
            heads_grad[3] = out_sum[...].astype(bf16).reshape(2, wide, model_width)
            if self.ship:
                self.parts["heads"].start(here, (heads_grad,), None, self.held(scratch, "heads"))

        self.parts["scatter"].finish(
            here,
            None,
            (out_ref,),
            self.held(scratch, "scatter"),
            lambda first: proj[pl.ds(first, rows), :],
            lambda: heads_ref[0:3].reshape(3 * width, model_width),
            early=early,
        )
        if self.ship:
            held = self.held(scratch, "heads")
            self.parts["heads"].finish(here, (heads_grad,), (quarter_ref,), held)
        for i in range(3):
            small_ref[i : i + 1, :] = jnp.sum(small[i], axis=0, keepdims=True)


def format_kernel(f0, f1, s0, s1, h0, h1, first_ref, second_ref, qkv_ref, out_ref):
    part = first_ref.shape[2] // 4
    half = h0.shape[3]
    for layer, (first, second, heads) in enumerate(((f0, s0, h0), (f1, s1, h1))):
        for i in range(4):
            first_ref[layer, :, i * part : (i + 1) * part] = first[i].astype(f32)
            second_ref[layer, i * part : (i + 1) * part, :] = second[i].astype(f32)
        for core in range(2):
            here = pl.ds(core * half, half)
            for kind in range(3):
                pair = jnp.concatenate([heads[core, kind], heads[2 + core, kind]], axis=0)
                qkv_ref[layer, kind, here, :] = jnp.transpose(pair.astype(f32))
            for y in range(2):
                wide = heads.shape[2]
                out_ref[layer, y * wide : (y + 1) * wide, here] = heads[2 * y + core, 3].astype(f32)


def format_weights(first, second, heads):
    _, width, part = first[0].shape
    wide = heads[0].shape[2]
    return pl.pallas_call(
        format_kernel,
        out_shape=(
            jax.ShapeDtypeStruct((2, width, 4 * part), f32),
            jax.ShapeDtypeStruct((2, 4 * part, width), f32),
            jax.ShapeDtypeStruct((2, 3, width, 2 * wide), f32),
            jax.ShapeDtypeStruct((2, 2 * wide, width), f32),
        ),
        in_specs=[pl.BlockSpec(memory_space=pltpu.VMEM)] * 6,
        out_specs=[pl.BlockSpec(memory_space=pltpu.VMEM)] * 4,
        compiler_params=vmem_params(None, 40),
    )(*first, *second, *heads)


def plane_device(
    tokens,
    segment_ids,
    cotangent,
    ln_attn_gain,
    ln_attn_bias,
    qkv_weight,
    qv_bias,
    head_scale,
    out_weight,
    out_bias,
    ln_post_gain,
    ln_post_bias,
    ln_ffn_gain,
    ln_ffn_bias,
    fc1_weight,
    fc1_bias,
    mid_gain,
    mid_bias,
    fc2_weight,
    fc2_bias,
):
    layers = qkv_weight.shape[0]
    model_width = tokens.shape[1]
    heads_all = head_scale.shape[1]
    head_width = model_width // heads_all
    hidden_here = fc1_weight.shape[2]
    hidden_all = hidden_here * 8
    quarter = hidden_here // 4
    half_width = model_width // 2
    x, y, core = lax.axis_index("x"), lax.axis_index("y"), lax.axis_index("core")
    quarter_at = 2 * y + core
    width = 2 * head_width
    ids = iter(range(1, 64))

    doc_row = segment_ids.astype(f32)[None, :]
    ((residual,), (docs,)) = run_tasks(ids, PlaneMove(tokens), PlaneMove(doc_row))
    residual = residual.astype(f32)

    def cut(values, at, size, axis):
        return lax.dynamic_slice_in_dim(values, at * size, size, axis)

    qkv_rows = jnp.transpose(qkv_weight, (0, 2, 3, 1))
    bias_heads = cut(qv_bias, y, head_width, 2)
    small = jnp.concatenate(
        [
            jnp.concatenate([bias_heads, bias_heads], axis=2).reshape(layers, 2 * width),
            cut(fc1_bias, quarter_at, quarter, 1),
            cut(mid_gain, quarter_at, quarter, 1),
            cut(mid_bias, quarter_at, quarter, 1),
        ],
        axis=1,
    )
    head_ids = ((2 * core + jnp.arange(2)) * 2 + x) * 2 + y
    head_onehot = (head_ids[:, None] == jnp.arange(heads_all)[None, :]).astype(f32)
    heads_here = [None] * layers

    stored = []
    for layer in range(layers):
        attn_in, attn_normal, attn_factor = norm_local(
            residual, ln_attn_gain[layer], ln_attn_bias[layer]
        )
        scale = jnp.sum(head_onehot * head_scale[layer][None, :], axis=1)
        scale_row = jnp.repeat(scale, head_width)[None, :]
        late = layer == 0
        sides = [WeightGather(fc1_weight, layer, 1, late)]
        if not late:
            sides.append(WeightGather(fc2_weight, layer, 0))
        ((branch, attn_rows, q, k, v, scaled, attended, logs, *got), (first_here,), *rest) = (
            run_tasks(
                ids,
                AttnForward(
                    attn_in.astype(bf16),
                    docs,
                    scale_row,
                    (qkv_rows, out_weight) if late else (heads_here[layer],),
                    small,
                    head_width,
                    layer,
                    late,
                ),
                *sides,
                mib=40,
            )
        )
        if late:
            heads_here[0], small = got

            def hidden_rows(at):
                part = small[:, :, 2 * width + at * quarter : 2 * width + (at + 1) * quarter]
                return jnp.transpose(part, (1, 0, 2)).reshape(layers, 4 * quarter)

            shift_hidden, gain_hidden, bias_hidden = map(hidden_rows, range(3))
        branch = branch + out_bias[layer]
        post_out, post_normal, post_factor = norm_local(
            branch, ln_post_gain[layer], ln_post_bias[layer]
        )
        middle = residual + post_out
        ffn_in, ffn_normal, ffn_factor = norm_local(middle, ln_ffn_gain[layer], ln_ffn_bias[layer])
        sides = []
        if layer + 1 < layers:
            sides.append(HeadGather(qkv_rows, out_weight, layer + 1, late))
        else:
            sides.append(PlaneMove(cotangent))
        ((ffn_out, ffn_rows, slope, hidden_normal, mixed, totals, *got), (side,)) = run_tasks(
            ids,
            FfnForward(
                ffn_in.astype(bf16),
                first_here,
                fc2_weight if late else rest[0][0],
                shift_hidden[layer][None],
                gain_hidden[layer][None],
                bias_hidden[layer][None],
                layer,
                late,
            ),
            *sides,
            mib=48,
        )
        second_here = got[0] if late else rest[0][0]
        if layer + 1 < layers:
            heads_here[layer + 1] = side
        stored.append(
            (
                first_here,
                second_here,
                attn_normal,
                attn_factor,
                attn_rows,
                q,
                k,
                v,
                attended,
                logs,
                scale_row,
                scaled,
                post_normal,
                post_factor,
                ffn_normal,
                ffn_factor,
                ffn_rows,
                slope,
                hidden_normal,
                mixed,
                totals,
            )
        )
        residual = middle + ffn_out + fc2_bias[layer]
    gradient_b = side
    gradient = gradient_b.astype(f32)

    first_done, second_done = [None] * layers, [None] * layers
    heads_done, hidden_done = [None] * layers, [None] * layers
    early_vectors, late_vectors = [None] * layers, [None] * layers
    pending = None
    for layer in reversed(range(layers)):
        (
            first_here,
            second_here,
            attn_normal,
            attn_factor,
            attn_rows,
            q,
            k,
            v,
            attended,
            logs,
            scale_row,
            scaled,
            post_normal,
            post_factor,
            ffn_normal,
            ffn_factor,
            ffn_rows,
            slope,
            hidden_normal,
            mixed,
            totals,
        ) = stored[layer]
        second_shift_grad = jnp.sum(gradient, axis=0)
        if pending is None:
            sides = [PlaneMove(residual.astype(bf16), back=True)]
        else:
            sides = [HeadScatter(pending[0]), LineThenRows(pending[1])]
        ((ffn_in_grad, first_grad, second_grad, hidden_grad), *got) = run_tasks(
            ids,
            FfnBackward(
                gradient_b,
                first_here,
                second_here,
                gain_hidden[layer][None],
                slope,
                hidden_normal,
                mixed,
                ffn_rows,
                totals,
            ),
            *sides,
            mib=60,
        )
        if pending is None:
            layer_output = got[0][0]
        else:
            heads_grad, hidden_done[layer + 1] = got[0][0], got[1][0]
        ffn_gain_grad = jnp.sum(ffn_in_grad * ffn_normal, axis=0)
        ffn_bias_grad = jnp.sum(ffn_in_grad, axis=0)
        middle_grad = gradient + norm_back(ffn_in_grad, ffn_normal, ffn_factor, ln_ffn_gain[layer])
        post_gain_grad = jnp.sum(middle_grad * post_normal, axis=0)
        post_bias_grad = jnp.sum(middle_grad, axis=0)
        branch_grad = norm_back(middle_grad, post_normal, post_factor, ln_post_gain[layer])
        out_shift_grad = jnp.sum(branch_grad, axis=0)
        early_vectors[layer] = jnp.stack(
            [
                out_shift_grad,
                post_gain_grad,
                post_bias_grad,
                ffn_gain_grad,
                ffn_bias_grad,
                second_shift_grad,
            ]
        )
        sides = [LineThenRows(first_grad), RowsGather(second_grad)]
        if layer == 0:
            sides.append(RowsGather(heads_grad))
            known = early_vectors + late_vectors[1:]
            count = sum(each.shape[0] for each in known)
            known.append(jnp.zeros((-count % 8, model_width), f32))
            sides.append(PlaneSum(jnp.concatenate(known, axis=0)))
        ((attn_in_grad, heads_grad, small_grad), (first_done[layer],), (second_done[layer],), *rest) = (
            run_tasks(
                ids,
                AttnBackward(
                    branch_grad.astype(bf16),
                    docs,
                    scale_row,
                    heads_here[layer],
                    q,
                    k,
                    v,
                    scaled,
                    attended,
                    logs,
                    attn_rows,
                    layer == 0,
                ),
                *sides,
                mib=48,
            )
        )
        scale_grad = jnp.sum(
            head_onehot * jnp.sum(small_grad[0].reshape(2, head_width), axis=1)[:, None], axis=0
        )
        bias_grad = jnp.transpose(small_grad[1:].reshape(2, 2, head_width), (1, 0, 2))
        hidden_grad = jnp.roll(hidden_grad, 1, axis=0).reshape(3, 4, quarter)
        hidden_grad = jnp.concatenate(
            [
                jnp.transpose(hidden_grad, (1, 0, 2)).reshape(4, -1),
                lax.dynamic_update_slice(
                    jnp.zeros((4, width), f32), bias_grad.reshape(2, width), (2 * core, 0)
                ),
            ],
            axis=1,
        ).reshape(4, -1, 128)
        pending = (heads_grad, hidden_grad)
        late_vectors[layer] = jnp.stack(
            [
                jnp.sum(attn_in_grad * attn_normal, axis=0),
                jnp.sum(attn_in_grad, axis=0),
                jnp.pad(scale_grad, (0, model_width - heads_all)),
            ]
        )
        gradient = middle_grad + norm_back(
            attn_in_grad, attn_normal, attn_factor, ln_attn_gain[layer]
        )
        gradient_b = gradient.astype(bf16)
    (heads_done[1],), (summed,) = rest
    ((vectors,), (heads_done[0],), (hidden_done[0],), (input_grad,)) = run_tasks(
        ids,
        PlaneThenLineSum(late_vectors[0], summed),
        RowsGather(pending[0]),
        LineThenRows(pending[1]),
        PlaneMove(gradient_b, back=True),
    )
    input_grad = input_grad.astype(f32)
    early = vectors[: 6 * layers].reshape(layers, 6, model_width)
    late = jnp.stack([vectors[-3:], vectors[6 * layers : 6 * layers + 3]])
    first_grad, second_grad, qkv_grad, out_grad = format_weights(
        first_done,
        second_done,
        heads_done,
    )
    hidden = jnp.stack(hidden_done).reshape(layers, 4, -1)
    bias_grad = jnp.sum(hidden[:, :, 3 * quarter :].reshape(layers, 2, 2, 2, head_width), axis=2)
    bias_grad = jnp.transpose(bias_grad, (0, 2, 1, 3)).reshape(layers, 2, width)
    hidden = hidden[:, :, : 3 * quarter].reshape(layers, 4, 3, quarter)
    hidden = jnp.transpose(hidden, (0, 2, 1, 3)).reshape(layers, 3, hidden_here)
    return (
        layer_output,
        input_grad,
        late[:, 0],
        late[:, 1],
        jnp.transpose(qkv_grad, (0, 2, 1, 3)),
        bias_grad,
        late[:, 2, :heads_all],
        out_grad,
        early[:, 0],
        early[:, 1],
        early[:, 2],
        early[:, 3],
        early[:, 4],
        first_grad,
        hidden[:, 0],
        hidden[:, 1],
        hidden[:, 2],
        second_grad,
        early[:, 5],
    )


def split_specs(rows, mp):
    both = tuple(rows) + tuple(mp)
    in_specs = (
        P(both, None),
        P(rows),
        P(both, None),
        P(),
        P(),
        P(None, None, None, mp),
        P(None, None, mp),
        P(),
        P(None, mp, None),
        P(),
        P(),
        P(),
        P(),
        P(),
        P(None, None, mp),
        P(None, mp),
        P(None, mp),
        P(None, mp),
        P(None, mp, None),
        P(),
    )
    out_specs = (
        P(both, None),
        P(both, None),
        P(),
        P(),
        P(None, None, None, mp),
        P(None, None, mp),
        P(),
        P(None, mp, None),
        P(),
        P(),
        P(),
        P(),
        P(),
        P(None, None, mp),
        P(None, mp),
        P(None, mp),
        P(None, mp),
        P(None, mp, None),
        P(),
    )
    return in_specs, out_specs


def solution(mesh):
    if mesh.shape["rows"] == 4 and mesh.shape["mp"] == 8:
        planes = Mesh(mesh.devices.reshape(2, 2, 4, 2), ("y", "core", "z", "x"))
        in_specs, out_specs = split_specs(("y", "core"), ("z", "x"))
        return jax.shard_map(
            plane_device, mesh=planes, in_specs=in_specs, out_specs=out_specs, check_vma=False
        )
    in_specs, out_specs = split_specs(("rows",), ("mp",))
    return jax.shard_map(
        per_device, mesh=mesh, in_specs=in_specs, out_specs=out_specs, check_vma=False
    )
```

profile of v0, /device:TPU:1, one launch (start us, length us, event | category | flops | bytes accessed | tf_op | source)
XLA Modules:
  0.0 617.7 jit_solution(15702185289831933940)
XLA Ops:
  4.0 26.3 %shard_map.339 = (bf16[256,1024]{1,0:T(8,128)(2,1)S(1)}, f32[1,2048]{1,0:T(1,128)S(1)}) custom-call(bf16[256,1024]{1,0:T(8,128)(2,1)S(1)} %copy-done.43, f32[1,2048]{1,0:T(1,128)S(1)} %bitcast.116), custom_call_target="tpu_custom_call" | custom-call | tf_op jit(solution)/shard_map/pallas_call | solution.py:619
  34.5 2.6 copy.68
  37.1 1.4 copy-done.2
  38.5 1.6 copy-done.4
  41.2 60.9 %shard_map.340 = (f32[256,1024]{1,0:T(8,128)S(1)}, bf16[2048,1024]{1,0:T(8,128)(2,1)}, bf16[2048,128]{1,0:T(8,128)(2,1)S(1)}, bf16[2048,128]{1,0:T(8,128)(2,1)S(...) custom-call(bf16[256,1024]{1,0:T(8,128)(2,1)S(1)} %copy-done.14, ...), custom_call_target="tpu_custom_call" | custom-call | tf_op jit(solution)/shard_map/pallas_call | solution.py:619
  104.0 53.1 %shard_map.341 = (f32[256,1024]{1,0:T(8,128)S(1)}, bf16[2048,1024]{1,0:T(8,128)(2,1)}, f32[2048,512]{1,0:T(8,128)}, f32[2048,512]{1,0:T(8,128)}, bf16[2048,512]{...) custom-call(bf16[256,1024]{1,0:T(8,128)(2,1)S(1)} %add_convert_fusion., ...), custom_call_target="tpu_custom_call" | custom-call | tf_op jit(solution)/shard_map/pallas_call | solution.py:619
  159.5 1.6 copy-done.3
  161.1 1.6 copy-done.5
  163.9 49.1 %shard_map.342 = (f32[256,1024]{1,0:T(8,128)S(1)}, bf16[2048,1024]{1,0:T(8,128)(2,1)}, bf16[2048,128]{1,0:T(8,128)(2,1)S(1)}, bf16[2048,128]{1,0:T(8,128)(2,1)S(...) custom-call(bf16[256,1024]{1,0:T(8,128)(2,1)S(1)} %add_convert_fusio, ...), custom_call_target="tpu_custom_call" | custom-call | tf_op jit(solution)/shard_map/pallas_call | solution.py:619
  214.8 57.1 %shard_map.343 = (f32[256,1024]{1,0:T(8,128)S(1)}, bf16[2048,1024]{1,0:T(8,128)(2,1)}, f32[2048,512]{1,0:T(8,128)}, f32[2048,512]{1,0:T(8,128)}, bf16[2048,512]{...) custom-call(bf16[256,1024]{1,0:T(8,128)(2,1)S(1)} %add_convert_fusion.1.refs_0_, ...), custom_call_target="tpu_custom_call" | custom-call | tf_op jit(solution)/shard_map/pallas_call | solution.py:619
  273.8 58.0 %shard_map.344 = (f32[256,1024]{1,0:T(8,128)}, bf16[4,1024,128]{2,1,0:T(8,128)(2,1)}, bf16[128,1024]{1,0:T(8,128)(2,1)}, f32[3,512]{1,0:T(4,128)}, bf16[256,1024]{1,0:T(8,128)(2,1)}) custom-call(bf16[256,1024]{1,0:T(8,128)(2,1)} %copy-done.12, bf16[1024,512]{1,0:T(8,128)(2,1)} %copy-done.9, bf16[512,1024]{1,0:T(8,128)(2,1)} %copy-done.10, ...), custom_call_target="tpu_custom_call" | custom-call | tf_op jit(solution)/shard_map/pallas_call | solution.py:619
  333.2 2.0 multiply_reduce_fusion.1
  335.3 2.8 multiply_reduce_fusion.2
  339.1 60.7 %shard_map.345 = (f32[256,1024]{1,0:T(8,128)S(1)}, bf16[4,2,64,1024]{3,2,1,0:T(8,128)(2,1)S(1)}, f32[3,128]{1,0:T(4,128)S(1)}, bf16[4,1024,128]{2,1,0:T(8,128)(2,1)S(1)}, bf16[4,128,1024]{2,1,0:T(8,128)(2,1)}) custom-call(bf16[256,1024]{1,0:T(8,128)(2,1)S(1)} %get-tuple-element.184.refs_0_, f32[1,2048]{1,0:T(1,128)S(1)} %get-tuple-element.89.refs_1_, ...), custom_call_target="tpu_custom_call" | custom-call | tf_op jit(solution)/shard_map/pallas_call | solution.py:619
  402.6 1.7 multiply_reduce_fusion
  404.4 1.9 fusion.16
  407.4 60.4 %shard_map.346 = (f32[256,1024]{1,0:T(8,128)}, bf16[4,1024,128]{2,1,0:T(8,128)(2,1)}, bf16[128,1024]{1,0:T(8,128)(2,1)}, f32[3,512]{1,0:T(4,128)}, bf16[4,64,512]{2,1,0:T(8,128)(2,1)}, /*index=5*/f32[4,4,128]{2,1,0:T(4,128)}) custom-call(bf16[256,1024]{1,0:T(8,128)(2,1)} %convert_element_type.52.refs_0_, bf16[1024,512]{1,0:T(8,128)(2,1)} %copy-done.6, ...), custom_call_target="tpu_custom_call" | custom-call | tf_op jit(solution)/shard_map/pallas_call | solution.py:619
  467.9 1.7 multiply_reduce_fusion.3
  469.6 3.0 multiply_reduce_fusion.4
  477.1 77.1 %shard_map.347 = (f32[256,1024]{1,0:T(8,128)S(1)}, bf16[4,64,512]{2,1,0:T(8,128)(2,1)S(1)}, f32[3,128]{1,0:T(4,128)S(1)}, bf16[4,1024,128]{2,1,0:T(8,128)(2,1)S(...) custom-call(bf16[256,1024]{1,0:T(8,128)(2,1)S(1)} %get-tuple-element.188.refs_0_, ...), custom_call_target="tpu_custom_call" | custom-call | tf_op jit(solution)/shard_map/pallas_call | solution.py:619
  556.9 40.5 %shard_map.348 = (f32[19,1024]{1,0:T(8,128)S(1)}, bf16[4,4,64,512]{3,2,1,0:T(8,128)(2,1)S(1)}, f32[4,4,128]{2,1,0:T(4,128)S(1)}, bf16[256,1024]{1,0:T(8,128)(2,1)S(1)}) custom-call(f32[3,1024]{1,0:T(4,128)S(1)} %pad_maximum_fusion.refs_0_, f32[16,1024]{1,0:T(8,128)S(1)} %get-tuple-element.140.refs_1_, bf16[4,64,512]{2,1,0:T(8,128)(2,1)S(1)} %copy-done.49, ...), custom_call_target="tpu_custom_call" | custom-call | tf_op jit(solution)/shard_map/pallas_call | solution.py:619
  599.5 1.2 copy-done.22
  604.4 5.3 shard_map.349
  615.7 1.9 copy.109
  (274 shorter events, 42.3 us)
Async XLA Ops:
  0.7 36.4 %copy-start.11 = (bf16[2,128,1024]{2,1,0:T(8,128)(2,1)S(1)}, bf16[2,128,1024]{2,1,0:T(8,128)(2,1)}, u32[]{:S(2)}) copy-start(bf16[2,128,1024]{2,1,0:T(8,128)(2,1)} %refs_7_.1) | copy-start | bytes 1572868
  33.4 68.7 %copy-start.63 = (f32[2,1024]{1,0:T(2,128)S(1)}, f32[2,1024]{1,0:T(2,128)}, u32[]{:S(2)}) copy-start(f32[2,1024]{1,0:T(2,128)} %param.29) | copy-start | bytes 24580
  41.2 61.4 %copy-start.64 = (f32[2,1024]{1,0:T(2,128)S(1)}, f32[2,1024]{1,0:T(2,128)}, u32[]{:S(2)}) copy-start(f32[2,1024]{1,0:T(2,128)} %param.30) | copy-start | bytes 24580
  41.2 61.4 %copy-start.65 = (f32[2,1024]{1,0:T(2,128)S(1)}, f32[2,1024]{1,0:T(2,128)}, u32[]{:S(2)}) copy-start(f32[2,1024]{1,0:T(2,128)} %param.31) | copy-start | bytes 24580
  41.2 62.2 %copy-start.66 = (f32[2,1024]{1,0:T(2,128)S(1)}, f32[2,1024]{1,0:T(2,128)}, u32[]{:S(2)}) copy-start(f32[2,1024]{1,0:T(2,128)} %param.32) | copy-start | bytes 24580
  41.2 62.2 %copy-start.67 = (f32[2,1024]{1,0:T(2,128)S(1)}, f32[2,1024]{1,0:T(2,128)}, u32[]{:S(2)}) copy-start(f32[2,1024]{1,0:T(2,128)} %param.33) | copy-start | bytes 24580
  102.1 55.0 %copy-start.6 = (bf16[1024,512]{1,0:T(8,128)(2,1)}, bf16[1024,512]{1,0:T(8,128)(2,1)S(1)}, u32[]{:S(2)}) copy-start(bf16[1024,512]{1,0:T(8,128)(2,1)S(1)} %get-tuple-element.91.refs_1_) | copy-start | bytes 3145732
  103.1 56.3 %copy-start.54 = (f32[256,1024]{1,0:T(8,128)}, f32[256,1024]{1,0:T(8,128)S(1)}, u32[]{:S(2)}) copy-start(f32[256,1024]{1,0:T(8,128)S(1)} %get-tuple-element.196) | copy-start | bytes 3145732
  103.1 55.1 %copy-start.68 = (f32[2,1024]{1,0:T(2,128)S(1)}, f32[2,1024]{1,0:T(2,128)}, u32[]{:S(2)}) copy-start(f32[2,1024]{1,0:T(2,128)} %param.39) | copy-start | bytes 24580
  103.7 54.6 %copy-start.50 = (f32[1,512]{1,0:T(1,128)}, f32[1,512]{1,0:T(1,128)S(1)}, u32[]{:S(2)}) copy-start(f32[1,512]{1,0:T(1,128)S(1)} %get-tuple-element.233.refs_4_.refs_3_) | copy-start | bytes 6148
  103.7 111.1 %copy-start.51 = (f32[1,512]{1,0:T(1,128)}, f32[1,512]{1,0:T(1,128)S(1)}, u32[]{:S(2)}) copy-start(f32[1,512]{1,0:T(1,128)S(1)} %get-tuple-element.232.refs_4_.refs_3_) | copy-start | bytes 6148
  163.9 49.7 %copy-start.57 = (f32[256,1024]{1,0:T(8,128)S(1)}, f32[256,1024]{1,0:T(8,128)}, u32[]{:S(2)}) copy-start(f32[256,1024]{1,0:T(8,128)} %copy-done.56) | copy-start | bytes 3145732
  213.1 58.8 %copy-start.9 = (bf16[1024,512]{1,0:T(8,128)(2,1)}, bf16[1024,512]{1,0:T(8,128)(2,1)S(1)}, u32[]{:S(2)}) copy-start(bf16[1024,512]{1,0:T(8,128)(2,1)S(1)} %get-tuple-element.96.refs_1_) | copy-start | bytes 3145732
  213.1 58.8 %copy-start.10 = (bf16[512,1024]{1,0:T(8,128)(2,1)}, bf16[512,1024]{1,0:T(8,128)(2,1)S(1)}, u32[]{:S(2)}) copy-start(bf16[512,1024]{1,0:T(8,128)(2,1)S(1)} %get-tuple-element.97.refs_2_) | copy-start | bytes 3145732
  214.0 59.8 %copy-start.58 = (f32[256,1024]{1,0:T(8,128)}, f32[256,1024]{1,0:T(8,128)S(1)}, u32[]{:S(2)}) copy-start(f32[256,1024]{1,0:T(8,128)S(1)} %get-tuple-element.192) | copy-start | bytes 3145732
  273.8 61.5 %copy-start.13 = (bf16[256,1024]{1,0:T(8,128)(2,1)S(1)}, bf16[256,1024]{1,0:T(8,128)(2,1)}, u32[]{:S(2)}) copy-start(bf16[256,1024]{1,0:T(8,128)(2,1)} %copy-done.12) | copy-start | bytes 1572868
  407.4 60.4 %copy-start.55 = (f32[256,1024]{1,0:T(8,128)S(1)}, f32[256,1024]{1,0:T(8,128)}, u32[]{:S(2)}) copy-start(f32[256,1024]{1,0:T(8,128)} %copy-done.54) | copy-start | bytes 3145732
  469.6 4.4 copy-start.28
  469.6 4.4 copy-start.30
  469.6 4.4 copy-start.45
  477.1 77.8 %copy-start.60 = (f32[256,1024]{1,0:T(8,128)S(1)}, f32[256,1024]{1,0:T(8,128)}, u32[]{:S(2)}) copy-start(f32[256,1024]{1,0:T(8,128)} %copy-done.59) | copy-start | bytes 3145732
  554.3 43.2 %copy-start.69 = (f32[4,4,128]{2,1,0:T(4,128)S(1)}, f32[4,4,128]{2,1,0:T(4,128)}, u32[]{:S(2)}) copy-start(f32[4,4,128]{2,1,0:T(4,128)} %get-tuple-element.153) | copy-start | bytes 24580
  554.3 45.2 %copy-start.21 = (bf16[4,1024,128]{2,1,0:T(8,128)(2,1)S(1)}, bf16[4,1024,128]{2,1,0:T(8,128)(2,1)}, u32[]{:S(2)}) copy-start(bf16[4,1024,128]{2,1,0:T(8,128)(2,1)} %copy-done.20) | copy-start | bytes 3145732
  599.5 18.0 %copy-start.1 = (f32[2,512]{1,0:T(2,128)S(1)}, f32[2,512]{1,0:T(2,128)}, u32[]{:S(2)}) copy-start(f32[2,512]{1,0:T(2,128)} %param.35) | copy-start | bytes 12292
  (47 other events, 72.1 us)
where the time goes:
time: 629 us; the launch traced here: 618 us
  Pallas kernels  548 us (87%)
  local copies, waits for them, and re-layouts  42.3 us (7%)
  other arithmetic  25.1 us (4%)
    pallas_call x10, Pallas kernels, run_tasks(): pl.pallas_call(kernel, out_shape=[out for task in tasks for out in task.o...  543 us
    unnamed x154, local copies, waits for them, and re-layouts  33.8 us

commit v1 on v0

--- a/solution.py
+++ b/solution.py
@@ -574,13 +574,13 @@
     scratch = ()
     reach = ()
 
-    def between(self):
+    def moment(self, name):
         pass
 
     def start(self, here, ins, outs, scratch):
         pass
 
-    def middle(self, here, ins, outs, scratch):
+    def at_moment(self, name, here, ins, outs, scratch):
         pass
 
     def finish(self, here, ins, outs, scratch):
@@ -608,11 +608,11 @@
         for task, *held in zip(tasks, *views):
             task.start(here, *held)
 
-        def between():
+        def moment(name):
             for task, *held in zip(tasks, *views):
-                task.middle(here, *held)
-
-        tasks[0].between = between
+                task.at_moment(name, here, *held)
+
+        tasks[0].moment = moment
         for task, *held in zip(tasks, *views):
             task.finish(here, *held)
 
@@ -633,15 +633,15 @@
 
 
 class PlaneMove(Task):
-    def __init__(self, values, back=False):
-        self.back = back
+    def __init__(self, values, back=False, when="midway"):
+        self.back, self.when = back, when
         self.arrays, self.spaces = (values,), (pltpu.HBM,)
         self.outs = (jax.ShapeDtypeStruct(values.shape, values.dtype),)
         self.out_spaces = (pltpu.HBM,)
         self.scratch = (
-            pltpu.VMEM((2, *values.shape), values.dtype),
+            pltpu.VMEM(values.shape, values.dtype),
             dma_sems(3),
-            dma_sems(3),
+            dma_sems(2),
         )
         self.reach = (BY_Y,) + BY_LINE
 
@@ -660,65 +660,55 @@
         held, send, recv = scratch
         targets, at_home, origin, origin_home = self.ends(here)
         bend = self.bend(here)
+        away_from = jnp.logical_not
         to_y = here.peer(*BY_Y)
-        legs = {}
+        first, second = [], []
         if not self.back:
-            legs["own"] = (bend, pltpu.make_async_copy(ins[0], held.at[here.y], recv.at[1]))
-            legs["over"] = (
-                jnp.logical_not(bend),
-                remote(ins[0], held.at[here.y], send.at[2], recv.at[0], to_y),
-            )
+            over = remote(ins[0], held, send.at[2], recv.at[0], to_y)
+            first.append((away_from(bend), over, True))
             for y in range(2):
-                away = remote(held.at[y], outs[0], send.at[y], recv.at[2], targets[y])
-                stay = pltpu.make_async_copy(held.at[y], outs[0], recv.at[2])
-                legs["away", y] = (bend & jnp.logical_not(at_home[y]), away)
-                legs["stay", y] = (bend & at_home[y], stay)
+                for legs, source, when in (
+                    (first, ins[0], bend & (here.y == y)),
+                    (second, held, bend & (here.y != y)),
+                ):
+                    away = remote(source, outs[0], send.at[y], recv.at[1], targets[y])
+                    stay = pltpu.make_async_copy(source, outs[0], recv.at[1])
+                    legs.append((when & away_from(at_home[y]), away, True))
+                    legs.append((when & at_home[y], stay, False))
         else:
-            group = here.z // 2
-            for y in range(2):
-                mine = group == y
-                away = remote(ins[0], held.at[y], send.at[2], recv.at[y], origin)
-                stay = pltpu.make_async_copy(ins[0], held.at[y], recv.at[y])
-                legs["away", y] = (mine & jnp.logical_not(origin_home), away)
-                legs["stay", y] = (mine & origin_home, stay)
-                own = pltpu.make_async_copy(held.at[y], outs[0], recv.at[2])
-                legs["own", y] = (bend & (here.y == y), own)
-                over = remote(held.at[y], outs[0], send.at[y], recv.at[2], to_y)
-                legs["over", y] = (bend & (here.y != y), over)
-        return legs
+            ends_there = here.z // 2 == here.y
+            for goes_on, target, slot in ((False, outs[0], 1), (True, held, 0)):
+                when = away_from(ends_there) if goes_on else ends_there
+                away = remote(ins[0], target, send.at[int(goes_on)], recv.at[slot], origin)
+                stay = pltpu.make_async_copy(ins[0], target, recv.at[slot])
+                first.append((when & away_from(origin_home), away, True))
+                first.append((when & origin_home, stay, False))
+            over = remote(held, outs[0], send.at[2], recv.at[1], to_y)
+            second.append((bend, over, True))
+        return first, second
 
     def start(self, here, ins, outs, scratch):
-        legs = self.plan(here, ins, outs, scratch)
-        firsts = ("away", "stay") if self.back else ("own", "over")
-        for key, (when, copy) in legs.items():
-            if key in firsts or key[0] in firsts:
+        for when, copy, _ in self.plan(here, ins, outs, scratch)[0]:
+            pl.when(when)(copy.start)
+
+    def at_moment(self, name, here, ins, outs, scratch):
+        if name == self.when:
+            held, _, recv = scratch
+
+            @pl.when(self.bend(here))
+            def _():
+                pltpu.make_async_copy(held, held, recv.at[0]).wait()
+
+            for when, copy, _ in self.plan(here, ins, outs, scratch)[1]:
                 pl.when(when)(copy.start)
-        self.moved = False
-
-    def middle(self, here, ins, outs, scratch):
-        legs = self.plan(here, ins, outs, scratch)
-        held, send, recv = scratch
-        bend = self.bend(here)
-
-        @pl.when(bend)
-        def _():
-            for slot in range(2):
-                pltpu.make_async_copy(held.at[0], held.at[0], recv.at[slot]).wait()
-
-        seconds = ("own", "over") if self.back else ("away", "stay")
-        for key, (when, copy) in legs.items():
-            if not isinstance(key, str) and key[0] in seconds:
-                pl.when(when)(copy.start)
-        self.moved = True
 
     def finish(self, here, ins, outs, scratch):
-        if not self.moved:
-            self.middle(here, ins, outs, scratch)
-        legs = self.plan(here, ins, outs, scratch)
-        pltpu.make_async_copy(outs[0], outs[0], scratch[2].at[2]).wait()
-        for key, (when, copy) in legs.items():
-            if key == "over" or key[0] in ("away", "over"):
-                pl.when(when)(copy.wait_send)
+        self.at_moment("end", here, ins, outs, scratch)
+        pltpu.make_async_copy(outs[0], outs[0], scratch[2].at[1]).wait()
+        for legs in self.plan(here, ins, outs, scratch):
+            for when, copy, is_remote in legs:
+                if is_remote:
+                    pl.when(when)(copy.wait_send)
 
 
 class PlaneGather(Task):
@@ -774,7 +764,7 @@
             copies[index].start()
         self.keep(here, ins[0], outs[0], scratch[2]).start()
 
-    def finish(self, here, ins, outs, scratch, work=None):
+    def finish(self, here, ins, outs, scratch, work=None, soon=None):
         rows = ins[0].shape[0]
         copies = self.copies(here, ins[0], outs[0], scratch[0], scratch[1])
 
@@ -803,6 +793,8 @@
         copies[6].wait_recv()
         copies[10].start()
         done(0, 1, 1)
+        if soon is not None:
+            soon()
         copies[9].wait_recv()
         copies[10].wait_recv()
         done(1, 1, 1)
@@ -979,9 +971,9 @@
 
 
 class HeadGather(Task):
-    def __init__(self, qkv, out, layer, midway=False):
+    def __init__(self, qkv, out, layer, when="start"):
         _, kinds, both, width = qkv.shape
-        self.layer, self.midway = layer, midway
+        self.layer, self.when = layer, when
         self.arrays, self.spaces = (qkv, out), (pltpu.HBM,) * 2
         self.outs = (jax.ShapeDtypeStruct((kinds + 1, 2, both // 2, width), qkv.dtype),)
         self.out_spaces = (pltpu.HBM,)
@@ -1021,11 +1013,10 @@
             pl.when(jnp.logical_not(at_home))(aways[4 * kind].start)
 
     def start(self, *held):
-        if not self.midway:
-            self.begin(*held)
-
-    def middle(self, *held):
-        if self.midway:
+        self.at_moment("start", *held)
+
+    def at_moment(self, name, *held):
+        if name == self.when:
             self.begin(*held)
 
     def finish(self, here, ins, outs, scratch):
@@ -1127,7 +1118,8 @@
 
 
 class RowsGather(Task):
-    def __init__(self, values):
+    def __init__(self, values, when="start"):
+        self.when = when
         self.arrays, self.spaces = (values,), (pltpu.HBM,)
         self.outs = (jax.ShapeDtypeStruct((4, *values.shape), values.dtype),)
         self.out_spaces = (pltpu.HBM,)
@@ -1146,7 +1138,14 @@
             remote(over, over, send_sem.at[2], recv_sem.at[2], to_core),
         )
 
-    def start(self, here, ins, outs, scratch):
+    def start(self, *held):
+        self.at_moment("start", *held)
+
+    def at_moment(self, name, *held):
+        if name == self.when:
+            self.begin(*held)
+
+    def begin(self, here, ins, outs, scratch):
         keep, by_y, by_core, again = self.copies(here, ins, outs, scratch)
         by_y.start()
         by_core.start()
@@ -1163,39 +1162,70 @@
         keep.wait()
 
 
-class PlaneThenLineSum(Task):
-    def __init__(self, values, ready):
-        rows, width = values.shape
-        both = (rows + ready.shape[0], width)
-        self.plane = PlaneSum(values)
-        self.arrays, self.spaces = (values, ready), (pltpu.VMEM,) * 2
-        self.outs, self.out_spaces = (jax.ShapeDtypeStruct(both, f32),), (pltpu.VMEM,)
+class StepSum(Task):
+    def __init__(self, values):
+        self.arrays, self.spaces = (values,), (pltpu.VMEM,)
+        self.outs = (jax.ShapeDtypeStruct(values.shape, f32),)
+        self.out_spaces = (pltpu.VMEM,)
         self.scratch = (
-            *self.plane.scratch,
-            pltpu.VMEM((4, *both), f32),
-            pltpu.VMEM(both, f32),
+            pltpu.VMEM((2, *values.shape), f32),
+            pltpu.VMEM((3, *values.shape), f32),
             dma_sems(3),
-            dma_sems(4),
-        )
-        self.reach = BY_PLANE + BY_Z
+            dma_sems(3),
+        )
+        self.reach = (BY_X, BY_Y, BY_CORE)
+
+    def leg(self, here, index, source, scratch):
+        _, got, send_sem, recv_sem = scratch
+        way = here.peer(*self.reach[index])
+        return remote(source, got.at[index], send_sem.at[index], recv_sem.at[index], way)
 
     def start(self, here, ins, outs, scratch):
-        self.plane.start(here, ins[:1], None, scratch[:3])
+        self.leg(here, 0, ins[0], scratch).start()
+
+    def at_moment(self, name, here, ins, outs, scratch):
+        part, got = scratch[:2]
+        if name == "midway":
+            self.leg(here, 0, ins[0], scratch).wait()
+            part[0] = ins[0][...] + got[0]
+            self.leg(here, 1, part.at[0], scratch).start()
+        if name == "closing":
+            self.leg(here, 1, part.at[0], scratch).wait()
+            part[1] = part[0] + got[1]
+            self.leg(here, 2, part.at[1], scratch).start()
 
     def finish(self, here, ins, outs, scratch):
-        got, mine, send_sem, recv_sem = scratch[3:]
-        rows = ins[0].shape[0]
-        first = ins[1].shape[0]
-        self.plane.finish(here, ins[:1], (mine.at[pl.ds(first, rows)],), scratch[:3])
-        mine[:first, :] = ins[1][...]
-        copies = [
-            remote(mine, got.at[here.z], send_sem.at[i], recv_sem.at[here.z], here.peer(*way))
+        part, got = scratch[:2]
+        self.leg(here, 2, part.at[1], scratch).wait()
+        outs[0][...] = part[1] + got[2]
+
+
+class LineSum(Task):
+    def __init__(self, values):
+        self.arrays, self.spaces = (values,), (pltpu.VMEM,)
+        self.outs = (jax.ShapeDtypeStruct(values.shape, f32),)
+        self.out_spaces = (pltpu.VMEM,)
+        self.scratch = (pltpu.VMEM((4, *values.shape), f32), dma_sems(3), dma_sems(4))
+        self.reach = BY_Z
+
+    def copies(self, here, ins, scratch):
+        got, send_sem, recv_sem = scratch
+        there, slot = got.at[here.z], recv_sem.at[here.z]
+        keep = pltpu.make_async_copy(ins[0], there, slot)
+        return keep, [
+            remote(ins[0], there, send_sem.at[i], slot, here.peer(*way))
             for i, way in enumerate(BY_Z)
         ]
+
+    def start(self, here, ins, outs, scratch):
+        keep, copies = self.copies(here, ins, scratch)
         for each in copies:
             each.start()
-        keep = pltpu.make_async_copy(mine, got.at[here.z], recv_sem.at[here.z])
         keep.start()
+
+    def finish(self, here, ins, outs, scratch):
+        got, _, recv_sem = scratch
+        _, copies = self.copies(here, ins, scratch)
         for plane in range(4):
             pltpu.make_async_copy(got.at[plane], got.at[plane], recv_sem.at[plane]).wait()
         outs[0][...] = (got[0] + got[1]) + (got[2] + got[3])
@@ -1245,7 +1275,35 @@
         return scratch[first:last]
 
 
-CHUNK = 32
+class PlaneThenLineSum(Parts):
+    def __init__(self, values):
+        self.arrays, self.spaces = (values,), (pltpu.VMEM,)
+        self.outs = (jax.ShapeDtypeStruct(values.shape, f32),)
+        self.out_spaces = (pltpu.VMEM,)
+        self.scratch = (pltpu.VMEM(values.shape, f32),)
+        self.use(plane=PlaneSum(values), line=LineSum(values))
+
+    def start(self, here, ins, outs, scratch):
+        self.parts["plane"].start(here, ins, None, self.held(scratch, "plane"))
+
+    def finish(self, here, ins, outs, scratch):
+        self.parts["plane"].finish(here, ins, scratch[:1], self.held(scratch, "plane"))
+        held = self.held(scratch, "line")
+        self.parts["line"].start(here, scratch[:1], None, held)
+        self.moment("midway")
+        self.parts["line"].finish(here, scratch[:1], outs, held)
+
+
+def norm_pull(grad_out, normal, factor, gain_row):
+    scaled = grad_out * gain_row
+    width = scaled.shape[1]
+    mean = jnp.sum(scaled, axis=1, keepdims=True) / width
+    inner = jnp.sum(scaled * normal, axis=1, keepdims=True) / width
+    return factor * (scaled - mean - normal * inner)
+
+
+NARROW = 128
+CHUNK = 256
 
 
 class FfnForward(Parts):
@@ -1336,7 +1394,7 @@
         if self.late:
             held = self.held(scratch, "second")
             self.parts["second"].finish(here, ins[2:3], outs[6:7], held)
-        self.between()
+        self.moment("midway")
 
         def rows_of(first):
             average = total_ref[0:1, pl.ds(first, rows)] / hidden_all
@@ -1359,6 +1417,7 @@
         def idle():
             keep_mixed.start()
             keep_normal.start()
+            self.moment("closing")
 
         self.parts["scatter"].finish(
             here,
@@ -1374,18 +1433,24 @@
 
 
 class FfnBackward(Parts):
-    def __init__(self, block, first, second, gain, slope, normal, mixed, ffn_rows, totals):
+    def __init__(
+        self, block, first, second, gain, slope, normal, mixed, ffn_rows, totals, gradient, norms
+    ):
         rows, width = block.shape
         hidden = second.shape[0]
         self.arrays = (block, first, second, gain, totals, slope, normal, mixed, ffn_rows)
         self.spaces = (pltpu.VMEM,) * 5 + (pltpu.HBM,) * 4
+        self.arrays += (gradient, *norms)
+        self.spaces += (pltpu.VMEM,) * 7
         self.outs = (
             jax.ShapeDtypeStruct((rows, width), f32),
             jax.ShapeDtypeStruct((4, width, hidden // 4), bf16),
             jax.ShapeDtypeStruct((hidden // 4, width), bf16),
             jax.ShapeDtypeStruct((3, hidden), f32),
-        )
-        self.out_spaces = (pltpu.VMEM,) * 4
+            jax.ShapeDtypeStruct((rows, width), bf16),
+            jax.ShapeDtypeStruct((8, width), f32),
+        )
+        self.out_spaces = (pltpu.VMEM,) * 6
         self.scratch = (
             pltpu.VMEM((8 * rows, width), bf16),
             pltpu.VMEM((8 * rows, hidden), f32),
@@ -1402,6 +1467,7 @@
             pltpu.VMEM((3, 8, hidden), f32),
             dma_sems(4),
             pltpu.VMEM((4, hidden // 4, width), bf16),
+            pltpu.VMEM((6, 8, width), f32),
         )
         self.use(
             gather=PlaneGather(block),
@@ -1424,8 +1490,8 @@
 
     def finish(self, here, ins, outs, scratch):
         block_ref, first_ref, second_ref, gain_ref, totals_ref = ins[:5]
-        out_ref, first_grad, second_quarter, small_ref = outs
-        second_grad = scratch[14]
+        out_ref, first_grad, second_quarter, small_ref, branch_ref, vector_ref = outs
+        second_grad, vectors = scratch[14:16]
         (
             rows_buf,
             slope,
@@ -1493,10 +1559,10 @@
         held = self.held(scratch, "sums")
         self.parts["sums"].start(here, (sums,), None, held)
         second_grad[...] = second_sum[...].astype(bf16).reshape(second_grad.shape)
+        load_slope.wait()
+        self.moment("midway")
         self.parts["second"].start(here, (second_grad,), None, self.held(scratch, "second"))
         self.parts["sums"].finish(here, (sums,), (got,), held)
-        load_slope.wait()
-        self.between()
 
         def rows_of(first):
             factor_columns(first)
@@ -1530,6 +1596,7 @@
             part = first_grad.shape[2]
             for i in range(4):
                 first_grad[i] = whole[:, i * part : (i + 1) * part]
+            self.moment("closing")
 
         self.parts["scatter"].finish(
             here,
@@ -1540,6 +1607,29 @@
             lambda: first_ref[...],
             idle=idle,
         )
+        gradient_ref, normal_1, factor_1, gain_1, normal_2, factor_2, gain_2 = ins[9:16]
+        vectors[...] = jnp.zeros_like(vectors)
+
+        def pull(at):
+            piece = pl.ds(at, NARROW)
+            grad, gradient = out_ref[piece, :], gradient_ref[piece, :]
+            normal = normal_1[piece, :]
+            vectors[3] += fold(grad * normal)
+            vectors[4] += fold(grad)
+            vectors[5] += fold(gradient)
+            middle = gradient + norm_pull(grad, normal, factor_1[piece, :], gain_1[...])
+            out_ref[piece, :] = middle
+            normal = normal_2[piece, :]
+            vectors[1] += fold(middle * normal)
+            vectors[2] += fold(middle)
+            branch = norm_pull(middle, normal, factor_2[piece, :], gain_2[...])
+            vectors[0] += fold(branch)
+            branch_ref[piece, :] = branch.astype(bf16)
+
+        in_chunks(rows, NARROW, pull)
+        vector_ref[...] = jnp.zeros_like(vector_ref)
+        for i in range(6):
+            vector_ref[i : i + 1, :] = jnp.sum(vectors[i], axis=0, keepdims=True)
         held = self.held(scratch, "second")
         self.parts["second"].finish(here, (second_grad,), (second_quarter,), held)
         for i in range(3):
@@ -1547,8 +1637,8 @@
 
 
 class WeightGather(Task):
-    def __init__(self, weights, layer, axis, midway=False):
-        self.layer, self.axis, self.midway = layer, axis, midway
+    def __init__(self, weights, layer, axis, when="start"):
+        self.layer, self.axis, self.when = layer, axis, when
         self.arrays, self.spaces = (weights,), (pltpu.HBM,)
         self.outs = (jax.ShapeDtypeStruct(weights.shape[1:], weights.dtype),)
         self.out_spaces = (pltpu.HBM,)
@@ -1577,11 +1667,10 @@
         keep.start()
 
     def start(self, *held):
-        if not self.midway:
-            self.begin(*held)
-
-    def middle(self, *held):
-        if self.midway:
+        self.at_moment("start", *held)
+
+    def at_moment(self, name, *held):
+        if name == self.when:
             self.begin(*held)
 
     def finish(self, here, ins, outs, scratch):
@@ -1591,28 +1680,26 @@
         keep.wait()
 
 
-class LineThenRows(Parts):
-    moved = False
-
-    def __init__(self, values):
-        shape = jax.ShapeDtypeStruct(values.shape[1:], values.dtype)
-        self.arrays, self.spaces = (values,), (pltpu.VMEM,)
-        self.outs = (jax.ShapeDtypeStruct((4, *shape.shape), values.dtype),)
-        self.out_spaces = (pltpu.HBM,)
-        self.scratch = (pltpu.VMEM(shape.shape, values.dtype),)
-        self.use(line=LineScatter(values), rows=RowsGather(shape))
+class ThenRows(Parts):
+    def __init__(self, first, when):
+        self.when = when
+        shape = first.outs[0]
+        self.arrays, self.spaces = first.arrays, first.spaces
+        rows = RowsGather(shape)
+        self.outs, self.out_spaces = rows.outs, rows.out_spaces
+        self.scratch = (pltpu.VMEM(shape.shape, shape.dtype),)
+        self.use(first=first, rows=rows)
 
     def start(self, here, ins, outs, scratch):
-        self.parts["line"].start(here, ins, None, self.held(scratch, "line"))
-
-    def middle(self, here, ins, outs, scratch):
-        self.parts["line"].finish(here, ins, scratch[:1], self.held(scratch, "line"))
-        self.parts["rows"].start(here, scratch[:1], outs, self.held(scratch, "rows"))
-        self.moved = True
+        self.parts["first"].start(here, ins, None, self.held(scratch, "first"))
+
+    def at_moment(self, name, here, ins, outs, scratch):
+        if name == self.when:
+            self.parts["first"].finish(here, ins, scratch[:1], self.held(scratch, "first"))
+            self.parts["rows"].begin(here, scratch[:1], outs, self.held(scratch, "rows"))
 
     def finish(self, here, ins, outs, scratch):
-        if not self.moved:
-            self.middle(here, ins, outs, scratch)
+        self.at_moment("end", here, ins, outs, scratch)
         self.parts["rows"].finish(here, scratch[:1], outs, self.held(scratch, "rows"))
 
 
@@ -1761,12 +1848,13 @@
 
 
 class AttnForward(Parts):
-    def __init__(self, block, docs, scale, heads, biases, wide, layer, late):
+    def __init__(self, block, docs, scale, heads, biases, wide, layer, late=None):
         rows, width = block.shape
         self.head_width, self.layer, self.late = wide, layer, late
         here = 2 * wide
         self.arrays = (block, docs, scale, biases, *heads)
-        self.spaces = (pltpu.VMEM,) * 3 + (pltpu.HBM if late else pltpu.VMEM,) * (1 + len(heads))
+        far = pltpu.HBM if late else pltpu.VMEM
+        self.spaces = (far, far, pltpu.VMEM) + (far,) * (1 + len(heads))
         column = jax.ShapeDtypeStruct((8 * rows, here), bf16)
         self.outs = (
             jax.ShapeDtypeStruct((rows, width), f32),
@@ -1791,19 +1879,58 @@
         parts = dict(gather=PlaneGather(block), scatter=PlaneScatter(rows, width, 0))
         if late:
             parts.update(heads=HeadGather(*heads, layer), biases=LineGather(biases))
+            parts.update(tokens=PlaneMove(block, when="push"), docs=PlaneMove(docs, when="push"))
             self.outs += parts["heads"].outs + parts["biases"].outs
-            self.out_spaces += (pltpu.VMEM,) * 2
+            self.outs += (jax.ShapeDtypeStruct(docs.shape, f32),)
+            self.outs += (jax.ShapeDtypeStruct(block.shape, f32),) * 2
+            self.outs += (jax.ShapeDtypeStruct((rows, 1), f32),)
+            self.out_spaces += (pltpu.VMEM,) * 6
+            self.scratch += (pltpu.VMEM(block.shape, bf16), pltpu.VMEM(block.shape, bf16))
+            self.arrays += tuple(late)
+            self.spaces += (pltpu.VMEM,) * 2
         self.use(**parts)
 
     def start(self, here, ins, outs, scratch):
-        self.parts["gather"].start(here, ins[:1], scratch[:1], self.held(scratch, "gather"))
         if self.late:
-            self.parts["heads"].start(here, ins[4:6], outs[8:9], self.held(scratch, "heads"))
-            self.parts["biases"].start(here, ins[3:4], outs[9:10], self.held(scratch, "biases"))
+            for name, at, target in (("tokens", 0, scratch[7]), ("docs", 1, outs[10])):
+                self.parts[name].start(here, (ins[at],), (target,), self.held(scratch, name))
+        else:
+            self.parts["gather"].start(here, ins[:1], scratch[:1], self.held(scratch, "gather"))
+
+    def first_norm(self, here, ins, outs, scratch):
+        tokens, block = scratch[7:9]
+        residual_ref, normal_ref, factor_ref = outs[11:14]
+        moves = [
+            (self.parts[name], (here, (ins[at],), (target,), self.held(scratch, name)))
+            for name, at, target in (("tokens", 0, tokens), ("docs", 1, outs[10]))
+        ]
+        for part, held in moves:
+            part.at_moment("push", *held)
+        self.parts["biases"].start(here, ins[3:4], outs[9:10], self.held(scratch, "biases"))
+        self.parts["heads"].start(here, ins[4:6], outs[8:9], self.held(scratch, "heads"))
+        for part, held in moves:
+            part.finish(*held)
+        values = tokens[...].astype(f32)
+        residual_ref[...] = values
+        width = values.shape[1]
+        centered = values - jnp.sum(values, axis=1, keepdims=True) / width
+        spread = jnp.sum(centered * centered, axis=1, keepdims=True) / width
+        factor = lax.rsqrt(spread + epsilon)
+        factor_ref[...] = factor
+        normal = centered * factor
+        normal_ref[...] = normal
+        block[...] = (normal * ins[6][...] + ins[7][...]).astype(bf16)
+        return block
 
     def finish(self, here, ins, outs, scratch):
         block_ref, doc_ref, scale_ref = ins[:3]
         heads_ref, bias_ref = outs[8:10] if self.late else (ins[4], ins[3])
+        if self.late:
+            doc_ref = outs[10]
+            block_ref = self.first_norm(here, ins, outs, scratch)
+            self.parts["gather"].start(
+                here, (block_ref,), scratch[:1], self.held(scratch, "gather")
+            )
         out_ref, rows_out, q_ref, k_ref, v_ref, z_ref, o_ref, l_ref = outs[:8]
         rows_buf, v_cols, s_buf, acc, top, total, save = scratch[:7]
         rows, model_width = block_ref.shape
@@ -1835,7 +1962,7 @@
 
         self.parts["gather"].finish(
             here,
-            ins[:1],
+            (block_ref,),
             scratch[:1],
             self.held(scratch, "gather"),
             None if self.late else work,
@@ -1846,7 +1973,7 @@
             self.parts["heads"].finish(here, ins[4:6], outs[8:9], self.held(scratch, "heads"))
             self.parts["biases"].finish(here, ins[3:4], outs[9:10], self.held(scratch, "biases"))
             in_chunks(8 * rows, rows, work)
-        self.between()
+        self.moment("midway")
 
         def rows_of(first):
             out = attend_block(
@@ -1863,25 +1990,32 @@
             self.held(scratch, "scatter"),
             rows_of,
             lambda: heads_ref[3].reshape(width, model_width),
+            idle=lambda: self.moment("closing"),
         )
         keep_rows.wait()
 
 
 class AttnBackward(Parts):
-    def __init__(self, block, docs, scale, heads, q, k, v, z, o, logs, attn_rows, ship):
+    def __init__(
+        self, block, docs, scale, heads, q, k, v, z, o, logs, attn_rows, ship, norm, hidden
+    ):
         rows, width = block.shape
         kinds, _, wide, _ = heads.shape
         self.head_width = wide
         here = 2 * wide
         self.arrays = (block, docs, scale, heads, q, k, v, z, o, logs, attn_rows)
         self.spaces = (pltpu.VMEM,) * 10 + (pltpu.HBM,)
+        self.arrays += (*norm, hidden)
+        self.spaces += (pltpu.VMEM,) * 5
         self.outs = (
             jax.ShapeDtypeStruct((rows, width), f32),
             jax.ShapeDtypeStruct((kinds, wide, width // 2) if ship else heads.shape, bf16),
-            jax.ShapeDtypeStruct((3, here), f32),
+            jax.ShapeDtypeStruct((4, 4, here), f32),
+            jax.ShapeDtypeStruct((rows, width), bf16),
+            jax.ShapeDtypeStruct((8, width), f32),
         )
         self.ship = ship
-        self.out_spaces = (pltpu.VMEM,) * 3
+        self.out_spaces = (pltpu.VMEM,) * 5
         self.scratch = (
             pltpu.VMEM((8 * rows, width), bf16),
             pltpu.VMEM((8 * rows, width), bf16),
@@ -1893,6 +2027,7 @@
             pltpu.VMEM((here, width), f32),
             pltpu.VMEM((3, 8, here), f32),
             dma_sems(1),
+            pltpu.VMEM((2, 8, width), f32),
             *([pltpu.VMEM(heads.shape, bf16)] if ship else []),
         )
         parts = dict(gather=PlaneGather(block), scatter=PlaneScatter(rows, width, 0))
@@ -1909,7 +2044,8 @@
 
     def finish(self, here, ins, outs, scratch):
         block_ref, doc_ref, scale_ref, heads_ref, q_ref, k_ref, v_ref, z_ref, o_ref, l_ref = ins[:10]
-        out_ref, quarter_ref, small_ref = outs
+        out_ref, quarter_ref, hidden_ref, rounded_ref, vector_ref = outs
+        middle_ref, normal_ref, factor_ref, gain_ref, sums_ref = ins[11:16]
         (
             rows_buf,
             attn_rows,
@@ -1921,7 +2057,8 @@
             out_sum,
             small,
         ) = scratch[:9]
-        heads_grad = scratch[10] if self.ship else quarter_ref
+        vectors = scratch[10]
+        heads_grad = scratch[11] if self.ship else quarter_ref
         rows, model_width = block_ref.shape
         wide = self.head_width
         width = 2 * wide
@@ -1965,7 +2102,12 @@
             small[1] += fold(grad.astype(f32))
 
         self.parts["gather"].finish(
-            here, ins[:1], scratch[:1], self.held(scratch, "gather"), work
+            here,
+            ins[:1],
+            scratch[:1],
+            self.held(scratch, "gather"),
+            work,
+            lambda: self.moment("soon"),
         )
 
         def settle(first):
@@ -1976,7 +2118,7 @@
             small[2] += fold(value_grad.astype(f32))
 
         in_chunks(8 * rows, rows, settle)
-        self.between()
+        self.moment("midway")
 
         def early():
             self.load(ins, scratch).wait()
@@ -1991,6 +2133,7 @@
             if self.ship:
                 self.parts["heads"].start(here, (heads_grad,), None, self.held(scratch, "heads"))
 
+        early()
         self.parts["scatter"].finish(
             here,
             None,
@@ -1998,47 +2141,155 @@
             self.held(scratch, "scatter"),
             lambda first: proj[pl.ds(first, rows), :],
             lambda: heads_ref[0:3].reshape(3 * width, model_width),
-            early=early,
-        )
+            idle=lambda: self.moment("closing"),
+        )
+        vectors[...] = jnp.zeros_like(vectors)
+
+        def pull(at):
+            piece = pl.ds(at, NARROW)
+            grad, normal = out_ref[piece, :], normal_ref[piece, :]
+            vectors[0] += fold(grad * normal)
+            vectors[1] += fold(grad)
+            gradient = middle_ref[piece, :] + norm_pull(
+                grad, normal, factor_ref[piece, :], gain_ref[...]
+            )
+            out_ref[piece, :] = gradient
+            rounded_ref[piece, :] = gradient.astype(bf16)
+
+        in_chunks(rows, NARROW, pull)
+        scale_cols, query_cols, value_cols = (
+            jnp.sum(small[i], axis=0, keepdims=True) for i in range(3)
+        )
+        vector_ref[...] = jnp.zeros_like(vector_ref)
+        for i in range(2):
+            vector_ref[i : i + 1, :] = jnp.sum(vectors[i], axis=0, keepdims=True)
+        lane = lax.broadcasted_iota(jnp.int32, (1, width), 1)
+        place = lax.broadcasted_iota(jnp.int32, (1, model_width), 1)
+        scale_row = jnp.zeros((1, model_width), f32)
+        for i in range(2):
+            head = ((2 * here.core + i) * 2 + here.x) * 2 + here.y
+            own = (lane >= i * wide) & (lane < (i + 1) * wide)
+            total = jnp.sum(jnp.where(own, scale_cols, 0.0), axis=1, keepdims=True)
+            scale_row = scale_row + jnp.where(place == head, total, 0.0)
+        vector_ref[2:3, :] = scale_row
+        pairs = [
+            jnp.concatenate(
+                [cols[:, i * wide : (i + 1) * wide] for cols in (query_cols, value_cols)], axis=1
+            )
+            for i in range(2)
+        ]
+        for shard in range(4):
+            for row, source in enumerate((2, 0, 1)):
+                cut = sums_ref[source : source + 1, shard * width : (shard + 1) * width]
+                hidden_ref[shard, row : row + 1, :] = cut
+            own = here.core == shard // 2
+            hidden_ref[shard, 3:4, :] = jnp.where(own, pairs[shard % 2], 0.0)
         if self.ship:
             held = self.held(scratch, "heads")
             self.parts["heads"].finish(here, (heads_grad,), (quarter_ref,), held)
-        for i in range(3):
-            small_ref[i : i + 1, :] = jnp.sum(small[i], axis=0, keepdims=True)
-
-
-def format_kernel(f0, f1, s0, s1, h0, h1, first_ref, second_ref, qkv_ref, out_ref):
-    part = first_ref.shape[2] // 4
-    half = h0.shape[3]
-    for layer, (first, second, heads) in enumerate(((f0, s0, h0), (f1, s1, h1))):
+
+
+def finish_kernel(layers, *refs):
+    (layer_ref, grad_ref), refs = refs[:2], refs[2:]
+    groups = []
+    for _ in range(6):
+        groups.append(refs[:layers])
+        refs = refs[layers:]
+    firsts, seconds, heads_all, hiddens, earlies, lates = groups
+    (
+        layer_out,
+        grad_out,
+        attn_gain,
+        attn_bias,
+        qkv_out,
+        bias_out,
+        scale_out,
+        out_out,
+        out_shift,
+        post_gain,
+        post_bias,
+        ffn_gain,
+        ffn_bias,
+        first_out,
+        first_shift,
+        mid_gain,
+        mid_bias,
+        second_out,
+        second_shift,
+    ) = refs
+    layer_out[...] = layer_ref[...]
+    grad_out[...] = grad_ref[...].astype(f32)
+    for layer in range(layers):
+        first, second, heads, hidden = (g[layer] for g in (firsts, seconds, heads_all, hiddens))
+        part = first.shape[2]
+        wide, half = heads.shape[2:]
+        row = slice(layer, layer + 1)
+        for i, ref in enumerate((out_shift, post_gain, post_bias, ffn_gain, ffn_bias, second_shift)):
+            ref[row, :] = earlies[layer][i : i + 1, :]
+        for i, ref in enumerate((attn_gain, attn_bias)):
+            ref[row, :] = lates[layer][i : i + 1, :]
+        scale_out[row, :] = lates[layer][2:3, 0 : scale_out.shape[1]]
         for i in range(4):
-            first_ref[layer, :, i * part : (i + 1) * part] = first[i].astype(f32)
-            second_ref[layer, i * part : (i + 1) * part, :] = second[i].astype(f32)
+            cut = slice(i * part, (i + 1) * part)
+            first_out[layer, :, cut] = first[i].astype(f32)
+            second_out[layer, cut, :] = second[i].astype(f32)
+            for at, ref in enumerate((first_shift, mid_gain, mid_bias)):
+                ref[row, cut] = hidden[i, at : at + 1, :]
+        biases = [hidden[2 * y, 3:4, :] + hidden[2 * y + 1, 3:4, :] for y in range(2)]
+        for i in range(2):
+            bias_out[layer, i : i + 1, :] = jnp.concatenate(
+                [each[:, i * wide : (i + 1) * wide] for each in biases], axis=1
+            )
         for core in range(2):
-            here = pl.ds(core * half, half)
+            here = slice(core * half, (core + 1) * half)
             for kind in range(3):
                 pair = jnp.concatenate([heads[core, kind], heads[2 + core, kind]], axis=0)
-                qkv_ref[layer, kind, here, :] = jnp.transpose(pair.astype(f32))
+                qkv_out[layer, kind, here, :] = jnp.transpose(pair.astype(f32))
             for y in range(2):
-                wide = heads.shape[2]
-                out_ref[layer, y * wide : (y + 1) * wide, here] = heads[2 * y + core, 3].astype(f32)
-
-
-def format_weights(first, second, heads):
-    _, width, part = first[0].shape
+                out_out[layer, y * wide : (y + 1) * wide, here] = heads[2 * y + core, 3].astype(f32)
+
+
+def finish_all(layer_output, gradient, heads_count, *groups):
+    firsts, seconds, heads = groups[:3]
+    layers = len(firsts)
+    rows, width = layer_output.shape
+    part = firsts[0].shape[2]
     wide = heads[0].shape[2]
-    return pl.pallas_call(
-        format_kernel,
-        out_shape=(
-            jax.ShapeDtypeStruct((2, width, 4 * part), f32),
-            jax.ShapeDtypeStruct((2, 4 * part, width), f32),
-            jax.ShapeDtypeStruct((2, 3, width, 2 * wide), f32),
-            jax.ShapeDtypeStruct((2, 2 * wide, width), f32),
-        ),
-        in_specs=[pl.BlockSpec(memory_space=pltpu.VMEM)] * 6,
-        out_specs=[pl.BlockSpec(memory_space=pltpu.VMEM)] * 4,
-        compiler_params=vmem_params(None, 40),
-    )(*first, *second, *heads)
+    vector = jax.ShapeDtypeStruct((layers, width), f32)
+    hidden = jax.ShapeDtypeStruct((layers, 4 * part), f32)
+    outs = (
+        jax.ShapeDtypeStruct((rows, width), bf16),
+        jax.ShapeDtypeStruct((rows, width), f32),
+        vector,
+        vector,
+        jax.ShapeDtypeStruct((layers, 3, width, 2 * wide), f32),
+        jax.ShapeDtypeStruct((layers, 2, 2 * wide), f32),
+        jax.ShapeDtypeStruct((layers, heads_count), f32),
+        jax.ShapeDtypeStruct((layers, 2 * wide, width), f32),
+        vector,
+        vector,
+        vector,
+        vector,
+        vector,
+        jax.ShapeDtypeStruct((layers, width, 4 * part), f32),
+        hidden,
+        hidden,
+        hidden,
+        jax.ShapeDtypeStruct((layers, 4 * part, width), f32),
+        vector,
+    )
+    arrays = [layer_output, gradient] + [each for group in groups for each in group]
+    results = list(
+        pl.pallas_call(
+            partial(finish_kernel, layers),
+            out_shape=outs,
+            in_specs=[pl.BlockSpec(memory_space=pltpu.VMEM)] * len(arrays),
+            out_specs=[pl.BlockSpec(memory_space=pltpu.VMEM)] * len(outs),
+            compiler_params=vmem_params(None, 44),
+        )(*arrays)
+    )
+    results[4] = jnp.transpose(results[4], (0, 2, 1, 3))
+    return tuple(results)
 
 
 def plane_device(
@@ -2076,9 +2327,7 @@
     width = 2 * head_width
     ids = iter(range(1, 64))
 
-    doc_row = segment_ids.astype(f32)[None, :]
-    ((residual,), (docs,)) = run_tasks(ids, PlaneMove(tokens), PlaneMove(doc_row))
-    residual = residual.astype(f32)
+    docs = segment_ids.astype(f32)[None, :]
 
     def cut(values, at, size, axis):
         return lax.dynamic_slice_in_dim(values, at * size, size, axis)
@@ -2100,20 +2349,25 @@
 
     stored = []
     for layer in range(layers):
-        attn_in, attn_normal, attn_factor = norm_local(
-            residual, ln_attn_gain[layer], ln_attn_bias[layer]
-        )
+        late = None
+        if layer == 0:
+            late = (ln_attn_gain[layer][None], ln_attn_bias[layer][None])
+            block = tokens
+        else:
+            attn_in, attn_normal, attn_factor = norm_local(
+                residual, ln_attn_gain[layer], ln_attn_bias[layer]
+            )
+            block = attn_in.astype(bf16)
         scale = jnp.sum(head_onehot * head_scale[layer][None, :], axis=1)
         scale_row = jnp.repeat(scale, head_width)[None, :]
-        late = layer == 0
-        sides = [WeightGather(fc1_weight, layer, 1, late)]
+        sides = [WeightGather(fc1_weight, layer, 1, "midway" if late else "start")]
         if not late:
             sides.append(WeightGather(fc2_weight, layer, 0))
         ((branch, attn_rows, q, k, v, scaled, attended, logs, *got), (first_here,), *rest) = (
             run_tasks(
                 ids,
                 AttnForward(
-                    attn_in.astype(bf16),
+                    block,
                     docs,
                     scale_row,
                     (qkv_rows, out_weight) if late else (heads_here[layer],),
@@ -2127,7 +2381,7 @@
             )
         )
         if late:
-            heads_here[0], small = got
+            heads_here[0], small, docs, residual, attn_normal, attn_factor = got
 
             def hidden_rows(at):
                 part = small[:, :, 2 * width + at * quarter : 2 * width + (at + 1) * quarter]
@@ -2142,7 +2396,7 @@
         ffn_in, ffn_normal, ffn_factor = norm_local(middle, ln_ffn_gain[layer], ln_ffn_bias[layer])
         sides = []
         if layer + 1 < layers:
-            sides.append(HeadGather(qkv_rows, out_weight, layer + 1, late))
+            sides.append(HeadGather(qkv_rows, out_weight, layer + 1, "midway" if late else "start"))
         else:
             sides.append(PlaneMove(cotangent))
         ((ffn_out, ffn_rows, slope, hidden_normal, mixed, totals, *got), (side,)) = run_tasks(
@@ -2155,7 +2409,7 @@
                 gain_hidden[layer][None],
                 bias_hidden[layer][None],
                 layer,
-                late,
+                late is not None,
             ),
             *sides,
             mib=48,
@@ -2194,8 +2448,8 @@
 
     first_done, second_done = [None] * layers, [None] * layers
     heads_done, hidden_done = [None] * layers, [None] * layers
-    early_vectors, late_vectors = [None] * layers, [None] * layers
-    pending = None
+    early_done, late_done = [None] * layers, [None] * layers
+    late_vectors = None
     for layer in reversed(range(layers)):
         (
             first_here,
@@ -2220,143 +2474,93 @@
             mixed,
             totals,
         ) = stored[layer]
-        second_shift_grad = jnp.sum(gradient, axis=0)
-        if pending is None:
+        last = layer + 1 == layers
+        if last:
             sides = [PlaneMove(residual.astype(bf16), back=True)]
         else:
-            sides = [HeadScatter(pending[0]), LineThenRows(pending[1])]
-        ((ffn_in_grad, first_grad, second_grad, hidden_grad), *got) = run_tasks(
+            sides = [RowsGather(heads_grad, "midway")]
+            sides.append(ThenRows(LineScatter(hidden_grad), "closing"))
+            sides += [LineSum(early_vectors), StepSum(late_vectors)]
+        ((gradient, first_grad, second_grad, hidden_sums, branch_b, early_vectors), *got) = (
+            run_tasks(
+                ids,
+                FfnBackward(
+                    gradient_b,
+                    first_here,
+                    second_here,
+                    gain_hidden[layer][None],
+                    slope,
+                    hidden_normal,
+                    mixed,
+                    ffn_rows,
+                    totals,
+                    gradient,
+                    (
+                        ffn_normal,
+                        ffn_factor,
+                        ln_ffn_gain[layer][None],
+                        post_normal,
+                        post_factor,
+                        ln_post_gain[layer][None],
+                    ),
+                ),
+                *sides,
+                mib=60,
+            )
+        )
+        if last:
+            layer_output = got[0][0]
+        else:
+            heads_done[layer + 1], hidden_done[layer + 1] = got[0][0], got[1][0]
+            early_done[layer + 1], late_vectors = got[2][0], got[3][0]
+        sides = [ThenRows(LineScatter(first_grad), "soon"), RowsGather(second_grad)]
+        sides.append(StepSum(early_vectors))
+        if not last:
+            sides.append(LineSum(late_vectors))
+        ((gradient, heads_grad, hidden_grad, gradient_b, late_vectors), *got) = run_tasks(
             ids,
-            FfnBackward(
-                gradient_b,
-                first_here,
-                second_here,
-                gain_hidden[layer][None],
-                slope,
-                hidden_normal,
-                mixed,
-                ffn_rows,
-                totals,
+            AttnBackward(
+                branch_b,
+                docs,
+                scale_row,
+                heads_here[layer],
+                q,
+                k,
+                v,
+                scaled,
+                attended,
+                logs,
+                attn_rows,
+                True,
+                (gradient, attn_normal, attn_factor, ln_attn_gain[layer][None]),
+                hidden_sums,
             ),
             *sides,
-            mib=60,
-        )
-        if pending is None:
-            layer_output = got[0][0]
-        else:
-            heads_grad, hidden_done[layer + 1] = got[0][0], got[1][0]
-        ffn_gain_grad = jnp.sum(ffn_in_grad * ffn_normal, axis=0)
-        ffn_bias_grad = jnp.sum(ffn_in_grad, axis=0)
-        middle_grad = gradient + norm_back(ffn_in_grad, ffn_normal, ffn_factor, ln_ffn_gain[layer])
-        post_gain_grad = jnp.sum(middle_grad * post_normal, axis=0)
-        post_bias_grad = jnp.sum(middle_grad, axis=0)
-        branch_grad = norm_back(middle_grad, post_normal, post_factor, ln_post_gain[layer])
-        out_shift_grad = jnp.sum(branch_grad, axis=0)
-        early_vectors[layer] = jnp.stack(
-            [
-                out_shift_grad,
-                post_gain_grad,
-                post_bias_grad,
-                ffn_gain_grad,
-                ffn_bias_grad,
-                second_shift_grad,
-            ]
-        )
-        sides = [LineThenRows(first_grad), RowsGather(second_grad)]
-        if layer == 0:
-            sides.append(RowsGather(heads_grad))
-            known = early_vectors + late_vectors[1:]
-            count = sum(each.shape[0] for each in known)
-            known.append(jnp.zeros((-count % 8, model_width), f32))
-            sides.append(PlaneSum(jnp.concatenate(known, axis=0)))
-        ((attn_in_grad, heads_grad, small_grad), (first_done[layer],), (second_done[layer],), *rest) = (
-            run_tasks(
-                ids,
-                AttnBackward(
-                    branch_grad.astype(bf16),
-                    docs,
-                    scale_row,
-                    heads_here[layer],
-                    q,
-                    k,
-                    v,
-                    scaled,
-                    attended,
-                    logs,
-                    attn_rows,
-                    layer == 0,
-                ),
-                *sides,
-                mib=48,
-            )
-        )
-        scale_grad = jnp.sum(
-            head_onehot * jnp.sum(small_grad[0].reshape(2, head_width), axis=1)[:, None], axis=0
-        )
-        bias_grad = jnp.transpose(small_grad[1:].reshape(2, 2, head_width), (1, 0, 2))
-        hidden_grad = jnp.roll(hidden_grad, 1, axis=0).reshape(3, 4, quarter)
-        hidden_grad = jnp.concatenate(
-            [
-                jnp.transpose(hidden_grad, (1, 0, 2)).reshape(4, -1),
-                lax.dynamic_update_slice(
-                    jnp.zeros((4, width), f32), bias_grad.reshape(2, width), (2 * core, 0)
-                ),
-            ],
-            axis=1,
-        ).reshape(4, -1, 128)
-        pending = (heads_grad, hidden_grad)
-        late_vectors[layer] = jnp.stack(
-            [
-                jnp.sum(attn_in_grad * attn_normal, axis=0),
-                jnp.sum(attn_in_grad, axis=0),
-                jnp.pad(scale_grad, (0, model_width - heads_all)),
-            ]
-        )
-        gradient = middle_grad + norm_back(
-            attn_in_grad, attn_normal, attn_factor, ln_attn_gain[layer]
-        )
-        gradient_b = gradient.astype(bf16)
-    (heads_done[1],), (summed,) = rest
-    ((vectors,), (heads_done[0],), (hidden_done[0],), (input_grad,)) = run_tasks(
-        ids,
-        PlaneThenLineSum(late_vectors[0], summed),
-        RowsGather(pending[0]),
-        LineThenRows(pending[1]),
-        PlaneMove(gradient_b, back=True),
+            mib=48,
+        )
+        first_done[layer], second_done[layer], early_vectors = got[0][0], got[1][0], got[2][0]
+        if not last:
+            late_done[layer + 1] = got[3][0]
+    ((late_done[0],), (early_done[0],), (input_grad,), (heads_done[0],), (hidden_done[0],)) = (
+        run_tasks(
+            ids,
+            PlaneThenLineSum(late_vectors),
+            LineSum(early_vectors),
+            PlaneMove(gradient_b, back=True),
+            RowsGather(heads_grad),
+            ThenRows(LineScatter(hidden_grad), "midway"),
+        )
     )
-    input_grad = input_grad.astype(f32)
-    early = vectors[: 6 * layers].reshape(layers, 6, model_width)
-    late = jnp.stack([vectors[-3:], vectors[6 * layers : 6 * layers + 3]])
-    first_grad, second_grad, qkv_grad, out_grad = format_weights(
+    return finish_all(
+        layer_output,
+        input_grad,
+        heads_all,
         first_done,
         second_done,
         heads_done,
-    )
-    hidden = jnp.stack(hidden_done).reshape(layers, 4, -1)
-    bias_grad = jnp.sum(hidden[:, :, 3 * quarter :].reshape(layers, 2, 2, 2, head_width), axis=2)
-    bias_grad = jnp.transpose(bias_grad, (0, 2, 1, 3)).reshape(layers, 2, width)
-    hidden = hidden[:, :, : 3 * quarter].reshape(layers, 4, 3, quarter)
-    hidden = jnp.transpose(hidden, (0, 2, 1, 3)).reshape(layers, 3, hidden_here)
-    return (
-        layer_output,
-        input_grad,
-        late[:, 0],
-        late[:, 1],
-        jnp.transpose(qkv_grad, (0, 2, 1, 3)),
-        bias_grad,
-        late[:, 2, :heads_all],
-        out_grad,
-        early[:, 0],
-        early[:, 1],
-        early[:, 2],
-        early[:, 3],
-        early[:, 4],
-        first_grad,
-        hidden[:, 0],
-        hidden[:, 1],
-        hidden[:, 2],
-        second_grad,
-        early[:, 5],
+        hidden_done,
+        early_done,
+        late_done,
     )
 
 

time: 629 us -> 577 us (0.917)
  Pallas kernels: 548 us -> 522 us
  other arithmetic: 25.1 us -> 11.6 us
  local copies, waits for them, and re-layouts: 42.3 us -> 32.1 us
    pallas_call x10 -> x9, Pallas kernels: 543 us -> 516 us  [run_tasks(): pl.pallas_call(kernel, out_shape=[out for task in tasks for out in task.o...]
    reduce_sum x14 -> x0, other arithmetic: 15 us -> none  [the longest x2 5.79 us: plane_device(): post_gain_grad = jnp.sum(middle_grad * post_normal, axis=0)]
    unnamed x154 -> x152, local copies, waits for them, and re-layouts: 33.8 us -> 25.4 us
where the time goes in v1:
time: 577 us; the launch traced here: 567 us
  Pallas kernels  522 us (90%)
  local copies, waits for them, and re-layouts  32.1 us (6%)
  other arithmetic  11.6 us (2%)
    pallas_call x9, Pallas kernels, run_tasks(): pl.pallas_call(kernel, out_shape=[out for task in tasks for out in task.o...  516 us
    unnamed x152, local copies, waits for them, and re-layouts  25.4 us

profile of v1, /device:TPU:1, one launch (start us, length us, event | category | flops | bytes accessed | tf_op | source)
XLA Modules:
  0.0 567.4 jit_solution(15522194392743522703)
XLA Ops:
  4.2 1.7 copy.46
  6.7 1.6 copy-done.4
  8.3 1.0 copy-done.11
  10.4 80.4 %shard_map.339 = (f32[256,1024]{1,0:T(8,128)S(1)}, bf16[2048,1024]{1,0:T(8,128)(2,1)}, bf16[2048,128]{1,0:T(8,128)(2,1)S(1)}, bf16[2048,128]{1,0:T(8,128)(2,1)S(...) custom-call(bf16[256,1024]{1,0:T(8,128)(2,1)S(1)} %copy-done.25, ...), custom_call_target="tpu_custom_call" | custom-call | tf_op jit(solution)/shard_map/pallas_call | solution.py:619
  92.5 1.3 fusion.2
  94.1 1.2 add_convert_fusion.3
  95.5 54.3 %shard_map.340 = (f32[256,1024]{1,0:T(8,128)S(1)}, bf16[2048,1024]{1,0:T(8,128)(2,1)}, f32[2048,512]{1,0:T(8,128)}, f32[2048,512]{1,0:T(8,128)}, bf16[2048,512]{...) custom-call(bf16[256,1024]{1,0:T(8,128)(2,1)S(1)} %get-tuple-element.2, ...), custom_call_target="tpu_custom_call" | custom-call | tf_op jit(solution)/shard_map/pallas_call | solution.py:619
  152.1 1.4 add_convert_fusion.2
  153.6 1.6 copy-done.5
  155.2 1.2 copy-done.9
  156.5 1.0 copy-done.14
  157.5 49.3 %shard_map.341 = (f32[256,1024]{1,0:T(8,128)S(1)}, bf16[2048,1024]{1,0:T(8,128)(2,1)}, bf16[2048,128]{1,0:T(8,128)(2,1)S(1)}, bf16[2048,128]{1,0:T(8,128)(2,1)S(...) custom-call(bf16[256,1024]{1,0:T(8,128)(2,1)S(1)} %copy-done.14, ...), custom_call_target="tpu_custom_call" | custom-call | tf_op jit(solution)/shard_map/pallas_call | solution.py:619
  207.3 1.3 fusion
  208.9 1.3 add_convert_fusion.1
  210.3 55.1 %shard_map.342 = (f32[256,1024]{1,0:T(8,128)S(1)}, bf16[2048,1024]{1,0:T(8,128)(2,1)}, f32[2048,512]{1,0:T(8,128)}, f32[2048,512]{1,0:T(8,128)}, bf16[2048,512]{...) custom-call(bf16[256,1024]{1,0:T(8,128)(2,1)S(1)} %get-tuple-element.215.refs_0_, ...), custom_call_target="tpu_custom_call" | custom-call | tf_op jit(solution)/shard_map/pallas_call | solution.py:619
  265.4 1.0 add_convert_fusion.refs_16_
  266.4 1.1 convert_element_type.23.refs_9_
  269.1 56.0 %shard_map.343 = (f32[256,1024]{1,0:T(8,128)}, bf16[4,1024,128]{2,1,0:T(8,128)(2,1)}, bf16[128,1024]{1,0:T(8,128)(2,1)}, f32[3,512]{1,0:T(4,128)}, bf16[256,1024...) custom-call(bf16[256,1024]{1,0:T(8,128)(2,1)} %copy-done.13, bf16[1024,512]{1,0:T(8,128)(2,1)} %copy-done.6, ...), custom_call_target="tpu_custom_call" | custom-call | tf_op jit(solution)/shard_map/pallas_call | solution.py:619
  328.8 63.1 %shard_map.344 = (f32[256,1024]{1,0:T(8,128)S(1)}, bf16[4,64,512]{2,1,0:T(8,128)(2,1)S(1)}, f32[4,4,128]{2,1,0:T(4,128)S(1)}, bf16[256,1024]{1,0:T(8,128)(2,1)S(...) custom-call(bf16[256,1024]{1,0:T(8,128)(2,1)S(1)} %copy-done.44, ...), custom_call_target="tpu_custom_call" | custom-call | tf_op jit(solution)/shard_map/pallas_call | solution.py:619
  397.8 61.3 %shard_map.345 = (f32[256,1024]{1,0:T(8,128)}, bf16[4,1024,128]{2,1,0:T(8,128)(2,1)}, bf16[128,1024]{1,0:T(8,128)(2,1)}, f32[3,512]{1,0:T(4,128)}, bf16[256,1024...) custom-call(bf16[256,1024]{1,0:T(8,128)(2,1)} %copy-done.42, ...), custom_call_target="tpu_custom_call" | custom-call | tf_op jit(solution)/shard_map/pallas_call | solution.py:619
  463.4 65.4 %shard_map.346 = (f32[256,1024]{1,0:T(8,128)}, bf16[4,64,512]{2,1,0:T(8,128)(2,1)S(1)}, f32[4,4,128]{2,1,0:T(4,128)S(1)}, bf16[256,1024]{1,0:T(8,128)(2,1)S(1)},...) custom-call(bf16[256,1024]{1,0:T(8,128)(2,1)S(1)} %copy-done.43, ...), custom_call_target="tpu_custom_call" | custom-call | tf_op jit(solution)/shard_map/pallas_call | solution.py:619
  528.8 31.4 %shard_map.347 = (f32[8,1024]{1,0:T(8,128)S(1)}, f32[8,1024]{1,0:T(8,128)S(1)}, bf16[256,1024]{1,0:T(8,128)(2,1)S(1)}, bf16[4,4,64,512]{3,2,1,0:T(8,128)(2,1)S(1)}, f32[4,4,128]{2,1,0:T(4,128)S(1)}) custom-call(f32[8,1024]{1,0:T(8,128)S(1)} %get-tuple-element.176.refs_0_, f32[8,1024]{1,0:T(8,128)S(1)} %get-tuple-element.177.refs_1_, ...), custom_call_target="tpu_custom_call" | custom-call | tf_op jit(solution)/shard_map/pallas_call | solution.py:619
  560.3 1.2 copy-done.21
  561.5 5.7 %shard_map.348 = (bf16[256,1024]{1,0:T(8,128)(2,1)}, f32[256,1024]{1,0:T(8,128)}, f32[2,1024]{1,0:T(2,128)}, f32[2,1024]{1,0:T(2,128)}, f32[2,3,1024,128]{3,2,1,...) custom-call(bf16[256,1024]{1,0:T(8,128)(2,1)S(1)} %copy-done.24, ...), custom_call_target="tpu_custom_call" | custom-call | tf_op jit(solution)/shard_map/pallas_call | solution.py:2283
  (191 shorter events, 25.6 us)
Async XLA Ops:
  0.7 91.2 %copy-start.69 = (f32[2,1024]{1,0:T(2,128)S(1)}, f32[2,1024]{1,0:T(2,128)}, u32[]{:S(2)}) copy-start(f32[2,1024]{1,0:T(2,128)} %param.29) | copy-start | bytes 24580
  4.2 88.2 %copy-start.74 = (f32[2,1024]{1,0:T(2,128)S(1)}, f32[2,1024]{1,0:T(2,128)}, u32[]{:S(2)}) copy-start(f32[2,1024]{1,0:T(2,128)} %param.32) | copy-start | bytes 24580
  5.9 87.9 %copy-start.2 = (bf16[2,1024,3,128]{1,3,2,0:T(8,128)(2,1)}, bf16[2,1024,3,128]{1,3,2,0:T(8,128)(2,1)S(1)}, u32[]{:S(2)}) copy-start(bf16[2,1024,3,128]{1,3,2,0:T(8,128)(2,1)S(1)} %copy.46) | copy-start | bytes 4718596
  5.9 86.5 %copy-start.73 = (f32[2,1024]{1,0:T(2,128)S(1)}, f32[2,1024]{1,0:T(2,128)}, u32[]{:S(2)}) copy-start(f32[2,1024]{1,0:T(2,128)} %param.30) | copy-start | bytes 24580
  5.9 86.5 %copy-start.70 = (f32[2,1024]{1,0:T(2,128)S(1)}, f32[2,1024]{1,0:T(2,128)}, u32[]{:S(2)}) copy-start(f32[2,1024]{1,0:T(2,128)} %param.31) | copy-start | bytes 24580
  92.4 57.4 %copy-start.67 = (f32[1,1024]{1,0:T(1,128)}, f32[1,1024]{1,0:T(1,128)S(1)}, u32[]{:S(2)}) copy-start(f32[1,1024]{1,0:T(1,128)S(1)} %get-tuple-element.241.refs_15_) | copy-start | bytes 12292
  92.4 57.4 %copy-start.68 = (f32[1,1024]{1,0:T(1,128)}, f32[1,1024]{1,0:T(1,128)S(1)}, u32[]{:S(2)}) copy-start(f32[1,1024]{1,0:T(1,128)S(1)} %get-tuple-element.261.refs_12_) | copy-start | bytes 12292
  92.4 114.9 %copy-start.65 = (f32[1,1024]{1,0:T(1,128)}, f32[1,1024]{1,0:T(1,128)S(1)}, u32[]{:S(2)}) copy-start(f32[1,1024]{1,0:T(1,128)S(1)} %get-tuple-element.240.refs_15_) | copy-start | bytes 12292
  92.5 116.5 %copy-start.66 = (f32[1,1024]{1,0:T(1,128)}, f32[1,1024]{1,0:T(1,128)S(1)}, u32[]{:S(2)}) copy-start(f32[1,1024]{1,0:T(1,128)S(1)} %get-tuple-element.260.refs_12_) | copy-start | bytes 12292
  94.1 56.6 %copy-start.72 = (f32[2,1024]{1,0:T(2,128)S(1)}, f32[2,1024]{1,0:T(2,128)}, u32[]{:S(2)}) copy-start(f32[2,1024]{1,0:T(2,128)} %param.39) | copy-start | bytes 24580
  95.4 114.8 %copy-start.55 = (f32[1,512]{1,0:T(1,128)}, f32[1,512]{1,0:T(1,128)S(1)}, u32[]{:S(2)}) copy-start(f32[1,512]{1,0:T(1,128)S(1)} %get-tuple-element.250.refs_4_.refs_3_) | copy-start | bytes 6148
  269.1 56.2 %copy-start.35 = (bf16[2048,128]{1,0:T(8,128)(2,1)S(1)}, bf16[2048,128]{1,0:T(8,128)(2,1)}, u32[]{:S(2)}) copy-start(bf16[2048,128]{1,0:T(8,128)(2,1)} %copy-done.34) | copy-start | bytes 1572868
  269.1 56.2 %copy-start.37 = (bf16[2048,128]{1,0:T(8,128)(2,1)S(1)}, bf16[2048,128]{1,0:T(8,128)(2,1)}, u32[]{:S(2)}) copy-start(bf16[2048,128]{1,0:T(8,128)(2,1)} %copy-done.36) | copy-start | bytes 1572868
  269.1 56.2 %copy-start.39 = (bf16[2048,128]{1,0:T(8,128)(2,1)S(1)}, bf16[2048,128]{1,0:T(8,128)(2,1)}, u32[]{:S(2)}) copy-start(bf16[2048,128]{1,0:T(8,128)(2,1)} %copy-done.38) | copy-start | bytes 1572868
  269.1 56.2 %copy-start.41 = (bf16[2048,128]{1,0:T(8,128)(2,1)S(1)}, bf16[2048,128]{1,0:T(8,128)(2,1)}, u32[]{:S(2)}) copy-start(bf16[2048,128]{1,0:T(8,128)(2,1)} %copy-done.40) | copy-start | bytes 1572868
  397.8 61.3 %copy-start.27 = (bf16[2048,128]{1,0:T(8,128)(2,1)S(1)}, bf16[2048,128]{1,0:T(8,128)(2,1)}, u32[]{:S(2)}) copy-start(bf16[2048,128]{1,0:T(8,128)(2,1)} %copy-done.26) | copy-start | bytes 1572868
  397.8 61.4 %copy-start.29 = (bf16[2048,128]{1,0:T(8,128)(2,1)S(1)}, bf16[2048,128]{1,0:T(8,128)(2,1)}, u32[]{:S(2)}) copy-start(bf16[2048,128]{1,0:T(8,128)(2,1)} %copy-done.28) | copy-start | bytes 1572868
  397.8 61.4 %copy-start.31 = (bf16[2048,128]{1,0:T(8,128)(2,1)S(1)}, bf16[2048,128]{1,0:T(8,128)(2,1)}, u32[]{:S(2)}) copy-start(bf16[2048,128]{1,0:T(8,128)(2,1)} %copy-done.30) | copy-start | bytes 1572868
  397.8 61.4 %copy-start.33 = (bf16[2048,128]{1,0:T(8,128)(2,1)S(1)}, bf16[2048,128]{1,0:T(8,128)(2,1)}, u32[]{:S(2)}) copy-start(bf16[2048,128]{1,0:T(8,128)(2,1)} %copy-done.32) | copy-start | bytes 1572868
  463.4 96.8 %copy-start.18 = (bf16[4,128,1024]{2,1,0:T(8,128)(2,1)S(1)}, bf16[4,128,1024]{2,1,0:T(8,128)(2,1)}, u32[]{:S(2)}) copy-start(bf16[4,128,1024]{2,1,0:T(8,128)(2,1)} %get-tuple-element.185.refs_5_) | copy-start | bytes 3145732
  463.4 96.9 %copy-start.20 = (bf16[4,4,64,512]{3,2,1,0:T(8,128)(2,1)S(1)}, bf16[4,4,64,512]{3,2,1,0:T(8,128)(2,1)}, u32[]{:S(2)}) copy-start(bf16[4,4,64,512]{3,2,1,0:T(8,128)(2,1)} %get-tuple-element.187.refs_7_) | copy-start | bytes 3145732
  463.4 96.9 %copy-start.24 = (bf16[256,1024]{1,0:T(8,128)(2,1)S(1)}, bf16[256,1024]{1,0:T(8,128)(2,1)}, u32[]{:S(2)}) copy-start(bf16[256,1024]{1,0:T(8,128)(2,1)} %get-tuple-element.133.refs_0_) | copy-start | bytes 1572868
  463.4 96.9 %copy-start.49 = (f32[8,1024]{1,0:T(8,128)S(1)}, f32[8,1024]{1,0:T(8,128)}, u32[]{:S(2)}) copy-start(f32[8,1024]{1,0:T(8,128)} %get-tuple-element.191.refs_11_) | copy-start | bytes 98308
  463.4 96.9 %copy-start.59 = (f32[4,4,128]{2,1,0:T(4,128)S(1)}, f32[4,4,128]{2,1,0:T(4,128)}, u32[]{:S(2)}) copy-start(f32[4,4,128]{2,1,0:T(4,128)} %get-tuple-element.189.refs_9_) | copy-start | bytes 24580
  (51 other events, 289.2 us)

commit v2 on v1

--- a/solution.py
+++ b/solution.py
@@ -587,13 +587,27 @@
         pass
 
 
-def run_tasks(ids, *tasks, mib=24):
+def run_tasks(ids, *tasks):
     reach = []
     for task in tasks:
         reach += [way for way in task.reach if way not in reach]
 
+    near = []
+    for task in tasks:
+        near += [space == pltpu.VMEM for space in task.spaces]
+    arrays = [array for task in tasks for array in task.arrays]
+    loaded = [i for i, each in enumerate(near) if each]
+
     def kernel(*refs):
         refs = list(refs)
+        *refs, load_sem = refs
+        held = refs[len(refs) - len(loaded) :]
+        refs = refs[: len(refs) - len(loaded)]
+        loads = []
+        for slot, index in enumerate(loaded):
+            loads.append(pltpu.make_async_copy(refs[index], held[slot], load_sem.at[slot]))
+            loads[-1].start()
+            refs[index] = held[slot]
         views = [[], [], []]
         for kind, name in enumerate(("arrays", "outs", "scratch")):
             for task in tasks:
@@ -605,6 +619,8 @@
         for way in reach:
             pl.semaphore_signal(barrier, inc=1, device_id=here.peer(*way), device_id_type=MESH_ID)
         pl.semaphore_wait(barrier, len(reach))
+        for each in loads:
+            each.wait()
         for task, *held in zip(tasks, *views):
             task.start(here, *held)
 
@@ -619,11 +635,13 @@
     results = pl.pallas_call(
         kernel,
         out_shape=[out for task in tasks for out in task.outs],
-        in_specs=[pl.BlockSpec(memory_space=s) for task in tasks for s in task.spaces],
+        in_specs=[pl.BlockSpec(memory_space=pltpu.HBM)] * len(arrays),
         out_specs=[pl.BlockSpec(memory_space=s) for task in tasks for s in task.out_spaces],
-        scratch_shapes=[each for task in tasks for each in task.scratch],
-        compiler_params=vmem_params(next(ids), mib),
-    )(*[array for task in tasks for array in task.arrays])
+        scratch_shapes=[each for task in tasks for each in task.scratch]
+        + [pltpu.VMEM(arrays[i].shape, arrays[i].dtype) for i in loaded]
+        + [dma_sems(len(loaded))],
+        compiler_params=vmem_params(next(ids), 60),
+    )(*arrays)
     results = list(results)
     split = []
     for task in tasks:
@@ -1019,18 +1037,25 @@
         if name == self.when:
             self.begin(*held)
 
-    def finish(self, here, ins, outs, scratch):
-        keeps, aways = self.copies(here, ins, outs, scratch)
+    def arrive(self, kind, outs, scratch):
         for shard in range(2):
             for part in range(2):
-                for kind, piece in enumerate(self.pieces(outs, shard, part)):
-                    recv_sem = scratch[1].at[4 * kind + 2 * shard + part]
-                    pltpu.make_async_copy(piece, piece, recv_sem).wait()
+                piece = self.pieces(outs, shard, part)[kind]
+                recv_sem = scratch[1].at[4 * kind + 2 * shard + part]
+                pltpu.make_async_copy(piece, piece, recv_sem).wait()
+
+    def sent(self, here, ins, outs, scratch):
+        keeps, aways = self.copies(here, ins, outs, scratch)
         for index, each in enumerate(aways):
             if index % 4:
                 each.wait_send()
         for kind in range(2):
             pl.when(here.z // 2 != here.core)(aways[4 * kind].wait_send)
+
+    def finish(self, here, ins, outs, scratch):
+        for kind in range(2):
+            self.arrive(kind, outs, scratch)
+        self.sent(here, ins, outs, scratch)
 
 
 class LineScatter(Task):
@@ -1275,25 +1300,6 @@
         return scratch[first:last]
 
 
-class PlaneThenLineSum(Parts):
-    def __init__(self, values):
-        self.arrays, self.spaces = (values,), (pltpu.VMEM,)
-        self.outs = (jax.ShapeDtypeStruct(values.shape, f32),)
-        self.out_spaces = (pltpu.VMEM,)
-        self.scratch = (pltpu.VMEM(values.shape, f32),)
-        self.use(plane=PlaneSum(values), line=LineSum(values))
-
-    def start(self, here, ins, outs, scratch):
-        self.parts["plane"].start(here, ins, None, self.held(scratch, "plane"))
-
-    def finish(self, here, ins, outs, scratch):
-        self.parts["plane"].finish(here, ins, scratch[:1], self.held(scratch, "plane"))
-        held = self.held(scratch, "line")
-        self.parts["line"].start(here, scratch[:1], None, held)
-        self.moment("midway")
-        self.parts["line"].finish(here, scratch[:1], outs, held)
-
-
 def norm_pull(grad_out, normal, factor, gain_row):
     scaled = grad_out * gain_row
     width = scaled.shape[1]
@@ -1302,17 +1308,69 @@
     return factor * (scaled - mean - normal * inner)
 
 
+class StepThenLine(Parts):
+    def __init__(self, values):
+        self.arrays, self.spaces = (values,), (pltpu.VMEM,)
+        self.outs = (jax.ShapeDtypeStruct(values.shape, f32),)
+        self.out_spaces = (pltpu.VMEM,)
+        self.scratch = (pltpu.VMEM(values.shape, f32),)
+        self.use(step=StepSum(values), line=LineSum(values))
+
+    def start(self, here, ins, outs, scratch):
+        self.parts["step"].start(here, ins, scratch[:1], self.held(scratch, "step"))
+
+    def at_moment(self, name, here, ins, outs, scratch):
+        held = (here, ins, scratch[:1], self.held(scratch, "step"))
+        self.parts["step"].at_moment(name, *held)
+        if name == "tail":
+            self.parts["step"].finish(*held)
+            self.parts["line"].start(here, scratch[:1], outs, self.held(scratch, "line"))
+
+    def finish(self, here, ins, outs, scratch):
+        self.parts["line"].finish(here, scratch[:1], outs, self.held(scratch, "line"))
+
+
+def normalize(values):
+    width = values.shape[1]
+    centered = values - jnp.sum(values, axis=1, keepdims=True) / width
+    factor = lax.rsqrt(jnp.sum(centered * centered, axis=1, keepdims=True) / width + epsilon)
+    return centered * factor, factor
+
+
+def wide_column(column):
+    return jnp.broadcast_to(column, (column.shape[0], 128))
+
+
+def hidden_row(small_ref, layer, at, part):
+    first = small_ref.shape[2] - (3 - at) * part
+    return jnp.concatenate(
+        [small_ref[z, layer : layer + 1, first : first + part] for z in range(4)], axis=1
+    )
+
+
+def scale_of(here, head_scale_ref, layer, wide):
+    row = head_scale_ref[layer : layer + 1, :]
+    place = lax.broadcasted_iota(jnp.int32, row.shape, 1)
+    pair = []
+    for i in range(2):
+        head = ((2 * here.core + i) * 2 + here.x) * 2 + here.y
+        pair.append(jnp.sum(jnp.where(place == head, row, 0.0), axis=1, keepdims=True))
+    lane = lax.broadcasted_iota(jnp.int32, (1, 2 * wide), 1)
+    return jnp.where(lane < wide, pair[0], pair[1])
+
+
 NARROW = 128
 CHUNK = 256
 
 
 class FfnForward(Parts):
-    def __init__(self, block, first, second, shift, gain, bias, layer, late):
+    def __init__(self, block, first, second, small, middle, shift, norm, layer, late):
         rows, width = block.shape
         hidden = first.shape[1]
-        self.late = late
-        self.arrays = (block, first, second, shift, gain, bias)
-        self.spaces = (pltpu.VMEM,) * 2 + (pltpu.HBM if late else pltpu.VMEM,) + (pltpu.VMEM,) * 3
+        self.late, self.layer, self.last = late, layer, norm is None
+        self.arrays = (block, first, second, small, middle, shift, *(norm or ()))
+        self.spaces = (pltpu.VMEM,) * 2 + (pltpu.HBM if late else pltpu.VMEM,)
+        self.spaces += (pltpu.VMEM,) * (len(self.arrays) - 3)
         self.outs = (
             jax.ShapeDtypeStruct((rows, width), f32),
             jax.ShapeDtypeStruct((8 * rows, width), bf16),
@@ -1322,6 +1380,12 @@
             jax.ShapeDtypeStruct((2, 8 * rows), f32),
         )
         self.out_spaces = (pltpu.VMEM,) + (pltpu.HBM,) * 4 + (pltpu.VMEM,)
+        self.outs += (jax.ShapeDtypeStruct((rows, width), bf16),)
+        if norm:
+            self.outs += (jax.ShapeDtypeStruct((rows, width), f32),)
+            self.outs += (jax.ShapeDtypeStruct((rows, 128), f32),)
+        self.out_spaces += (pltpu.VMEM,) * (len(self.outs) - 6)
+        self.base = len(self.outs)
         self.scratch = (
             pltpu.VMEM((8 * rows, width), bf16),
             pltpu.VMEM((8 * rows, hidden), f32),
@@ -1346,13 +1410,15 @@
         self.parts["gather"].start(here, ins[:1], scratch[:1], self.held(scratch, "gather"))
         if self.late:
             held = self.held(scratch, "second")
-            self.parts["second"].start(here, ins[2:3], outs[6:7], held)
+            self.parts["second"].start(here, ins[2:3], outs[self.base :], held)
 
     def finish(self, here, ins, outs, scratch):
-        block_ref, first_ref, second_ref, shift_ref, gain_ref, bias_ref = ins
+        block_ref, first_ref, second_ref, small_ref, middle_ref, row_ref = ins[:6]
+        part = first_ref.shape[1] // 4
+        shift, gain, bias = (hidden_row(small_ref, self.layer, at, part) for at in range(3))
         out_ref, rows_out, slope_out, normal_out, mixed_out, total_ref = outs[:6]
         if self.late:
-            second_ref = outs[6]
+            second_ref = outs[self.base]
         rows_buf, before, active, mixed, sums, columns, save = scratch[:7]
         rows = block_ref.shape[0]
         hidden_all = 8 * first_ref.shape[1]
@@ -1367,7 +1433,7 @@
 
             def step(at):
                 piece = pl.ds(pl.multiple_of(first + at, CHUNK), CHUNK)
-                u = before[piece, :] + shift_ref[...]
+                u = before[piece, :] + shift
                 area = 0.5 * (1.0 + lax.erf(u * 0.5**0.5))
                 a = u * area
                 active[piece, :] = a
@@ -1393,7 +1459,7 @@
         self.parts["sums"].finish(here, (sums,), (total_ref,), held)
         if self.late:
             held = self.held(scratch, "second")
-            self.parts["second"].finish(here, ins[2:3], outs[6:7], held)
+            self.parts["second"].finish(here, ins[2:3], outs[self.base :], held)
         self.moment("midway")
 
         def rows_of(first):
@@ -1406,7 +1472,7 @@
                 pair = columns[pl.ds(at, CHUNK), :]
                 normal = (active[piece, :] - pair[:, 0:1]) * pair[:, 64:65]
                 active[piece, :] = normal
-                mixed[piece, :] = (normal * gain_ref[...] + bias_ref[...]).astype(bf16)
+                mixed[piece, :] = (normal * gain + bias).astype(bf16)
 
             in_chunks(rows, CHUNK, step)
             return mixed[pl.ds(first, rows), :]
@@ -1428,17 +1494,46 @@
             lambda: second_ref[...],
             idle=idle,
         )
+        layer = slice(self.layer, self.layer + 1)
+        after = slice(self.layer + 1, self.layer + 2)
+
+        def settle(at):
+            piece = pl.ds(at, NARROW)
+            residual = middle_ref[piece, :] + out_ref[piece, :] + row_ref[layer, :]
+            out_ref[piece, :] = residual
+            if self.last:
+                outs[6][piece, :] = residual.astype(bf16)
+            else:
+                normal, factor = normalize(residual)
+                outs[6][piece, :] = (normal * ins[6][after, :] + ins[7][after, :]).astype(bf16)
+                outs[7][piece, :] = normal
+                outs[8][piece, :] = wide_column(factor)
+
+        in_chunks(rows, NARROW, settle)
         for each in (keep_rows, keep_slope, keep_mixed, keep_normal):
             each.wait()
 
 
 class FfnBackward(Parts):
     def __init__(
-        self, block, first, second, gain, slope, normal, mixed, ffn_rows, totals, gradient, norms
+        self,
+        block,
+        first,
+        second,
+        small,
+        slope,
+        normal,
+        mixed,
+        ffn_rows,
+        totals,
+        gradient,
+        norms,
+        layer,
     ):
+        self.layer = layer
         rows, width = block.shape
         hidden = second.shape[0]
-        self.arrays = (block, first, second, gain, totals, slope, normal, mixed, ffn_rows)
+        self.arrays = (block, first, second, small, totals, slope, normal, mixed, ffn_rows)
         self.spaces = (pltpu.VMEM,) * 5 + (pltpu.HBM,) * 4
         self.arrays += (gradient, *norms)
         self.spaces += (pltpu.VMEM,) * 7
@@ -1489,7 +1584,8 @@
             each.start()
 
     def finish(self, here, ins, outs, scratch):
-        block_ref, first_ref, second_ref, gain_ref, totals_ref = ins[:5]
+        block_ref, first_ref, second_ref, hidden_ref, totals_ref = ins[:5]
+        mid_gain = hidden_row(hidden_ref, self.layer, 1, first_ref.shape[1] // 4)
         out_ref, first_grad, second_quarter, small_ref, branch_ref, vector_ref = outs
         second_grad, vectors = scratch[14:16]
         (
@@ -1541,7 +1637,7 @@
                 grad = grads[piece, :]
                 small[0] += fold(grad * normal)
                 small[1] += fold(grad)
-                scaled = grad * gain_ref[...]
+                scaled = grad * mid_gain
                 grads[piece, :] = scaled
                 columns[pl.ds(at, CHUNK), :] = both_columns(
                     jnp.sum(scaled, axis=1, keepdims=True),
@@ -1609,20 +1705,23 @@
         )
         gradient_ref, normal_1, factor_1, gain_1, normal_2, factor_2, gain_2 = ins[9:16]
         vectors[...] = jnp.zeros_like(vectors)
+        layer = slice(self.layer, self.layer + 1)
 
         def pull(at):
             piece = pl.ds(at, NARROW)
-            grad, gradient = out_ref[piece, :], gradient_ref[piece, :]
+            grad, gradient = out_ref[piece, :], gradient_ref[piece, :].astype(f32)
             normal = normal_1[piece, :]
             vectors[3] += fold(grad * normal)
             vectors[4] += fold(grad)
             vectors[5] += fold(gradient)
-            middle = gradient + norm_pull(grad, normal, factor_1[piece, :], gain_1[...])
+            middle = gradient + norm_pull(
+                grad, normal, factor_1[piece, 0:1], gain_1[layer, :]
+            )
             out_ref[piece, :] = middle
             normal = normal_2[piece, :]
             vectors[1] += fold(middle * normal)
             vectors[2] += fold(middle)
-            branch = norm_pull(middle, normal, factor_2[piece, :], gain_2[...])
+            branch = norm_pull(middle, normal, factor_2[piece, 0:1], gain_2[layer, :])
             vectors[0] += fold(branch)
             branch_ref[piece, :] = branch.astype(bf16)
 
@@ -1848,7 +1947,9 @@
 
 
 class AttnForward(Parts):
-    def __init__(self, block, docs, scale, heads, biases, wide, layer, late=None):
+    def __init__(
+        self, block, docs, scale, heads, biases, wide, layer, norms, residual=None, late=None
+    ):
         rows, width = block.shape
         self.head_width, self.layer, self.late = wide, layer, late
         here = 2 * wide
@@ -1866,7 +1967,12 @@
             jax.ShapeDtypeStruct((8 * rows, here), f32),
             jax.ShapeDtypeStruct((8 * rows // BLOCK, 1, 2 * BLOCK), f32),
         )
-        self.out_spaces = (pltpu.VMEM, pltpu.HBM) + (pltpu.VMEM,) * 6
+        wide_shape = jax.ShapeDtypeStruct((rows, 128), f32)
+        self.outs += (self.outs[0], wide_shape, self.outs[0], wide_shape)
+        self.outs += (jax.ShapeDtypeStruct((rows, width), bf16),)
+        self.out_spaces = (pltpu.VMEM, pltpu.HBM) + (pltpu.VMEM,) * 11
+        self.arrays += tuple(norms)
+        self.spaces += (pltpu.VMEM,) * 5
         self.scratch = (
             pltpu.VMEM((8 * rows, width), bf16),
             pltpu.VMEM((here, 8 * rows), bf16),
@@ -1883,50 +1989,54 @@
             self.outs += parts["heads"].outs + parts["biases"].outs
             self.outs += (jax.ShapeDtypeStruct(docs.shape, f32),)
             self.outs += (jax.ShapeDtypeStruct(block.shape, f32),) * 2
-            self.outs += (jax.ShapeDtypeStruct((rows, 1), f32),)
+            self.outs += (wide_shape,)
             self.out_spaces += (pltpu.VMEM,) * 6
             self.scratch += (pltpu.VMEM(block.shape, bf16), pltpu.VMEM(block.shape, bf16))
+            self.scratch += (pltpu.VMEM(docs.shape, docs.dtype),)
             self.arrays += tuple(late)
             self.spaces += (pltpu.VMEM,) * 2
+        else:
+            self.arrays += (residual,)
+            self.spaces += (pltpu.VMEM,)
+        self.base = 3 + 1 + len(heads)
         self.use(**parts)
 
     def start(self, here, ins, outs, scratch):
         if self.late:
-            for name, at, target in (("tokens", 0, scratch[7]), ("docs", 1, outs[10])):
+            for name, at, target in (("tokens", 0, scratch[7]), ("docs", 1, scratch[9])):
                 self.parts[name].start(here, (ins[at],), (target,), self.held(scratch, name))
         else:
             self.parts["gather"].start(here, ins[:1], scratch[:1], self.held(scratch, "gather"))
 
     def first_norm(self, here, ins, outs, scratch):
         tokens, block = scratch[7:9]
-        residual_ref, normal_ref, factor_ref = outs[11:14]
+        residual_ref, normal_ref, factor_ref = outs[16:19]
         moves = [
             (self.parts[name], (here, (ins[at],), (target,), self.held(scratch, name)))
-            for name, at, target in (("tokens", 0, tokens), ("docs", 1, outs[10]))
+            for name, at, target in (("tokens", 0, tokens), ("docs", 1, scratch[9]))
         ]
         for part, held in moves:
             part.at_moment("push", *held)
-        self.parts["biases"].start(here, ins[3:4], outs[9:10], self.held(scratch, "biases"))
-        self.parts["heads"].start(here, ins[4:6], outs[8:9], self.held(scratch, "heads"))
+        self.parts["biases"].start(here, ins[3:4], outs[14:15], self.held(scratch, "biases"))
+        self.parts["heads"].start(here, ins[4:6], outs[13:14], self.held(scratch, "heads"))
         for part, held in moves:
             part.finish(*held)
+        outs[15][...] = scratch[9][...].astype(f32)
+        gain, bias = (ref[self.layer : self.layer + 1, :] for ref in ins[self.base + 5 :])
         values = tokens[...].astype(f32)
         residual_ref[...] = values
-        width = values.shape[1]
-        centered = values - jnp.sum(values, axis=1, keepdims=True) / width
-        spread = jnp.sum(centered * centered, axis=1, keepdims=True) / width
-        factor = lax.rsqrt(spread + epsilon)
-        factor_ref[...] = factor
-        normal = centered * factor
+        normal, factor = normalize(values)
+        factor_ref[...] = wide_column(factor)
         normal_ref[...] = normal
-        block[...] = (normal * ins[6][...] + ins[7][...]).astype(bf16)
+        block[...] = (normal * gain + bias).astype(bf16)
         return block
 
     def finish(self, here, ins, outs, scratch):
         block_ref, doc_ref, scale_ref = ins[:3]
-        heads_ref, bias_ref = outs[8:10] if self.late else (ins[4], ins[3])
+        scale_row = scale_of(here, scale_ref, self.layer, self.head_width)
+        heads_ref, bias_ref = outs[13:15] if self.late else (ins[4], ins[3])
         if self.late:
-            doc_ref = outs[10]
+            doc_ref = outs[15]
             block_ref = self.first_norm(here, ins, outs, scratch)
             self.parts["gather"].start(
                 here, (block_ref,), scratch[:1], self.held(scratch, "gather")
@@ -1970,16 +2080,17 @@
         keep_rows = pltpu.make_async_copy(rows_buf, rows_out, save.at[0])
         keep_rows.start()
         if self.late:
-            self.parts["heads"].finish(here, ins[4:6], outs[8:9], self.held(scratch, "heads"))
-            self.parts["biases"].finish(here, ins[3:4], outs[9:10], self.held(scratch, "biases"))
+            self.parts["heads"].arrive(0, outs[13:14], self.held(scratch, "heads"))
+            self.parts["biases"].finish(here, ins[3:4], outs[14:15], self.held(scratch, "biases"))
             in_chunks(8 * rows, rows, work)
+            self.parts["heads"].arrive(1, outs[13:14], self.held(scratch, "heads"))
         self.moment("midway")
 
         def rows_of(first):
             out = attend_block(
                 wide, first, q_ref, k_ref, v_cols, doc_ref, o_ref, l_ref, s_buf, acc, top, total
             )
-            z = (out * scale_ref[...]).astype(bf16)
+            z = (out * scale_row).astype(bf16)
             z_ref[pl.ds(first, rows), :] = z
             return z
 
@@ -1992,13 +2103,38 @@
             lambda: heads_ref[3].reshape(width, model_width),
             idle=lambda: self.moment("closing"),
         )
+        residual_ref = outs[16] if self.late else ins[self.base + 5]
+        layer = slice(self.layer, self.layer + 1)
+        shift, gain_1, bias_1, gain_2, bias_2 = (
+            ref[layer, :] for ref in ins[self.base : self.base + 5]
+        )
+        normal_1, factor_1, normal_2, factor_2, next_ref = outs[8:13]
+
+        def settle(at):
+            piece = pl.ds(at, NARROW)
+            normal, factor = normalize(out_ref[piece, :] + shift)
+            normal_1[piece, :] = normal
+            factor_1[piece, :] = wide_column(factor)
+            middle = residual_ref[piece, :] + (normal * gain_1 + bias_1)
+            out_ref[piece, :] = middle
+            normal, factor = normalize(middle)
+            normal_2[piece, :] = normal
+            factor_2[piece, :] = wide_column(factor)
+            next_ref[piece, :] = (normal * gain_2 + bias_2).astype(bf16)
+
+        in_chunks(rows, NARROW, settle)
         keep_rows.wait()
+        if self.late:
+            held = self.held(scratch, "heads")
+            self.parts["heads"].sent(here, ins[4:6], outs[13:14], held)
 
 
 class AttnBackward(Parts):
     def __init__(
-        self, block, docs, scale, heads, q, k, v, z, o, logs, attn_rows, ship, norm, hidden
+        self, block, docs, scale, heads, q, k, v, z, o, logs, attn_rows, norm, hidden, layer, end
     ):
+        self.end = end
+        self.layer = layer
         rows, width = block.shape
         kinds, _, wide, _ = heads.shape
         self.head_width = wide
@@ -2007,15 +2143,23 @@
         self.spaces = (pltpu.VMEM,) * 10 + (pltpu.HBM,)
         self.arrays += (*norm, hidden)
         self.spaces += (pltpu.VMEM,) * 5
-        self.outs = (
-            jax.ShapeDtypeStruct((rows, width), f32),
-            jax.ShapeDtypeStruct((kinds, wide, width // 2) if ship else heads.shape, bf16),
-            jax.ShapeDtypeStruct((4, 4, here), f32),
-            jax.ShapeDtypeStruct((rows, width), bf16),
-            jax.ShapeDtypeStruct((8, width), f32),
-        )
-        self.ship = ship
-        self.out_spaces = (pltpu.VMEM,) * 5
+        move, heads_sum = PlaneMove(block, back=True, when="push"), HeadScatter(heads)
+        vector, sums = jax.ShapeDtypeStruct((8, width), f32), jax.ShapeDtypeStruct((4, 4, here), f32)
+        quarter = heads_sum.outs[0]
+        if end:
+            tail = dict(
+                move=move,
+                vectors=PlaneSum(vector),
+                line=LineSum(vector),
+                rows=RowsGather(quarter),
+                hidden=ThenRows(LineScatter(sums), "push"),
+            )
+            self.outs = move.outs + (vector,) + tail["rows"].outs + tail["hidden"].outs
+            self.out_spaces = (pltpu.HBM, pltpu.VMEM, pltpu.HBM, pltpu.HBM)
+        else:
+            self.outs = (jax.ShapeDtypeStruct((rows, width), f32), quarter, sums)
+            self.outs += (jax.ShapeDtypeStruct((rows, width), bf16), vector)
+            self.out_spaces = (pltpu.VMEM,) * 5
         self.scratch = (
             pltpu.VMEM((8 * rows, width), bf16),
             pltpu.VMEM((8 * rows, width), bf16),
@@ -2028,11 +2172,19 @@
             pltpu.VMEM((3, 8, here), f32),
             dma_sems(1),
             pltpu.VMEM((2, 8, width), f32),
-            *([pltpu.VMEM(heads.shape, bf16)] if ship else []),
-        )
+            pltpu.VMEM(heads.shape, bf16),
+        )
+        if end:
+            self.scratch += (
+                pltpu.VMEM((rows, width), f32),
+                pltpu.VMEM(quarter.shape, bf16),
+                pltpu.VMEM(sums.shape, f32),
+                pltpu.VMEM((rows, width), bf16),
+                pltpu.VMEM(vector.shape, f32),
+                pltpu.VMEM(vector.shape, f32),
+            )
         parts = dict(gather=PlaneGather(block), scatter=PlaneScatter(rows, width, 0))
-        if ship:
-            parts["heads"] = HeadScatter(heads)
+        parts.update(heads=heads_sum, **(tail if end else {}))
         self.use(**parts)
 
     def load(self, ins, scratch):
@@ -2044,7 +2196,8 @@
 
     def finish(self, here, ins, outs, scratch):
         block_ref, doc_ref, scale_ref, heads_ref, q_ref, k_ref, v_ref, z_ref, o_ref, l_ref = ins[:10]
-        out_ref, quarter_ref, hidden_ref, rounded_ref, vector_ref = outs
+        results = scratch[12:17] if self.end else outs
+        out_ref, quarter_ref, hidden_ref, rounded_ref, vector_ref = results
         middle_ref, normal_ref, factor_ref, gain_ref, sums_ref = ins[11:16]
         (
             rows_buf,
@@ -2058,7 +2211,8 @@
             small,
         ) = scratch[:9]
         vectors = scratch[10]
-        heads_grad = scratch[11] if self.ship else quarter_ref
+        heads_grad = scratch[11]
+        scale_row = scale_of(here, scale_ref, self.layer, self.head_width)
         rows, model_width = block_ref.shape
         wide = self.head_width
         width = 2 * wide
@@ -2086,7 +2240,7 @@
             grad = attend_block_back(
                 wide,
                 first,
-                (scaled_grad * scale_ref[...]).astype(bf16),
+                (scaled_grad * scale_row).astype(bf16),
                 q_ref,
                 k_ref,
                 k_cols,
@@ -2130,8 +2284,7 @@
             )
             heads_grad[0:3] = qkv_grad.astype(bf16).reshape(3, 2, wide, model_width)
             heads_grad[3] = out_sum[...].astype(bf16).reshape(2, wide, model_width)
-            if self.ship:
-                self.parts["heads"].start(here, (heads_grad,), None, self.held(scratch, "heads"))
+            self.parts["heads"].start(here, (heads_grad,), None, self.held(scratch, "heads"))
 
         early()
         self.parts["scatter"].finish(
@@ -2144,6 +2297,7 @@
             idle=lambda: self.moment("closing"),
         )
         vectors[...] = jnp.zeros_like(vectors)
+        layer = slice(self.layer, self.layer + 1)
 
         def pull(at):
             piece = pl.ds(at, NARROW)
@@ -2151,12 +2305,15 @@
             vectors[0] += fold(grad * normal)
             vectors[1] += fold(grad)
             gradient = middle_ref[piece, :] + norm_pull(
-                grad, normal, factor_ref[piece, :], gain_ref[...]
+                grad, normal, factor_ref[piece, 0:1], gain_ref[layer, :]
             )
             out_ref[piece, :] = gradient
             rounded_ref[piece, :] = gradient.astype(bf16)
 
         in_chunks(rows, NARROW, pull)
+        if self.end:
+            home = (here, (rounded_ref,), outs[:1], self.held(scratch, "move"))
+            self.parts["move"].start(*home)
         scale_cols, query_cols, value_cols = (
             jnp.sum(small[i], axis=0, keepdims=True) for i in range(3)
         )
@@ -2165,13 +2322,13 @@
             vector_ref[i : i + 1, :] = jnp.sum(vectors[i], axis=0, keepdims=True)
         lane = lax.broadcasted_iota(jnp.int32, (1, width), 1)
         place = lax.broadcasted_iota(jnp.int32, (1, model_width), 1)
-        scale_row = jnp.zeros((1, model_width), f32)
+        head_sums = jnp.zeros((1, model_width), f32)
         for i in range(2):
             head = ((2 * here.core + i) * 2 + here.x) * 2 + here.y
             own = (lane >= i * wide) & (lane < (i + 1) * wide)
             total = jnp.sum(jnp.where(own, scale_cols, 0.0), axis=1, keepdims=True)
-            scale_row = scale_row + jnp.where(place == head, total, 0.0)
-        vector_ref[2:3, :] = scale_row
+            head_sums = head_sums + jnp.where(place == head, total, 0.0)
+        vector_ref[2:3, :] = head_sums
         pairs = [
             jnp.concatenate(
                 [cols[:, i * wide : (i + 1) * wide] for cols in (query_cols, value_cols)], axis=1
@@ -2184,12 +2341,38 @@
                 hidden_ref[shard, row : row + 1, :] = cut
             own = here.core == shard // 2
             hidden_ref[shard, 3:4, :] = jnp.where(own, pairs[shard % 2], 0.0)
-        if self.ship:
-            held = self.held(scratch, "heads")
-            self.parts["heads"].finish(here, (heads_grad,), (quarter_ref,), held)
+        self.moment("tail")
+        held = (here, (heads_grad,), (quarter_ref,), self.held(scratch, "heads"))
+        if not self.end:
+            self.parts["heads"].finish(*held)
+            return
+        sum_held = (here, (vector_ref,), (scratch[17],), self.held(scratch, "vectors"))
+        line_held = (here, (scratch[17],), outs[1:2], self.held(scratch, "line"))
+        rows_held = (here, (quarter_ref,), outs[2:3], self.held(scratch, "rows"))
+        hidden_held = (here, (hidden_ref,), outs[3:4], self.held(scratch, "hidden"))
+        self.parts["vectors"].start(*sum_held)
+        self.parts["hidden"].start(*hidden_held)
+        self.parts["heads"].finish(*held)
+        self.parts["rows"].begin(*rows_held)
+        self.parts["vectors"].finish(*sum_held)
+        self.parts["line"].start(*line_held)
+        self.parts["move"].at_moment("push", *home)
+        self.parts["hidden"].at_moment("push", *hidden_held)
+        self.parts["line"].finish(*line_held)
+        self.parts["rows"].finish(*rows_held)
+        self.parts["hidden"].finish(*hidden_held)
+        self.parts["move"].finish(*home)
 
 
 def finish_kernel(layers, *refs):
+    count = 2 + 6 * layers
+    far, refs, sems = refs[:count], refs[count:-1], refs[-1]
+    refs, near = refs[: len(refs) - count], refs[len(refs) - count :]
+    loads = [pltpu.make_async_copy(a, b, sems.at[i]) for i, (a, b) in enumerate(zip(far, near))]
+    order = [0, 1] + [2 + g * layers + i for i in range(layers - 1, -1, -1) for g in range(6)]
+    for index in order:
+        loads[index].start()
+    refs = (*near, *refs)
     (layer_ref, grad_ref), refs = refs[:2], refs[2:]
     groups = []
     for _ in range(6):
@@ -2217,9 +2400,13 @@
         second_out,
         second_shift,
     ) = refs
+    loads[0].wait()
     layer_out[...] = layer_ref[...]
+    loads[1].wait()
     grad_out[...] = grad_ref[...].astype(f32)
-    for layer in range(layers):
+    for layer in range(layers - 1, -1, -1):
+        for group in range(6):
+            loads[2 + group * layers + layer].wait()
         first, second, heads, hidden = (g[layer] for g in (firsts, seconds, heads_all, hiddens))
         part = first.shape[2]
         wide, half = heads.shape[2:]
@@ -2283,9 +2470,13 @@
         pl.pallas_call(
             partial(finish_kernel, layers),
             out_shape=outs,
-            in_specs=[pl.BlockSpec(memory_space=pltpu.VMEM)] * len(arrays),
+            in_specs=[pl.BlockSpec(memory_space=pltpu.HBM)] * len(arrays),
             out_specs=[pl.BlockSpec(memory_space=pltpu.VMEM)] * len(outs),
-            compiler_params=vmem_params(None, 44),
+            scratch_shapes=[
+                *[pltpu.VMEM(each.shape, each.dtype) for each in arrays],
+                dma_sems(len(arrays)),
+            ],
+            compiler_params=vmem_params(None, 60),
         )(*arrays)
     )
     results[4] = jnp.transpose(results[4], (0, 2, 1, 3))
@@ -2327,7 +2518,7 @@
     width = 2 * head_width
     ids = iter(range(1, 64))
 
-    docs = segment_ids.astype(f32)[None, :]
+    docs = segment_ids[None, :]
 
     def cut(values, at, size, axis):
         return lax.dynamic_slice_in_dim(values, at * size, size, axis)
@@ -2343,93 +2534,79 @@
         ],
         axis=1,
     )
-    head_ids = ((2 * core + jnp.arange(2)) * 2 + x) * 2 + y
-    head_onehot = (head_ids[:, None] == jnp.arange(heads_all)[None, :]).astype(f32)
     heads_here = [None] * layers
+    norms = (out_bias, ln_post_gain, ln_post_bias, ln_ffn_gain, ln_ffn_bias)
+    attn_norm = (ln_attn_gain, ln_attn_bias)
 
     stored = []
     for layer in range(layers):
-        late = None
-        if layer == 0:
-            late = (ln_attn_gain[layer][None], ln_attn_bias[layer][None])
-            block = tokens
+        first, last = layer == 0, layer + 1 == layers
+        if first:
+            task = AttnForward(
+                tokens,
+                docs,
+                head_scale,
+                (qkv_rows, out_weight),
+                small,
+                head_width,
+                layer,
+                norms,
+                late=attn_norm,
+            )
+            sides = [WeightGather(fc1_weight, layer, 1, "midway")]
         else:
-            attn_in, attn_normal, attn_factor = norm_local(
-                residual, ln_attn_gain[layer], ln_attn_bias[layer]
+            task = AttnForward(
+                block,
+                docs,
+                head_scale,
+                (heads_here[layer],),
+                small,
+                head_width,
+                layer,
+                norms,
+                residual=residual,
             )
-            block = attn_in.astype(bf16)
-        scale = jnp.sum(head_onehot * head_scale[layer][None, :], axis=1)
-        scale_row = jnp.repeat(scale, head_width)[None, :]
-        sides = [WeightGather(fc1_weight, layer, 1, "midway" if late else "start")]
-        if not late:
-            sides.append(WeightGather(fc2_weight, layer, 0))
-        ((branch, attn_rows, q, k, v, scaled, attended, logs, *got), (first_here,), *rest) = (
-            run_tasks(
-                ids,
-                AttnForward(
-                    block,
-                    docs,
-                    scale_row,
-                    (qkv_rows, out_weight) if late else (heads_here[layer],),
-                    small,
-                    head_width,
-                    layer,
-                    late,
-                ),
-                *sides,
-                mib=40,
-            )
-        )
-        if late:
-            heads_here[0], small, docs, residual, attn_normal, attn_factor = got
-
-            def hidden_rows(at):
-                part = small[:, :, 2 * width + at * quarter : 2 * width + (at + 1) * quarter]
-                return jnp.transpose(part, (1, 0, 2)).reshape(layers, 4 * quarter)
-
-            shift_hidden, gain_hidden, bias_hidden = map(hidden_rows, range(3))
-        branch = branch + out_bias[layer]
-        post_out, post_normal, post_factor = norm_local(
-            branch, ln_post_gain[layer], ln_post_bias[layer]
-        )
-        middle = residual + post_out
-        ffn_in, ffn_normal, ffn_factor = norm_local(middle, ln_ffn_gain[layer], ln_ffn_bias[layer])
-        sides = []
-        if layer + 1 < layers:
-            sides.append(HeadGather(qkv_rows, out_weight, layer + 1, "midway" if late else "start"))
-        else:
-            sides.append(PlaneMove(cotangent))
-        ((ffn_out, ffn_rows, slope, hidden_normal, mixed, totals, *got), (side,)) = run_tasks(
+            sides = [WeightGather(fc1_weight, layer, 1), WeightGather(fc2_weight, layer, 0)]
+        (got, (first_here,), *rest) = run_tasks(ids, task, *sides)
+        middle, attn_rows, q, k, v, scaled, attended, logs = got[:8]
+        post_normal, post_factor, ffn_normal, ffn_factor, block = got[8:13]
+        if first:
+            heads_here[0], small, docs, _, attn_normal, attn_factor = got[13:]
+        here = (attn_normal, attn_factor)
+        sides = [PlaneMove(cotangent)]
+        if not last:
+            sides = [HeadGather(qkv_rows, out_weight, layer + 1, "midway" if first else "start")]
+        (got, (side,)) = run_tasks(
             ids,
             FfnForward(
-                ffn_in.astype(bf16),
+                block,
                 first_here,
-                fc2_weight if late else rest[0][0],
-                shift_hidden[layer][None],
-                gain_hidden[layer][None],
-                bias_hidden[layer][None],
+                fc2_weight if first else rest[0][0],
+                small,
+                middle,
+                fc2_bias,
+                None if last else attn_norm,
                 layer,
-                late is not None,
+                first,
             ),
             *sides,
-            mib=48,
-        )
-        second_here = got[0] if late else rest[0][0]
-        if layer + 1 < layers:
+        )
+        residual, ffn_rows, slope, hidden_normal, mixed, totals, block = got[:7]
+        second_here = got[-1] if first else rest[0][0]
+        if not last:
+            attn_normal, attn_factor = got[7:9]
             heads_here[layer + 1] = side
         stored.append(
             (
                 first_here,
                 second_here,
-                attn_normal,
-                attn_factor,
+                *here,
                 attn_rows,
                 q,
                 k,
                 v,
                 attended,
                 logs,
-                scale_row,
                 scaled,
                 post_normal,
                 post_factor,
@@ -2442,9 +2619,7 @@
                 totals,
             )
         )
-        residual = middle + ffn_out + fc2_bias[layer]
-    gradient_b = side
-    gradient = gradient_b.astype(f32)
+    gradient = gradient_b = side
 
     first_done, second_done = [None] * layers, [None] * layers
     heads_done, hidden_done = [None] * layers, [None] * layers
@@ -2462,7 +2637,6 @@
             v,
             attended,
             logs,
-            scale_row,
             scaled,
             post_normal,
             post_factor,
@@ -2476,7 +2650,7 @@
         ) = stored[layer]
         last = layer + 1 == layers
         if last:
-            sides = [PlaneMove(residual.astype(bf16), back=True)]
+            sides = [PlaneMove(block, back=True)]
         else:
             sides = [RowsGather(heads_grad, "midway")]
             sides.append(ThenRows(LineScatter(hidden_grad), "closing"))
@@ -2488,7 +2662,7 @@
                     gradient_b,
                     first_here,
                     second_here,
-                    gain_hidden[layer][None],
+                    small,
                     slope,
                     hidden_normal,
                     mixed,
@@ -2498,14 +2672,14 @@
                     (
                         ffn_normal,
                         ffn_factor,
-                        ln_ffn_gain[layer][None],
+                        ln_ffn_gain,
                         post_normal,
                         post_factor,
-                        ln_post_gain[layer][None],
+                        ln_post_gain,
                     ),
+                    layer,
                 ),
                 *sides,
-                mib=60,
             )
         )
         if last:
@@ -2514,15 +2688,15 @@
             heads_done[layer + 1], hidden_done[layer + 1] = got[0][0], got[1][0]
             early_done[layer + 1], late_vectors = got[2][0], got[3][0]
         sides = [ThenRows(LineScatter(first_grad), "soon"), RowsGather(second_grad)]
-        sides.append(StepSum(early_vectors))
+        sides.append(StepThenLine(early_vectors) if layer == 0 else StepSum(early_vectors))
         if not last:
             sides.append(LineSum(late_vectors))
-        ((gradient, heads_grad, hidden_grad, gradient_b, late_vectors), *got) = run_tasks(
+        (results, *got) = run_tasks(
             ids,
             AttnBackward(
                 branch_b,
                 docs,
-                scale_row,
+                head_scale,
                 heads_here[layer],
                 q,
                 k,
@@ -2531,26 +2705,21 @@
                 attended,
                 logs,
                 attn_rows,
-                True,
-                (gradient, attn_normal, attn_factor, ln_attn_gain[layer][None]),
+                (gradient, attn_normal, attn_factor, ln_attn_gain),
                 hidden_sums,
+                layer,
+                layer == 0,
             ),
             *sides,
-            mib=48,
         )
         first_done[layer], second_done[layer], early_vectors = got[0][0], got[1][0], got[2][0]
         if not last:
             late_done[layer + 1] = got[3][0]
-    ((late_done[0],), (early_done[0],), (input_grad,), (heads_done[0],), (hidden_done[0],)) = (
-        run_tasks(
-            ids,
-            PlaneThenLineSum(late_vectors),
-            LineSum(early_vectors),
-            PlaneMove(gradient_b, back=True),
-            RowsGather(heads_grad),
-            ThenRows(LineScatter(hidden_grad), "midway"),
-        )
-    )
+        if layer == 0:
+            input_grad, late_done[0], heads_done[0], hidden_done[0] = results
+            early_done[0] = early_vectors
+        else:
+            gradient, heads_grad, hidden_grad, gradient_b, late_vectors = results
     return finish_all(
         layer_output,
         input_grad,

time: 577 us -> 544 us (0.943)
  local copies, waits for them, and re-layouts: 32.1 us -> 4.72 us
  other arithmetic: 11.6 us -> 0.68 us
    unnamed x152 -> x6, local copies, waits for them, and re-layouts: 25.4 us -> 3.27 us
    convert_element_type x6 -> x0, other arithmetic: 6.87 us -> none  [the longest x2 2.51 us: plane_device(): ffn_in.astype(bf16)]
    pallas_call x9 -> x8, Pallas kernels: 516 us -> 519 us  [run_tasks(): pl.pallas_call(kernel, out_shape=[out for task in tasks for out in task.o...]
where the time goes in v2:
time: 544 us; the launch traced here: 534 us
  Pallas kernels  527 us (97%)
    pallas_call x8, Pallas kernels, run_tasks(): pl.pallas_call(kernel, out_shape=[out for task in tasks for out in task.o...  519 us

profile of v2, /device:TPU:1, one launch (start us, length us, event | category | flops | bytes accessed | tf_op | source)
XLA Modules:
  0.0 533.8 jit_solution(17448831612660241656)
XLA Ops:
  0.7 0.0 copy-start
  0.7 0.7 copy-done
  1.4 0.8 constant_dynamic-slice_fusion.3
  2.1 0.1 maximum_bitcast_fusion
  2.2 0.7 constant_dynamic-slice_fusion
  2.9 0.6 pad_maximum_fusion.refs_3_
  3.5 2.6 copy.39
  6.1 85.7 %shard_map.339 = (f32[256,1024]{1,0:T(8,128)}, bf16[2048,1024]{1,0:T(8,128)(2,1)}, bf16[2048,128]{1,0:T(8,128)(2,1)}, bf16[2048,128]{1,0:T(8,128)(2,1)}, bf16[20...) custom-call(bf16[256,1024]{1,0:T(8,128)(2,1)} %refs_0_.1, ...), custom_call_target="tpu_custom_call" | custom-call | tf_op jit(solution)/shard_map/pallas_call | solution.py:635
  91.8 56.3 %shard_map.340 = (f32[256,1024]{1,0:T(8,128)}, bf16[2048,1024]{1,0:T(8,128)(2,1)}, f32[2048,512]{1,0:T(8,128)}, f32[2048,512]{1,0:T(8,128)}, bf16[2048,512]{1,0:...) custom-call(bf16[256,1024]{1,0:T(8,128)(2,1)} %get-tuple-element.123, ...), custom_call_target="tpu_custom_call" | custom-call | tf_op jit(solution)/shard_map/pallas_call | solution.py:635
  148.1 53.0 %shard_map.341 = (f32[256,1024]{1,0:T(8,128)}, bf16[2048,1024]{1,0:T(8,128)(2,1)}, bf16[2048,128]{1,0:T(8,128)(2,1)}, bf16[2048,128]{1,0:T(8,128)(2,1)}, bf16[20...) custom-call(bf16[256,1024]{1,0:T(8,128)(2,1)} %get-tuple-element.127, ...), custom_call_target="tpu_custom_call" | custom-call | tf_op jit(solution)/shard_map/pallas_call | solution.py:635
  201.1 56.7 %shard_map.342 = (f32[256,1024]{1,0:T(8,128)}, bf16[2048,1024]{1,0:T(8,128)(2,1)}, f32[2048,512]{1,0:T(8,128)}, f32[2048,512]{1,0:T(8,128)}, bf16[2048,512]{1,0:...) custom-call(bf16[256,1024]{1,0:T(8,128)(2,1)} %get-tuple-element.131.refs_0_, ...), custom_call_target="tpu_custom_call" | custom-call | tf_op jit(solution)/shard_map/pallas_call | solution.py:635
  257.8 53.8 %shard_map.343 = (f32[256,1024]{1,0:T(8,128)}, bf16[4,1024,128]{2,1,0:T(8,128)(2,1)}, bf16[128,1024]{1,0:T(8,128)(2,1)}, f32[3,512]{1,0:T(4,128)}, bf16[256,1024...) custom-call(bf16[256,1024]{1,0:T(8,128)(2,1)} %get-tuple-element.135.refs_0_.refs_9_, ...), custom_call_target="tpu_custom_call" | custom-call | tf_op jit(solution)/shard_map/pallas_call | solution.py:635
  311.6 63.4 %shard_map.344 = (f32[256,1024]{1,0:T(8,128)}, bf16[4,64,512]{2,1,0:T(8,128)(2,1)}, f32[4,4,128]{2,1,0:T(4,128)}, bf16[256,1024]{1,0:T(8,128)(2,1)}, f32[8,1024]...) custom-call(bf16[256,1024]{1,0:T(8,128)(2,1)} %get-tuple-element.147.refs_0_, ...), custom_call_target="tpu_custom_call" | custom-call | tf_op jit(solution)/shard_map/pallas_call | solution.py:635
  375.1 59.1 %shard_map.345 = (f32[256,1024]{1,0:T(8,128)}, bf16[4,1024,128]{2,1,0:T(8,128)(2,1)}, bf16[128,1024]{1,0:T(8,128)(2,1)}, f32[3,512]{1,0:T(4,128)}, bf16[256,1024...) custom-call(bf16[256,1024]{1,0:T(8,128)(2,1)} %get-tuple-element.162, ...), custom_call_target="tpu_custom_call" | custom-call | tf_op jit(solution)/shard_map/pallas_call | solution.py:635
  434.1 0.0 copy-start.1
  434.2 90.8 %shard_map.346 = (bf16[256,1024]{1,0:T(8,128)(2,1)}, f32[8,1024]{1,0:T(8,128)}, bf16[4,4,64,512]{3,2,1,0:T(8,128)(2,1)}, f32[4,4,128]{2,1,0:T(4,128)}, bf16[4,10...) custom-call(bf16[256,1024]{1,0:T(8,128)(2,1)} %get-tuple-element.178.refs_0_, ...), custom_call_target="tpu_custom_call" | custom-call | tf_op jit(solution)/shard_map/pallas_call | solution.py:635
  524.9 8.6 %shard_map.347 = (bf16[256,1024]{1,0:T(8,128)(2,1)}, f32[256,1024]{1,0:T(8,128)}, f32[2,1024]{1,0:T(2,128)}, f32[2,1024]{1,0:T(2,128)}, f32[2,3,1024,128]{3,2,1,...) custom-call(bf16[256,1024]{1,0:T(8,128)(2,1)} %get-tuple-element.146, ...), custom_call_target="tpu_custom_call" | custom-call | tf_op jit(solution)/shard_map/pallas_call | solution.py:2470
  533.5 0.0 copy-done.1
  (2 shorter events, 0.0 us)
Async XLA Ops:
  0.7 0.7 copy-start
  434.1 99.4 %copy-start.1 = (f32[2,512]{1,0:T(2,128)S(1)}, f32[2,512]{1,0:T(2,128)}, u32[]{:S(2)}) copy-start(f32[2,512]{1,0:T(2,128)} %param.35) | copy-start | bytes 12292

commit v3 on v2

--- a/solution.py
+++ b/solution.py
@@ -782,7 +782,7 @@
             copies[index].start()
         self.keep(here, ins[0], outs[0], scratch[2]).start()
 
-    def finish(self, here, ins, outs, scratch, work=None, soon=None):
+    def finish(self, here, ins, outs, scratch, work=None, moment=None):
         rows = ins[0].shape[0]
         copies = self.copies(here, ins[0], outs[0], scratch[0], scratch[1])
 
@@ -800,6 +800,8 @@
         for index in range(4):
             copies[index].wait_recv()
             copies[5 + index].start()
+        if moment is not None:
+            moment("spare")
         done(0, 1, 0)
         done(0, 0, 1)
         copies[7].wait_recv()
@@ -811,12 +813,102 @@
         copies[6].wait_recv()
         copies[10].start()
         done(0, 1, 1)
-        if soon is not None:
-            soon()
+        if moment is not None:
+            moment("soon")
         copies[9].wait_recv()
         copies[10].wait_recv()
         done(1, 1, 1)
         for each in copies:
+            each.wait_send()
+
+
+class OrderedGather(PlaneGather):
+    def ends(self, here):
+        over_x = here.core == 0
+        first = (jnp.where(over_x, 1 - here.x, here.x), jnp.where(over_x, here.y, 1 - here.y))
+        second = (jnp.where(over_x, here.x, 1 - here.x), jnp.where(over_x, 1 - here.y, here.y))
+        return first, second
+
+    def copies(self, here, x_ref, o_ref, send_sem, recv_sem):
+        half = x_ref.shape[0] // 2
+        first, second = self.ends(here)
+        to_first, to_second = ({"x": at[0], "y": at[1]} for at in (first, second))
+        to_core = here.peer(*BY_CORE)
+
+        def copy(index, source, target, way):
+            return remote(source, target, send_sem.at[index], recv_sem.at[index], way)
+
+        def pass_on(index, way, *at):
+            return copy(index, self.place(here, o_ref, *at), self.place(here, o_ref, *at), way)
+
+        own = [self.place(here, o_ref, here.x, here.y, part) for part in (0, 1)]
+        mine = [x_ref.at[pl.ds(part * half, half)] for part in (0, 1)]
+        far = (1 - here.x, 1 - here.y)
+        return [
+            copy(0, mine[0], own[0], to_first),
+            copy(1, mine[1], own[1], to_first),
+            copy(2, mine[1], own[1], to_second),
+            copy(3, mine[0], own[0], to_second),
+            copy(4, x_ref, self.place(here, o_ref, here.x, here.y), to_core),
+            pass_on(5, to_second, *first, 0),
+            pass_on(6, to_first, *second, 1),
+            pass_on(7, to_core, *first),
+            pass_on(8, to_core, *second),
+            pass_on(9, to_core, *far, 0),
+            pass_on(10, to_core, *far, 1),
+        ]
+
+    def start(self, here, ins, outs, scratch):
+        copies = self.copies(here, ins[0], outs[0], scratch[0], scratch[1])
+        for index in (0, 1, 4):
+            copies[index].start()
+        self.keep(here, ins[0], outs[0], scratch[2]).start()
+
+    def finish(self, here, ins, outs, scratch, work=None, moment=None):
+        rows = ins[0].shape[0]
+        copies = self.copies(here, ins[0], outs[0], scratch[0], scratch[1])
+        first, second = self.ends(here)
+        far = (1 - here.x, 1 - here.y)
+
+        def done(at_core, at):
+            if work is not None:
+                work(pl.multiple_of(here.block(at_core, *at) * rows, rows))
+
+        self.keep(here, ins[0], outs[0], scratch[2]).wait()
+        done(here.core, (here.x, here.y))
+        copies[0].wait_send()
+        copies[1].wait_send()
+        copies[2].start()
+        copies[3].start()
+        copies[4].wait_recv()
+        done(1 - here.core, (here.x, here.y))
+        copies[0].wait_recv()
+        copies[5].start()
+        copies[1].wait_recv()
+        copies[7].start()
+        done(here.core, first)
+        copies[7].wait_recv()
+        done(1 - here.core, second)
+        copies[2].wait_recv()
+        copies[6].start()
+        copies[3].wait_recv()
+        copies[8].start()
+        if moment is not None:
+            moment("spare")
+        done(here.core, second)
+        copies[8].wait_recv()
+        done(1 - here.core, first)
+        copies[5].wait_recv()
+        copies[9].start()
+        copies[6].wait_recv()
+        copies[10].start()
+        done(here.core, far)
+        if moment is not None:
+            moment("soon")
+        copies[9].wait_recv()
+        copies[10].wait_recv()
+        done(1 - here.core, far)
+        for each in copies[2:]:
             each.wait_send()
 
 
@@ -1284,7 +1376,7 @@
 
 
 class Parts(Task):
-    def use(self, **parts):
+    def use(self, parts):
         self.parts = parts
         self.scratch = list(self.scratch)
         self.at = {}
@@ -1314,7 +1406,7 @@
         self.outs = (jax.ShapeDtypeStruct(values.shape, f32),)
         self.out_spaces = (pltpu.VMEM,)
         self.scratch = (pltpu.VMEM(values.shape, f32),)
-        self.use(step=StepSum(values), line=LineSum(values))
+        self.use(dict(step=StepSum(values), line=LineSum(values)))
 
     def start(self, here, ins, outs, scratch):
         self.parts["step"].start(here, ins, scratch[:1], self.held(scratch, "step"))
@@ -1404,7 +1496,7 @@
             parts["second"] = WeightGather(second, layer, 0)
             self.outs += parts["second"].outs
             self.out_spaces += (pltpu.VMEM,)
-        self.use(**parts)
+        self.use(parts)
 
     def start(self, here, ins, outs, scratch):
         self.parts["gather"].start(here, ins[:1], scratch[:1], self.held(scratch, "gather"))
@@ -1565,10 +1657,12 @@
             pltpu.VMEM((6, 8, width), f32),
         )
         self.use(
+            dict(
             gather=PlaneGather(block),
             scatter=PlaneScatter(rows, width, 1),
             second=LineScatter(jax.ShapeDtypeStruct((4, hidden // 4, width), bf16)),
             sums=PlaneSum(jax.ShapeDtypeStruct((2, 8 * rows), f32)),
+            )
         )
 
     def loads(self, ins, scratch):
@@ -1787,7 +1881,7 @@
         rows = RowsGather(shape)
         self.outs, self.out_spaces = rows.outs, rows.out_spaces
         self.scratch = (pltpu.VMEM(shape.shape, shape.dtype),)
-        self.use(first=first, rows=rows)
+        self.use(dict(first=first, rows=rows))
 
     def start(self, here, ins, outs, scratch):
         self.parts["first"].start(here, ins, None, self.held(scratch, "first"))
@@ -1985,7 +2079,10 @@
         parts = dict(gather=PlaneGather(block), scatter=PlaneScatter(rows, width, 0))
         if late:
             parts.update(heads=HeadGather(*heads, layer), biases=LineGather(biases))
-            parts.update(tokens=PlaneMove(block, when="push"), docs=PlaneMove(docs, when="push"))
+            half = jax.ShapeDtypeStruct((rows // 2, width), block.dtype)
+            for i in range(2):
+                parts["tokens", i] = PlaneMove(half, when="push")
+            parts["docs"] = PlaneMove(docs, when="push")
             self.outs += parts["heads"].outs + parts["biases"].outs
             self.outs += (jax.ShapeDtypeStruct(docs.shape, f32),)
             self.outs += (jax.ShapeDtypeStruct(block.shape, f32),) * 2
@@ -1999,22 +2096,31 @@
             self.arrays += (residual,)
             self.spaces += (pltpu.VMEM,)
         self.base = 3 + 1 + len(heads)
-        self.use(**parts)
+        self.use(parts)
 
     def start(self, here, ins, outs, scratch):
         if self.late:
-            for name, at, target in (("tokens", 0, scratch[7]), ("docs", 1, scratch[9])):
-                self.parts[name].start(here, (ins[at],), (target,), self.held(scratch, name))
+            for part, held in self.moves(here, ins, scratch):
+                part.start(*held)
         else:
             self.parts["gather"].start(here, ins[:1], scratch[:1], self.held(scratch, "gather"))
+
+    def moves(self, here, ins, scratch):
+        half = ins[0].shape[0] // 2
+        triples = []
+        for i in range(2):
+            piece = pl.ds(i * half, half)
+            triples.append((("tokens", i), ins[0].at[piece], scratch[7].at[piece]))
+        triples.append(("docs", ins[1], scratch[9]))
+        return [
+            (self.parts[name], (here, (source,), (target,), self.held(scratch, name)))
+            for name, source, target in triples
+        ]
 
     def first_norm(self, here, ins, outs, scratch):
         tokens, block = scratch[7:9]
         residual_ref, normal_ref, factor_ref = outs[16:19]
-        moves = [
-            (self.parts[name], (here, (ins[at],), (target,), self.held(scratch, name)))
-            for name, at, target in (("tokens", 0, tokens), ("docs", 1, scratch[9]))
-        ]
+        moves = self.moves(here, ins, scratch)
         for part, held in moves:
             part.at_moment("push", *held)
         self.parts["biases"].start(here, ins[3:4], outs[14:15], self.held(scratch, "biases"))
@@ -2143,23 +2249,27 @@
         self.spaces = (pltpu.VMEM,) * 10 + (pltpu.HBM,)
         self.arrays += (*norm, hidden)
         self.spaces += (pltpu.VMEM,) * 5
-        move, heads_sum = PlaneMove(block, back=True, when="push"), HeadScatter(heads)
+        self.shipped = kinds if end else kinds // 2
+        leaving = jax.ShapeDtypeStruct((self.shipped, *heads.shape[1:]), bf16)
+        staying = jax.ShapeDtypeStruct((kinds - self.shipped, *heads.shape[1:]), bf16)
+        heads_sum = HeadScatter(leaving)
+        half_rows = jax.ShapeDtypeStruct((rows // 2, width), bf16)
         vector, sums = jax.ShapeDtypeStruct((8, width), f32), jax.ShapeDtypeStruct((4, 4, here), f32)
         quarter = heads_sum.outs[0]
         if end:
-            tail = dict(
-                move=move,
+            tail = {("move", i): PlaneMove(half_rows, True, "push") for i in range(2)}
+            tail.update(
                 vectors=PlaneSum(vector),
                 line=LineSum(vector),
                 rows=RowsGather(quarter),
                 hidden=ThenRows(LineScatter(sums), "push"),
             )
-            self.outs = move.outs + (vector,) + tail["rows"].outs + tail["hidden"].outs
+            self.outs = (jax.ShapeDtypeStruct((rows, width), bf16), vector) + tail["rows"].outs + tail["hidden"].outs
             self.out_spaces = (pltpu.HBM, pltpu.VMEM, pltpu.HBM, pltpu.HBM)
         else:
             self.outs = (jax.ShapeDtypeStruct((rows, width), f32), quarter, sums)
-            self.outs += (jax.ShapeDtypeStruct((rows, width), bf16), vector)
-            self.out_spaces = (pltpu.VMEM,) * 5
+            self.outs += (jax.ShapeDtypeStruct((rows, width), bf16), vector, staying)
+            self.out_spaces = (pltpu.VMEM,) * 6
         self.scratch = (
             pltpu.VMEM((8 * rows, width), bf16),
             pltpu.VMEM((8 * rows, width), bf16),
@@ -2183,9 +2293,10 @@
                 pltpu.VMEM(vector.shape, f32),
                 pltpu.VMEM(vector.shape, f32),
             )
-        parts = dict(gather=PlaneGather(block), scatter=PlaneScatter(rows, width, 0))
-        parts.update(heads=heads_sum, **(tail if end else {}))
-        self.use(**parts)
+        parts = dict(gather=OrderedGather(block), scatter=PlaneScatter(rows, width, 0))
+        parts.update(tail if end else {})
+        parts["heads"] = heads_sum
+        self.use(parts)
 
     def load(self, ins, scratch):
         return pltpu.make_async_copy(ins[10], scratch[1], scratch[9].at[0])
@@ -2197,7 +2308,7 @@
     def finish(self, here, ins, outs, scratch):
         block_ref, doc_ref, scale_ref, heads_ref, q_ref, k_ref, v_ref, z_ref, o_ref, l_ref = ins[:10]
         results = scratch[12:17] if self.end else outs
-        out_ref, quarter_ref, hidden_ref, rounded_ref, vector_ref = results
+        out_ref, quarter_ref, hidden_ref, rounded_ref, vector_ref = results[:5]
         middle_ref, normal_ref, factor_ref, gain_ref, sums_ref = ins[11:16]
         (
             rows_buf,
@@ -2212,6 +2323,7 @@
         ) = scratch[:9]
         vectors = scratch[10]
         heads_grad = scratch[11]
+        leaving = (heads_grad.at[pl.ds(0, self.shipped)],)
         scale_row = scale_of(here, scale_ref, self.layer, self.head_width)
         rows, model_width = block_ref.shape
         wide = self.head_width
@@ -2261,7 +2373,7 @@
             scratch[:1],
             self.held(scratch, "gather"),
             work,
-            lambda: self.moment("soon"),
+            self.moment,
         )
 
         def settle(first):
@@ -2284,7 +2396,9 @@
             )
             heads_grad[0:3] = qkv_grad.astype(bf16).reshape(3, 2, wide, model_width)
             heads_grad[3] = out_sum[...].astype(bf16).reshape(2, wide, model_width)
-            self.parts["heads"].start(here, (heads_grad,), None, self.held(scratch, "heads"))
+            self.parts["heads"].start(here, leaving, None, self.held(scratch, "heads"))
+            if not self.end:
+                outs[5][...] = heads_grad[self.shipped :]
 
         early()
         self.parts["scatter"].finish(
@@ -2310,10 +2424,17 @@
             out_ref[piece, :] = gradient
             rounded_ref[piece, :] = gradient.astype(bf16)
 
-        in_chunks(rows, NARROW, pull)
+        home = []
         if self.end:
-            home = (here, (rounded_ref,), outs[:1], self.held(scratch, "move"))
-            self.parts["move"].start(*home)
+            for i in range(2):
+                piece = pl.ds(i * (rows // 2), rows // 2)
+                held = self.held(scratch, ("move", i))
+                refs = (rounded_ref.at[piece],), (outs[0].at[piece],)
+                home.append((self.parts["move", i], (here, *refs, held)))
+                pull(i * NARROW)
+                home[i][0].start(*home[i][1])
+        else:
+            in_chunks(rows, NARROW, pull)
         scale_cols, query_cols, value_cols = (
             jnp.sum(small[i], axis=0, keepdims=True) for i in range(3)
         )
@@ -2342,7 +2463,7 @@
             own = here.core == shard // 2
             hidden_ref[shard, 3:4, :] = jnp.where(own, pairs[shard % 2], 0.0)
         self.moment("tail")
-        held = (here, (heads_grad,), (quarter_ref,), self.held(scratch, "heads"))
+        held = (here, leaving, (quarter_ref,), self.held(scratch, "heads"))
         if not self.end:
             self.parts["heads"].finish(*held)
             return
@@ -2356,12 +2477,14 @@
         self.parts["rows"].begin(*rows_held)
         self.parts["vectors"].finish(*sum_held)
         self.parts["line"].start(*line_held)
-        self.parts["move"].at_moment("push", *home)
+        for part, refs in home:
+            part.at_moment("push", *refs)
         self.parts["hidden"].at_moment("push", *hidden_held)
         self.parts["line"].finish(*line_held)
         self.parts["rows"].finish(*rows_held)
         self.parts["hidden"].finish(*hidden_held)
-        self.parts["move"].finish(*home)
+        for part, refs in home:
+            part.finish(*refs)
 
 
 def finish_kernel(layers, *refs):
@@ -2652,8 +2775,7 @@
         if last:
             sides = [PlaneMove(block, back=True)]
         else:
-            sides = [RowsGather(heads_grad, "midway")]
-            sides.append(ThenRows(LineScatter(hidden_grad), "closing"))
+            sides = [HeadScatter(heads_rest), ThenRows(LineScatter(hidden_grad), "closing")]
             sides += [LineSum(early_vectors), StepSum(late_vectors)]
         ((gradient, first_grad, second_grad, hidden_sums, branch_b, early_vectors), *got) = (
             run_tasks(
@@ -2685,12 +2807,14 @@
         if last:
             layer_output = got[0][0]
         else:
-            heads_done[layer + 1], hidden_done[layer + 1] = got[0][0], got[1][0]
-            early_done[layer + 1], late_vectors = got[2][0], got[3][0]
-        sides = [ThenRows(LineScatter(first_grad), "soon"), RowsGather(second_grad)]
+            heads_rest, hidden_done[layer + 1], early_done[layer + 1], late_vectors = (
+                each[0] for each in got
+            )
+            heads_grad = jnp.concatenate([heads_grad, heads_rest], axis=0)
+        sides = [ThenRows(LineScatter(first_grad), "soon"), RowsGather(second_grad, "spare")]
         sides.append(StepThenLine(early_vectors) if layer == 0 else StepSum(early_vectors))
         if not last:
-            sides.append(LineSum(late_vectors))
+            sides += [LineSum(late_vectors), RowsGather(heads_grad, "spare")]
         (results, *got) = run_tasks(
             ids,
             AttnBackward(
@@ -2714,12 +2838,12 @@
         )
         first_done[layer], second_done[layer], early_vectors = got[0][0], got[1][0], got[2][0]
         if not last:
-            late_done[layer + 1] = got[3][0]
+            late_done[layer + 1], heads_done[layer + 1] = got[3][0], got[4][0]
         if layer == 0:
             input_grad, late_done[0], heads_done[0], hidden_done[0] = results
             early_done[0] = early_vectors
         else:
-            gradient, heads_grad, hidden_grad, gradient_b, late_vectors = results
+            gradient, heads_grad, hidden_grad, gradient_b, late_vectors, heads_rest = results
     return finish_all(
         layer_output,
         input_grad,

time: 544 us -> 537 us (0.987)
  Pallas kernels: 527 us -> 520 us
    pallas_call x8, Pallas kernels: 519 us -> 512 us  [run_tasks(): pl.pallas_call(kernel, out_shape=[out for task in tasks for out in task.o...]
where the time goes in v3:
time: 537 us; the launch traced here: 529 us
  Pallas kernels  520 us (97%)
    pallas_call x8, Pallas kernels, run_tasks(): pl.pallas_call(kernel, out_shape=[out for task in tasks for out in task.o...  512 us

profile of v3, /device:TPU:1, one launch (start us, length us, event | category | flops | bytes accessed | tf_op | source)
XLA Modules:
  0.0 528.5 jit_solution(5725045979145120063)
XLA Ops:
  0.7 0.0 copy-start
  0.7 0.7 copy-done
  1.4 0.8 constant_dynamic-slice_fusion.3
  2.1 0.1 maximum_bitcast_fusion
  2.2 0.7 constant_dynamic-slice_fusion
  2.9 0.6 pad_maximum_fusion.1.refs_3_
  3.5 2.6 copy.39
  6.1 85.8 %shard_map.339 = (f32[256,1024]{1,0:T(8,128)}, bf16[2048,1024]{1,0:T(8,128)(2,1)}, bf16[2048,128]{1,0:T(8,128)(2,1)}, bf16[2048,128]{1,0:T(8,128)(2,1)}, bf16[20...) custom-call(bf16[256,1024]{1,0:T(8,128)(2,1)} %refs_0_.1, ...), custom_call_target="tpu_custom_call" | custom-call | tf_op jit(solution)/shard_map/pallas_call | solution.py:635
  91.9 56.3 %shard_map.340 = (f32[256,1024]{1,0:T(8,128)}, bf16[2048,1024]{1,0:T(8,128)(2,1)}, f32[2048,512]{1,0:T(8,128)}, f32[2048,512]{1,0:T(8,128)}, bf16[2048,512]{1,0:...) custom-call(bf16[256,1024]{1,0:T(8,128)(2,1)} %get-tuple-element.125, ...), custom_call_target="tpu_custom_call" | custom-call | tf_op jit(solution)/shard_map/pallas_call | solution.py:635
  148.2 53.0 %shard_map.341 = (f32[256,1024]{1,0:T(8,128)}, bf16[2048,1024]{1,0:T(8,128)(2,1)}, bf16[2048,128]{1,0:T(8,128)(2,1)}, bf16[2048,128]{1,0:T(8,128)(2,1)}, bf16[20...) custom-call(bf16[256,1024]{1,0:T(8,128)(2,1)} %get-tuple-element.129, ...), custom_call_target="tpu_custom_call" | custom-call | tf_op jit(solution)/shard_map/pallas_call | solution.py:635
  201.2 56.8 %shard_map.342 = (f32[256,1024]{1,0:T(8,128)}, bf16[2048,1024]{1,0:T(8,128)(2,1)}, f32[2048,512]{1,0:T(8,128)}, f32[2048,512]{1,0:T(8,128)}, bf16[2048,512]{1,0:...) custom-call(bf16[256,1024]{1,0:T(8,128)(2,1)} %get-tuple-element.133.refs_0_, ...), custom_call_target="tpu_custom_call" | custom-call | tf_op jit(solution)/shard_map/pallas_call | solution.py:635
  257.9 53.8 %shard_map.343 = (f32[256,1024]{1,0:T(8,128)}, bf16[4,1024,128]{2,1,0:T(8,128)(2,1)}, bf16[128,1024]{1,0:T(8,128)(2,1)}, f32[3,512]{1,0:T(4,128)}, bf16[256,1024...) custom-call(bf16[256,1024]{1,0:T(8,128)(2,1)} %get-tuple-element.137.refs_0_.refs_9_, ...), custom_call_target="tpu_custom_call" | custom-call | tf_op jit(solution)/shard_map/pallas_call | solution.py:635
  311.7 60.8 %shard_map.344 = (f32[256,1024]{1,0:T(8,128)}, bf16[2,64,512]{2,1,0:T(8,128)(2,1)}, f32[4,4,128]{2,1,0:T(4,128)}, bf16[256,1024]{1,0:T(8,128)(2,1)}, f32[8,1024]...) custom-call(bf16[256,1024]{1,0:T(8,128)(2,1)} %get-tuple-element.149, ...), custom_call_target="tpu_custom_call" | custom-call | tf_op jit(solution)/shard_map/pallas_call | solution.py:635
  372.5 0.0 copy-start.2
  372.5 57.8 %shard_map.345 = (f32[256,1024]{1,0:T(8,128)}, bf16[4,1024,128]{2,1,0:T(8,128)(2,1)}, bf16[128,1024]{1,0:T(8,128)(2,1)}, f32[3,512]{1,0:T(4,128)}, bf16[256,1024...) custom-call(bf16[256,1024]{1,0:T(8,128)(2,1)} %get-tuple-element.164, ...), custom_call_target="tpu_custom_call" | custom-call | tf_op jit(solution)/shard_map/pallas_call | solution.py:635
  430.4 0.0 copy-done.2
  430.4 1.6 pad_maximum_fusion.refs_20_
  432.0 0.0 copy-start.1
  432.0 87.7 %shard_map.346 = (bf16[256,1024]{1,0:T(8,128)(2,1)}, f32[8,1024]{1,0:T(8,128)}, bf16[4,4,64,512]{3,2,1,0:T(8,128)(2,1)}, f32[4,4,128]{2,1,0:T(4,128)}, bf16[4,10...) custom-call(bf16[256,1024]{1,0:T(8,128)(2,1)} %get-tuple-element.180, ...), custom_call_target="tpu_custom_call" | custom-call | tf_op jit(solution)/shard_map/pallas_call | solution.py:635
  519.7 8.6 %shard_map.347 = (bf16[256,1024]{1,0:T(8,128)(2,1)}, f32[256,1024]{1,0:T(8,128)}, f32[2,1024]{1,0:T(2,128)}, f32[2,1024]{1,0:T(2,128)}, f32[2,3,1024,128]{3,2,1,...) custom-call(bf16[256,1024]{1,0:T(8,128)(2,1)} %get-tuple-element.148, ...), custom_call_target="tpu_custom_call" | custom-call | tf_op jit(solution)/shard_map/pallas_call | solution.py:2593
  528.3 0.0 copy-done.1
  (2 shorter events, 0.0 us)
Async XLA Ops:
  0.7 0.7 copy-start
  372.5 57.8 %copy-start.2 = (bf16[2,64,512]{2,1,0:T(8,128)(2,1)S(1)}, bf16[2,64,512]{2,1,0:T(8,128)(2,1)}, u32[]{:S(2)}) copy-start(bf16[2,64,512]{2,1,0:T(8,128)(2,1)} %get-tuple-element.197) | copy-start | bytes 393220
  432.0 96.3 %copy-start.1 = (f32[2,512]{1,0:T(2,128)S(1)}, f32[2,512]{1,0:T(2,128)}, u32[]{:S(2)}) copy-start(f32[2,512]{1,0:T(2,128)} %param.35) | copy-start | bytes 12292

commit v4 on v3

--- a/solution.py
+++ b/solution.py
@@ -514,6 +514,7 @@
 EVERY = ("y", "core", "z", "x")
 f32 = jnp.float32
 bf16 = jnp.bfloat16
+GATHER, SCATTER, SECOND, MIDWAY = "gather", "scatter", "second", "midway"
 
 
 def vmem_params(collective_id=None, mib=24):
@@ -651,7 +652,7 @@
 
 
 class PlaneMove(Task):
-    def __init__(self, values, back=False, when="midway"):
+    def __init__(self, values, back=False, when=MIDWAY):
         self.back, self.when = back, when
         self.arrays, self.spaces = (values,), (pltpu.HBM,)
         self.outs = (jax.ShapeDtypeStruct(values.shape, values.dtype),)
@@ -1302,7 +1303,7 @@
 
     def at_moment(self, name, here, ins, outs, scratch):
         part, got = scratch[:2]
-        if name == "midway":
+        if name == MIDWAY:
             self.leg(here, 0, ins[0], scratch).wait()
             part[0] = ins[0][...] + got[0]
             self.leg(here, 1, part.at[0], scratch).start()
@@ -1493,16 +1494,16 @@
             sums=PlaneSum(jax.ShapeDtypeStruct((2, 8 * rows), f32)),
         )
         if late:
-            parts["second"] = WeightGather(second, layer, 0)
-            self.outs += parts["second"].outs
+            parts[SECOND] = WeightGather(second, layer, 0)
+            self.outs += parts[SECOND].outs
             self.out_spaces += (pltpu.VMEM,)
         self.use(parts)
 
     def start(self, here, ins, outs, scratch):
-        self.parts["gather"].start(here, ins[:1], scratch[:1], self.held(scratch, "gather"))
+        self.parts[GATHER].start(here, ins[:1], scratch[:1], self.held(scratch, GATHER))
         if self.late:
-            held = self.held(scratch, "second")
-            self.parts["second"].start(here, ins[2:3], outs[self.base :], held)
+            held = self.held(scratch, SECOND)
+            self.parts[SECOND].start(here, ins[2:3], outs[self.base :], held)
 
     def finish(self, here, ins, outs, scratch):
         block_ref, first_ref, second_ref, small_ref, middle_ref, row_ref = ins[:6]
@@ -1539,8 +1540,8 @@
             sums[0:1, pl.ds(first, rows)] = turned[0:1]
             sums[1:2, pl.ds(first, rows)] = turned[64:65]
 
-        self.parts["gather"].finish(
-            here, ins[:1], scratch[:1], self.held(scratch, "gather"), work
+        self.parts[GATHER].finish(
+            here, ins[:1], scratch[:1], self.held(scratch, GATHER), work
         )
         held = self.held(scratch, "sums")
         self.parts["sums"].start(here, (sums,), None, held)
@@ -1550,9 +1551,9 @@
         keep_slope.start()
         self.parts["sums"].finish(here, (sums,), (total_ref,), held)
         if self.late:
-            held = self.held(scratch, "second")
-            self.parts["second"].finish(here, ins[2:3], outs[self.base :], held)
-        self.moment("midway")
+            held = self.held(scratch, SECOND)
+            self.parts[SECOND].finish(here, ins[2:3], outs[self.base :], held)
+        self.moment(MIDWAY)
 
         def rows_of(first):
             average = total_ref[0:1, pl.ds(first, rows)] / hidden_all
@@ -1577,11 +1578,11 @@
             keep_normal.start()
             self.moment("closing")
 
-        self.parts["scatter"].finish(
+        self.parts[SCATTER].finish(
             here,
             None,
             (out_ref,),
-            self.held(scratch, "scatter"),
+            self.held(scratch, SCATTER),
             rows_of,
             lambda: second_ref[...],
             idle=idle,
@@ -1673,7 +1674,7 @@
         ]
 
     def start(self, here, ins, outs, scratch):
-        self.parts["gather"].start(here, ins[:1], scratch[:1], self.held(scratch, "gather"))
+        self.parts[GATHER].start(here, ins[:1], scratch[:1], self.held(scratch, GATHER))
         for each in self.loads(ins, scratch):
             each.start()
 
@@ -1743,15 +1744,15 @@
             sums[0:1, pl.ds(first, rows)] = turned[0:1]
             sums[1:2, pl.ds(first, rows)] = turned[64:65]
 
-        self.parts["gather"].finish(
-            here, ins[:1], scratch[:1], self.held(scratch, "gather"), work
+        self.parts[GATHER].finish(
+            here, ins[:1], scratch[:1], self.held(scratch, GATHER), work
         )
         held = self.held(scratch, "sums")
         self.parts["sums"].start(here, (sums,), None, held)
         second_grad[...] = second_sum[...].astype(bf16).reshape(second_grad.shape)
         load_slope.wait()
-        self.moment("midway")
-        self.parts["second"].start(here, (second_grad,), None, self.held(scratch, "second"))
+        self.moment(MIDWAY)
+        self.parts[SECOND].start(here, (second_grad,), None, self.held(scratch, SECOND))
         self.parts["sums"].finish(here, (sums,), (got,), held)
 
         def rows_of(first):
@@ -1788,11 +1789,11 @@
                 first_grad[i] = whole[:, i * part : (i + 1) * part]
             self.moment("closing")
 
-        self.parts["scatter"].finish(
+        self.parts[SCATTER].finish(
             here,
             None,
             (out_ref,),
-            self.held(scratch, "scatter"),
+            self.held(scratch, SCATTER),
             rows_of,
             lambda: first_ref[...],
             idle=idle,
@@ -1823,8 +1824,8 @@
         vector_ref[...] = jnp.zeros_like(vector_ref)
         for i in range(6):
             vector_ref[i : i + 1, :] = jnp.sum(vectors[i], axis=0, keepdims=True)
-        held = self.held(scratch, "second")
-        self.parts["second"].finish(here, (second_grad,), (second_quarter,), held)
+        held = self.held(scratch, SECOND)
+        self.parts[SECOND].finish(here, (second_grad,), (second_quarter,), held)
         for i in range(3):
             small_ref[i : i + 1, :] = jnp.sum(small[i], axis=0, keepdims=True)
 
@@ -2103,7 +2104,7 @@
             for part, held in self.moves(here, ins, scratch):
                 part.start(*held)
         else:
-            self.parts["gather"].start(here, ins[:1], scratch[:1], self.held(scratch, "gather"))
+            self.parts[GATHER].start(here, ins[:1], scratch[:1], self.held(scratch, GATHER))
 
     def moves(self, here, ins, scratch):
         half = ins[0].shape[0] // 2
@@ -2144,8 +2145,8 @@
         if self.late:
             doc_ref = outs[15]
             block_ref = self.first_norm(here, ins, outs, scratch)
-            self.parts["gather"].start(
-                here, (block_ref,), scratch[:1], self.held(scratch, "gather")
+            self.parts[GATHER].start(
+                here, (block_ref,), scratch[:1], self.held(scratch, GATHER)
             )
         out_ref, rows_out, q_ref, k_ref, v_ref, z_ref, o_ref, l_ref = outs[:8]
         rows_buf, v_cols, s_buf, acc, top, total, save = scratch[:7]
@@ -2176,11 +2177,11 @@
             v_ref[block, :] = v
             v_cols[:, block] = turned(v)
 
-        self.parts["gather"].finish(
+        self.parts[GATHER].finish(
             here,
             (block_ref,),
             scratch[:1],
-            self.held(scratch, "gather"),
+            self.held(scratch, GATHER),
             None if self.late else work,
         )
         keep_rows = pltpu.make_async_copy(rows_buf, rows_out, save.at[0])
@@ -2190,7 +2191,7 @@
             self.parts["biases"].finish(here, ins[3:4], outs[14:15], self.held(scratch, "biases"))
             in_chunks(8 * rows, rows, work)
             self.parts["heads"].arrive(1, outs[13:14], self.held(scratch, "heads"))
-        self.moment("midway")
+        self.moment(MIDWAY)
 
         def rows_of(first):
             out = attend_block(
@@ -2200,11 +2201,11 @@
             z_ref[pl.ds(first, rows), :] = z
             return z
 
-        self.parts["scatter"].finish(
+        self.parts[SCATTER].finish(
             here,
             None,
             (out_ref,),
-            self.held(scratch, "scatter"),
+            self.held(scratch, SCATTER),
             rows_of,
             lambda: heads_ref[3].reshape(width, model_width),
             idle=lambda: self.moment("closing"),
@@ -2302,7 +2303,7 @@
         return pltpu.make_async_copy(ins[10], scratch[1], scratch[9].at[0])
 
     def start(self, here, ins, outs, scratch):
-        self.parts["gather"].start(here, ins[:1], scratch[:1], self.held(scratch, "gather"))
+        self.parts[GATHER].start(here, ins[:1], scratch[:1], self.held(scratch, GATHER))
         self.load(ins, scratch).start()
 
     def finish(self, here, ins, outs, scratch):
@@ -2367,11 +2368,11 @@
             proj[block, 0:width] = grad
             small[1] += fold(grad.astype(f32))
 
-        self.parts["gather"].finish(
+        self.parts[GATHER].finish(
             here,
             ins[:1],
             scratch[:1],
-            self.held(scratch, "gather"),
+            self.held(scratch, GATHER),
             work,
             self.moment,
         )
@@ -2384,7 +2385,7 @@
             small[2] += fold(value_grad.astype(f32))
 
         in_chunks(8 * rows, rows, settle)
-        self.moment("midway")
+        self.moment(MIDWAY)
 
         def early():
             self.load(ins, scratch).wait()
@@ -2401,11 +2402,11 @@
                 outs[5][...] = heads_grad[self.shipped :]
 
         early()
-        self.parts["scatter"].finish(
+        self.parts[SCATTER].finish(
             here,
             None,
             (out_ref,),
-            self.held(scratch, "scatter"),
+            self.held(scratch, SCATTER),
             lambda first: proj[pl.ds(first, rows), :],
             lambda: heads_ref[0:3].reshape(3 * width, model_width),
             idle=lambda: self.moment("closing"),
@@ -2676,7 +2677,7 @@
                 norms,
                 late=attn_norm,
             )
-            sides = [WeightGather(fc1_weight, layer, 1, "midway")]
+            sides = [WeightGather(fc1_weight, layer, 1, MIDWAY)]
         else:
             task = AttnForward(
                 block,
@@ -2698,7 +2699,7 @@
         here = (attn_normal, attn_factor)
         sides = [PlaneMove(cotangent)]
         if not last:
-            sides = [HeadGather(qkv_rows, out_weight, layer + 1, "midway" if first else "start")]
+            sides = [HeadGather(qkv_rows, out_weight, layer + 1, MIDWAY if first else "start")]
         (got, (side,)) = run_tasks(
             ids,
             FfnForward(

time: 537 us -> 537 us (level)
  no operation moved by 1% of the time
where the time goes in v4:
time: 537 us; the launch traced here: 529 us
  Pallas kernels  520 us (97%)
    pallas_call x8, Pallas kernels, run_tasks(): pl.pallas_call(kernel, out_shape=[out for task in tasks for out in task.o...  512 us

profile of v4, /device:TPU:1, one launch (start us, length us, event | category | flops | bytes accessed | tf_op | source)
XLA Modules:
  0.0 528.5 jit_solution(5725045979145120063)
XLA Ops:
  0.7 0.0 copy-start
  0.7 0.7 copy-done
  1.4 0.8 constant_dynamic-slice_fusion.3
  2.1 0.1 maximum_bitcast_fusion
  2.2 0.7 constant_dynamic-slice_fusion
  2.9 0.6 pad_maximum_fusion.1.refs_3_
  3.5 2.6 copy.39
  6.1 85.8 %shard_map.339 = (f32[256,1024]{1,0:T(8,128)}, bf16[2048,1024]{1,0:T(8,128)(2,1)}, bf16[2048,128]{1,0:T(8,128)(2,1)}, bf16[2048,128]{1,0:T(8,128)(2,1)}, bf16[20...) custom-call(bf16[256,1024]{1,0:T(8,128)(2,1)} %refs_0_.1, ...), custom_call_target="tpu_custom_call" | custom-call | tf_op jit(solution)/shard_map/pallas_call | solution.py:636
  91.9 56.3 %shard_map.340 = (f32[256,1024]{1,0:T(8,128)}, bf16[2048,1024]{1,0:T(8,128)(2,1)}, f32[2048,512]{1,0:T(8,128)}, f32[2048,512]{1,0:T(8,128)}, bf16[2048,512]{1,0:...) custom-call(bf16[256,1024]{1,0:T(8,128)(2,1)} %get-tuple-element.125, ...), custom_call_target="tpu_custom_call" | custom-call | tf_op jit(solution)/shard_map/pallas_call | solution.py:636
  148.2 53.0 %shard_map.341 = (f32[256,1024]{1,0:T(8,128)}, bf16[2048,1024]{1,0:T(8,128)(2,1)}, bf16[2048,128]{1,0:T(8,128)(2,1)}, bf16[2048,128]{1,0:T(8,128)(2,1)}, bf16[20...) custom-call(bf16[256,1024]{1,0:T(8,128)(2,1)} %get-tuple-element.129, ...), custom_call_target="tpu_custom_call" | custom-call | tf_op jit(solution)/shard_map/pallas_call | solution.py:636
  201.2 56.8 %shard_map.342 = (f32[256,1024]{1,0:T(8,128)}, bf16[2048,1024]{1,0:T(8,128)(2,1)}, f32[2048,512]{1,0:T(8,128)}, f32[2048,512]{1,0:T(8,128)}, bf16[2048,512]{1,0:...) custom-call(bf16[256,1024]{1,0:T(8,128)(2,1)} %get-tuple-element.133.refs_0_, ...), custom_call_target="tpu_custom_call" | custom-call | tf_op jit(solution)/shard_map/pallas_call | solution.py:636
  257.9 53.8 %shard_map.343 = (f32[256,1024]{1,0:T(8,128)}, bf16[4,1024,128]{2,1,0:T(8,128)(2,1)}, bf16[128,1024]{1,0:T(8,128)(2,1)}, f32[3,512]{1,0:T(4,128)}, bf16[256,1024...) custom-call(bf16[256,1024]{1,0:T(8,128)(2,1)} %get-tuple-element.137.refs_0_.refs_9_, ...), custom_call_target="tpu_custom_call" | custom-call | tf_op jit(solution)/shard_map/pallas_call | solution.py:636
  311.7 60.8 %shard_map.344 = (f32[256,1024]{1,0:T(8,128)}, bf16[2,64,512]{2,1,0:T(8,128)(2,1)}, f32[4,4,128]{2,1,0:T(4,128)}, bf16[256,1024]{1,0:T(8,128)(2,1)}, f32[8,1024]...) custom-call(bf16[256,1024]{1,0:T(8,128)(2,1)} %get-tuple-element.149, ...), custom_call_target="tpu_custom_call" | custom-call | tf_op jit(solution)/shard_map/pallas_call | solution.py:636
  372.5 0.0 copy-start.2
  372.5 57.8 %shard_map.345 = (f32[256,1024]{1,0:T(8,128)}, bf16[4,1024,128]{2,1,0:T(8,128)(2,1)}, bf16[128,1024]{1,0:T(8,128)(2,1)}, f32[3,512]{1,0:T(4,128)}, bf16[256,1024...) custom-call(bf16[256,1024]{1,0:T(8,128)(2,1)} %get-tuple-element.164, ...), custom_call_target="tpu_custom_call" | custom-call | tf_op jit(solution)/shard_map/pallas_call | solution.py:636
  430.4 0.0 copy-done.2
  430.4 1.6 pad_maximum_fusion.refs_20_
  432.0 0.0 copy-start.1
  432.0 87.7 %shard_map.346 = (bf16[256,1024]{1,0:T(8,128)(2,1)}, f32[8,1024]{1,0:T(8,128)}, bf16[4,4,64,512]{3,2,1,0:T(8,128)(2,1)}, f32[4,4,128]{2,1,0:T(4,128)}, bf16[4,10...) custom-call(bf16[256,1024]{1,0:T(8,128)(2,1)} %get-tuple-element.180, ...), custom_call_target="tpu_custom_call" | custom-call | tf_op jit(solution)/shard_map/pallas_call | solution.py:636
  519.7 8.6 %shard_map.347 = (bf16[256,1024]{1,0:T(8,128)(2,1)}, f32[256,1024]{1,0:T(8,128)}, f32[2,1024]{1,0:T(2,128)}, f32[2,1024]{1,0:T(2,128)}, f32[2,3,1024,128]{3,2,1,...) custom-call(bf16[256,1024]{1,0:T(8,128)(2,1)} %get-tuple-element.148, ...), custom_call_target="tpu_custom_call" | custom-call | tf_op jit(solution)/shard_map/pallas_call | solution.py:2594
  528.3 0.0 copy-done.1
  (2 shorter events, 0.0 us)
Async XLA Ops:
  0.7 0.7 copy-start
  372.5 57.8 %copy-start.2 = (bf16[2,64,512]{2,1,0:T(8,128)(2,1)S(1)}, bf16[2,64,512]{2,1,0:T(8,128)(2,1)}, u32[]{:S(2)}) copy-start(bf16[2,64,512]{2,1,0:T(8,128)(2,1)} %get-tuple-element.197) | copy-start | bytes 393220
  432.0 96.3 %copy-start.1 = (f32[2,512]{1,0:T(2,128)S(1)}, f32[2,512]{1,0:T(2,128)}, u32[]{:S(2)}) copy-start(f32[2,512]{1,0:T(2,128)} %param.35) | copy-start | bytes 12292

commit v5 on v4

--- a/solution.py
+++ b/solution.py
@@ -652,8 +652,8 @@
 
 
 class PlaneMove(Task):
-    def __init__(self, values, back=False, when=MIDWAY):
-        self.back, self.when = back, when
+    def __init__(self, values, back=False, when=MIDWAY, first="start"):
+        self.back, self.when, self.first = back, when, first
         self.arrays, self.spaces = (values,), (pltpu.HBM,)
         self.outs = (jax.ShapeDtypeStruct(values.shape, values.dtype),)
         self.out_spaces = (pltpu.HBM,)
@@ -706,11 +706,13 @@
             second.append((bend, over, True))
         return first, second
 
-    def start(self, here, ins, outs, scratch):
-        for when, copy, _ in self.plan(here, ins, outs, scratch)[0]:
-            pl.when(when)(copy.start)
+    def start(self, *held):
+        self.at_moment("start", *held)
 
     def at_moment(self, name, here, ins, outs, scratch):
+        if name == self.first:
+            for when, copy, _ in self.plan(here, ins, outs, scratch)[0]:
+                pl.when(when)(copy.start)
         if name == self.when:
             held, _, recv = scratch
 
@@ -2690,36 +2692,40 @@
                 norms,
                 residual=residual,
             )
-            sides = [WeightGather(fc1_weight, layer, 1), WeightGather(fc2_weight, layer, 0)]
+            sides = [WeightGather(fc1_weight, layer, 1)]
+        if last:
+            sides.append(PlaneMove(cotangent, when="closing", first=MIDWAY))
         (got, (first_here,), *rest) = run_tasks(ids, task, *sides)
         middle, attn_rows, q, k, v, scaled, attended, logs = got[:8]
         post_normal, post_factor, ffn_normal, ffn_factor, block = got[8:13]
         if first:
             heads_here[0], small, docs, _, attn_normal, attn_factor = got[13:]
         here = (attn_normal, attn_factor)
-        sides = [PlaneMove(cotangent)]
+        if last:
+            gradient = gradient_b = rest[0][0]
+        sides = []
         if not last:
             sides = [HeadGather(qkv_rows, out_weight, layer + 1, MIDWAY if first else "start")]
-        (got, (side,)) = run_tasks(
+        (got, *rest) = run_tasks(
             ids,
             FfnForward(
                 block,
                 first_here,
-                fc2_weight if first else rest[0][0],
+                fc2_weight,
                 small,
                 middle,
                 fc2_bias,
                 None if last else attn_norm,
                 layer,
-                first,
+                True,
             ),
             *sides,
         )
         residual, ffn_rows, slope, hidden_normal, mixed, totals, block = got[:7]
-        second_here = got[-1] if first else rest[0][0]
+        second_here = got[-1]
         if not last:
             attn_normal, attn_factor = got[7:9]
-            heads_here[layer + 1] = side
+            heads_here[layer + 1] = rest[0][0]
         stored.append(
             (
                 first_here,
@@ -2743,8 +2749,6 @@
                 totals,
             )
         )
-    gradient = gradient_b = side
-
     first_done, second_done = [None] * layers, [None] * layers
     heads_done, hidden_done = [None] * layers, [None] * layers
     early_done, late_done = [None] * layers, [None] * layers

time: 537 us -> 537 us (level)
  no operation moved by 1% of the time
where the time goes in v5:
time: 537 us; the launch traced here: 528 us
  Pallas kernels  520 us (97%)
    pallas_call x8, Pallas kernels, run_tasks(): pl.pallas_call(kernel, out_shape=[out for task in tasks for out in task.o...  511 us

profile of v5, /device:TPU:1, one launch (start us, length us, event | category | flops | bytes accessed | tf_op | source)
XLA Modules:
  0.0 527.7 jit_solution(11854594085198383139)
XLA Ops:
  0.7 0.0 copy-start
  0.7 0.7 copy-done
  1.4 0.8 constant_dynamic-slice_fusion.3
  2.1 0.1 maximum_bitcast_fusion
  2.2 0.7 constant_dynamic-slice_fusion
  2.9 0.6 pad_maximum_fusion.1.refs_3_
  3.5 2.6 copy.39
  6.1 85.8 %shard_map.339 = (f32[256,1024]{1,0:T(8,128)}, bf16[2048,1024]{1,0:T(8,128)(2,1)}, bf16[2048,128]{1,0:T(8,128)(2,1)}, bf16[2048,128]{1,0:T(8,128)(2,1)}, bf16[20...) custom-call(bf16[256,1024]{1,0:T(8,128)(2,1)} %refs_0_.1, ...), custom_call_target="tpu_custom_call" | custom-call | tf_op jit(solution)/shard_map/pallas_call | solution.py:636
  91.9 56.3 %shard_map.340 = (f32[256,1024]{1,0:T(8,128)}, bf16[2048,1024]{1,0:T(8,128)(2,1)}, f32[2048,512]{1,0:T(8,128)}, f32[2048,512]{1,0:T(8,128)}, bf16[2048,512]{1,0:...) custom-call(bf16[256,1024]{1,0:T(8,128)(2,1)} %get-tuple-element.125, ...), custom_call_target="tpu_custom_call" | custom-call | tf_op jit(solution)/shard_map/pallas_call | solution.py:636
  148.2 54.4 %shard_map.341 = (f32[256,1024]{1,0:T(8,128)}, bf16[2048,1024]{1,0:T(8,128)(2,1)}, bf16[2048,128]{1,0:T(8,128)(2,1)}, bf16[2048,128]{1,0:T(8,128)(2,1)}, bf16[20...) custom-call(bf16[256,1024]{1,0:T(8,128)(2,1)} %get-tuple-element.129, ...), custom_call_target="tpu_custom_call" | custom-call | tf_op jit(solution)/shard_map/pallas_call | solution.py:636
  202.6 53.7 %shard_map.342 = (f32[256,1024]{1,0:T(8,128)}, bf16[2048,1024]{1,0:T(8,128)(2,1)}, f32[2048,512]{1,0:T(8,128)}, f32[2048,512]{1,0:T(8,128)}, bf16[2048,512]{1,0:...) custom-call(bf16[256,1024]{1,0:T(8,128)(2,1)} %get-tuple-element.135.refs_0_, ...), custom_call_target="tpu_custom_call" | custom-call | tf_op jit(solution)/shard_map/pallas_call | solution.py:636
  256.3 54.5 %shard_map.343 = (f32[256,1024]{1,0:T(8,128)}, bf16[4,1024,128]{2,1,0:T(8,128)(2,1)}, bf16[128,1024]{1,0:T(8,128)(2,1)}, f32[3,512]{1,0:T(4,128)}, bf16[256,1024...) custom-call(bf16[256,1024]{1,0:T(8,128)(2,1)} %get-tuple-element.133.refs_0_.refs_9_, ...), custom_call_target="tpu_custom_call" | custom-call | tf_op jit(solution)/shard_map/pallas_call | solution.py:636
  310.8 60.9 %shard_map.344 = (f32[256,1024]{1,0:T(8,128)}, bf16[2,64,512]{2,1,0:T(8,128)(2,1)}, f32[4,4,128]{2,1,0:T(4,128)}, bf16[256,1024]{1,0:T(8,128)(2,1)}, f32[8,1024]...) custom-call(bf16[256,1024]{1,0:T(8,128)(2,1)} %get-tuple-element.149, ...), custom_call_target="tpu_custom_call" | custom-call | tf_op jit(solution)/shard_map/pallas_call | solution.py:636
  371.8 0.0 copy-start.2
  371.8 57.8 %shard_map.345 = (f32[256,1024]{1,0:T(8,128)}, bf16[4,1024,128]{2,1,0:T(8,128)(2,1)}, bf16[128,1024]{1,0:T(8,128)(2,1)}, f32[3,512]{1,0:T(4,128)}, bf16[256,1024...) custom-call(bf16[256,1024]{1,0:T(8,128)(2,1)} %get-tuple-element.164, ...), custom_call_target="tpu_custom_call" | custom-call | tf_op jit(solution)/shard_map/pallas_call | solution.py:636
  429.6 0.0 copy-done.2
  429.6 1.6 pad_maximum_fusion.refs_20_
  431.3 0.0 copy-start.1
  431.3 87.7 %shard_map.346 = (bf16[256,1024]{1,0:T(8,128)(2,1)}, f32[8,1024]{1,0:T(8,128)}, bf16[4,4,64,512]{3,2,1,0:T(8,128)(2,1)}, f32[4,4,128]{2,1,0:T(4,128)}, bf16[4,10...) custom-call(bf16[256,1024]{1,0:T(8,128)(2,1)} %get-tuple-element.180, ...), custom_call_target="tpu_custom_call" | custom-call | tf_op jit(solution)/shard_map/pallas_call | solution.py:636
  518.9 8.6 %shard_map.347 = (bf16[256,1024]{1,0:T(8,128)(2,1)}, f32[256,1024]{1,0:T(8,128)}, f32[2,1024]{1,0:T(2,128)}, f32[2,1024]{1,0:T(2,128)}, f32[2,3,1024,128]{3,2,1,...) custom-call(bf16[256,1024]{1,0:T(8,128)(2,1)} %get-tuple-element.148, ...), custom_call_target="tpu_custom_call" | custom-call | tf_op jit(solution)/shard_map/pallas_call | solution.py:2596
  527.5 0.0 copy-done.1
  (2 shorter events, 0.0 us)
Async XLA Ops:
  0.7 0.7 copy-start
  371.8 57.8 %copy-start.2 = (bf16[2,64,512]{2,1,0:T(8,128)(2,1)S(1)}, bf16[2,64,512]{2,1,0:T(8,128)(2,1)}, u32[]{:S(2)}) copy-start(bf16[2,64,512]{2,1,0:T(8,128)(2,1)} %get-tuple-element.197) | copy-start | bytes 393220
  431.3 96.2 %copy-start.1 = (f32[2,512]{1,0:T(2,128)S(1)}, f32[2,512]{1,0:T(2,128)}, u32[]{:S(2)}) copy-start(f32[2,512]{1,0:T(2,128)} %param.35) | copy-start | bytes 12292
